TPU v7x, 32 devices: a whole 2x2x4 slice. The times are simulated.
32 devices in a mesh: lat: 4 (over y, core), lon: 8 (over z, x).
Axes of the slice: x: 2, y: 2, z: 4, core: 2. Of those that a mesh axis runs over, the one named last changes fastest.
Arguments:
- field: float32 [256, 4, 1024], P(None, 'lat', 'lon'), may hold values from -6 to 6
- cotangent: float32 [256, 4, 1024], P(None, 'lat', 'lon'), may hold values from -6 to 6
- conv_weight: float32 [3, 3, 256, 256], replicated, may hold values from -0.125 to 0.125
- spectral_filter: float32 [2, 256, 1024], P(None, None, 'lon'), may hold values from -6 to 6
Outputs:
- output: float32 [256, 4, 1024], P(None, 'lat', 'lon')
- input_grad: float32 [256, 4, 1024], P(None, 'lat', 'lon')
- filter_grad: float32 [2, 256, 1024], P(None, None, 'lon')
All inputs are finite; a program needn't handle non-finite values.
Results may differ from a plain program's by a relative error of at most 0.00014.
Values sent between devices are 32-bit elements; how exact they have to be, the bound alone decides.
No kernel may reach another device: no remote copies, remote signals or barrier semaphores. Data moves between devices by JAX's collectives and lax.ppermute only.
A program may use at most 64 MiB of HBM per device.

v0:
```python
import jax
import jax.numpy as jnp
from jax import lax
from jax.sharding import PartitionSpec as P

precise = lax.Precision.HIGHEST


def padded_2(array, sides, width, wrap):
    for axis, dim in sides:
        peers, length = (lax.axis_size(axis), array.shape[dim])
        up = [(i, (i + 1) % peers) for i in range(peers if wrap else peers - 1)]
        down = [(j, i) for i, j in up]
        last = lax.slice_in_dim(array, length - width, length, axis=dim)
        leading = lax.slice_in_dim(array, 0, width, axis=dim)
        before = lax.ppermute(last, axis, up)
        after = lax.ppermute(leading, axis, down)
        array = jnp.concatenate([before, array, after], axis=dim)
    return array


def partner(array, axis, stride):
    return lax.ppermute(array, axis, [(i, i ^ 1 << stride) for i in range(lax.axis_size(axis))])


def angle_table(first, second, modulus):
    product = first[:, None] * second[None, :] % modulus
    return 2.0 * jnp.pi / modulus * product.astype(jnp.float32)


def apply_taps(padded, taps, lat_rows, columns):
    total = jnp.zeros((taps.shape[2], lat_rows, columns), jnp.float32)
    for tap_row in range(3):
        for tap_col in range(3):
            window = padded[:, tap_row : tap_row + lat_rows, tap_col : tap_col + columns]
            total = total + jnp.einsum(
                "oi,iab->oab", taps[tap_row, tap_col], window, precision=precise
            )
    return total


def with_rims(field):
    wider = padded_2(field, (("lon", 2),), 1, True)
    return padded_2(wider, (("lat", 1),), 1, False)


def local_forward(real_part, imag_part):
    columns = real_part.shape[-1]
    places = lax.iota(jnp.int32, columns)
    angles = angle_table(places, places, columns)
    cosine = jnp.cos(angles)
    sine = jnp.sin(angles)
    out_real = jnp.dot(real_part, cosine, precision=precise) + jnp.dot(
        imag_part, sine, precision=precise
    )
    out_imag = jnp.dot(imag_part, cosine, precision=precise) - jnp.dot(
        real_part, sine, precision=precise
    )
    return (out_real, out_imag)


def local_inverse(real_part, imag_part):
    columns = real_part.shape[-1]
    places = lax.iota(jnp.int32, columns)
    angles = angle_table(places, places, columns)
    cosine = jnp.cos(angles)
    sine = jnp.sin(angles)
    out_real = jnp.dot(real_part, cosine, precision=precise) - jnp.dot(
        imag_part, sine, precision=precise
    )
    out_imag = jnp.dot(imag_part, cosine, precision=precise) + jnp.dot(
        real_part, sine, precision=precise
    )
    return (out_real / columns, out_imag / columns)


def section_angles(place, bit_pos, columns):
    offsets = lax.iota(jnp.int32, columns)
    start = place % 2**bit_pos * columns
    span = 2 * columns * 2**bit_pos
    angles = 2.0 * jnp.pi / span * (start + offsets).astype(jnp.float32)
    upper = place // 2**bit_pos % 2 == 1
    return (jnp.cos(angles), jnp.sin(angles), upper)


def forward_pairs(field):
    extent = lax.axis_size("lon")
    width_bits = extent.bit_length() - 1
    place = lax.axis_index("lon")
    columns = field.shape[-1]
    data = jnp.stack([field, jnp.zeros_like(field)])
    for bit_pos in reversed(range(width_bits)):
        other = partner(data, "lon", bit_pos)
        cosine, sine, upper = section_angles(place, bit_pos, columns)
        differ = other - data
        turned = jnp.stack(
            [differ[0] * cosine + differ[1] * sine, differ[1] * cosine - differ[0] * sine]
        )
        data = jnp.where(upper, turned, data + other)
    out_real, out_imag = local_forward(data[0], data[1])
    return jnp.stack([out_real, out_imag])


def inverse_pairs(spectrum):
    extent = lax.axis_size("lon")
    width_bits = extent.bit_length() - 1
    place = lax.axis_index("lon")
    columns = spectrum.shape[-1]
    back_real, back_imag = local_inverse(spectrum[0], spectrum[1])
    data = jnp.stack([back_real, back_imag])
    for bit_pos in range(width_bits):
        cosine, sine, upper = section_angles(place, bit_pos, columns)
        turned = jnp.stack([data[0] * cosine - data[1] * sine, data[1] * cosine + data[0] * sine])
        outgoing = jnp.where(upper, turned, data)
        other = partner(outgoing, "lon", bit_pos)
        data = jnp.where(upper, other - outgoing, outgoing + other) * 0.5
    return data[0]


def on_device(field, cotangent, conv_weight, spectral_filter):
    lat_rows = field.shape[1]
    columns = field.shape[2]
    total_len = columns * lax.axis_size("lon")
    mixed = apply_taps(with_rims(field), conv_weight, lat_rows, columns)
    hidden_spec = forward_pairs(mixed)
    cot_spec = forward_pairs(cotangent)
    gain_real = spectral_filter[0][:, None, :]
    gain_imag = spectral_filter[1][:, None, :]
    filtered = jnp.stack(
        [
            gain_real * hidden_spec[0] - gain_imag * hidden_spec[1],
            gain_real * hidden_spec[1] + gain_imag * hidden_spec[0],
        ]
    )
    adjoint = jnp.stack(
        [
            gain_real * cot_spec[0] + gain_imag * cot_spec[1],
            gain_real * cot_spec[1] - gain_imag * cot_spec[0],
        ]
    )
    shaped = inverse_pairs(filtered)
    back_field = inverse_pairs(adjoint)
    output = field + shaped
    local_grad = (
        jnp.stack(
            [
                jnp.sum(hidden_spec[0] * cot_spec[0] + hidden_spec[1] * cot_spec[1], axis=1),
                jnp.sum(hidden_spec[0] * cot_spec[1] - hidden_spec[1] * cot_spec[0], axis=1),
            ]
        )
        / total_len
    )
    filter_grad = lax.psum(local_grad, "lat")
    flipped_taps = jnp.transpose(conv_weight[::-1, ::-1], (0, 1, 3, 2))
    input_grad = cotangent + apply_taps(with_rims(back_field), flipped_taps, lat_rows, columns)
    return (output, input_grad, filter_grad)


def solution(mesh):
    placed = (P(None, "lat", "lon"), P(None, "lat", "lon"), P(), P(None, None, "lon"))
    return jax.shard_map(
        on_device,
        mesh=mesh,
        in_specs=placed,
        out_specs=(P(None, "lat", "lon"), P(None, "lat", "lon"), P(None, None, "lon")),
        check_vma=False,
    )
```

profile of v0, /device:TPU:0, one launch (start us, length us, event | category | flops | bytes accessed | tf_op | source)
XLA Modules:
  0.0 160.2 jit_solution(5387698934362358511)
XLA Ops:
  7.2 1.5 fusion.164
  8.7 3.0 %collective-permute-start = (f32[256,1,1]{2,1,0:T(1,128)S(1)}, f32[256,1,1]{2,1,0:T(1,128)S(1)}, u32[]{:S(2)}, u32[]{:S(2)}) collective-permute-start(f32[256,1,1]{2,1,0:T(1,128)S(1)} %get-tuple-element.54), channel_id=1, source_target_pairs={{0,1},{1,2},{2,3},{3,4},{4,5},{5,6},{6,7},{7,0},{8,9},{9,10},{10,1... | collective-permute-start | bytes 3080 | tf_op jit(solution)/shard_map/ppermute | solution.py:16
  11.7 3.1 %collective-permute-start.1 = (f32[256,1,1]{2,1,0:T(1,128)S(1)}, f32[256,1,1]{2,1,0:T(1,128)S(1)}, u32[]{:S(2)}, u32[]{:S(2)}) collective-permute-start(f32[256,1,1]{2,1,0:T(1,128)S(1)} %get-tuple-element.55), channel_id=1, source_target_pairs={{1,0},{2,1},{3,2},{4,3},{5,4},{6,5},{7,6},{0,7},{9,8},{10,9},{11,1... | collective-permute-start | bytes 3080 | tf_op jit(solution)/shard_map/ppermute | solution.py:17
  14.8 1.0 copy.14
  15.8 1.0 collective-permute-start.10
  16.8 1.6 %collective-permute-done = f32[256,1,1]{2,1,0:T(1,128)S(1)} collective-permute-done((f32[256,1,1]{2,1,0:T(1,128)S(1)}, f32[256,1,1]{2,1,0:T(1,128)S(1)}, u32[]{:S(2)}, u32[]{:S(2)}) %collective-permute-start) | collective-permute-done | bytes 1056 | tf_op jit(solution)/shard_map/ppermute | solution.py:16
  18.4 1.0 collective-permute-done.1
  19.4 1.8 %pad_maximum_fusion = f32[256,1,130]{2,1,0:T(1,128)S(1)} fusion(f32[256,1,1]{2,1,0:T(1,128)S(1)} %collective-permute-done.1, f32[256,1,128]{2,1,0:T(1,128)} %param.4, f32[256,1,1]{2,1,0:T(1,128)S(1)} %collective-permute-done), kind=kLoop, calls=%fused_computation.49 | loop fusion | flops 66560 | bytes 266240 | tf_op jit(solution)/shard_map/concatenate | solution.py:18
  21.2 1.3 collective-permute-start.3
  22.5 3.0 %collective-permute-start.2 = (f32[256,1,130]{2,1,0:T(1,128)S(1)}, f32[256,1,130]{2,1,0:T(1,128)S(1)}, u32[]{:S(2)}, u32[]{:S(2)}) collective-permute-start(f32[256,1,130]{2,1,0:T(1,128)S(1)} %pad_maximum_fusion), channel_id=1, source_target_pairs={{0,8},{8,16},{16,24},{1,9},{9,17},{17,25},{2,10},{10,18},{18,26},{... | collective-permute-start | bytes 399368 | tf_op jit(solution)/shard_map/ppermute | solution.py:16
  25.6 1.9 %pad_maximum_fusion.4 = (f32[256,1,128]{2,1,0:T(1,128)S(1)}, f32[256,1,128]{2,1,0:T(1,128)S(1)}) fusion(f32[256,1,1]{2,1,0:T(1,128)S(1)} %collective-permute-done.1, f32[256,1,128]{2,1,0:T(1,128)} %param.4, f32[256,1,1]{2,1,0:T(1,128)S(1)} %collective-permute-done), kind=kLoop, calls=%fused_computation.105 | loop fusion | flops 65536 | bytes 395264 | tf_op jit(solution)/shard_map/concatenate | solution.py:18
  33.1 2.3 %collective-permute-start.4 = (f32[2,256,1,128]{1,3,2,0:T(8,128)}, f32[2,256,1,128]{1,3,2,0:T(8,128)S(1)}, u32[]{:S(2)}, u32[]{:S(2)}) collective-permute-start(f32[2,256,1,128]{1,3,2,0:T(8,128)} %stack.108), channel_id=1, source_target_pairs={{0,4},{1,5},{2,6},{3,7},{4,0},{5,1},{6,2},{7,3},{8,12},{9,13},{10,... | collective-permute-start | bytes 786440 | tf_op jit(solution)/shard_map/ppermute | solution.py:23
  35.5 13.2 %collective-permute-done.4 = f32[2,256,1,128]{1,3,2,0:T(8,128)S(1)} collective-permute-done((f32[2,256,1,128]{1,3,2,0:T(8,128)}, f32[2,256,1,128]{1,3,2,0:T(8,128)S(1)}, u32[]{:S(2)}, u32[]{:S(2)}) %collective-permute-start.4) | collective-permute-done | bytes 262176 | tf_op jit(solution)/shard_map/ppermute | solution.py:23
  51.3 1.3 collective-permute-start.11
  52.7 6.6 %collective-permute-done.5 = f32[2,256,1,128]{1,3,2,0:T(8,128)} collective-permute-done((f32[2,256,1,128]{1,3,2,0:T(8,128)}, f32[2,256,1,128]{1,3,2,0:T(8,128)}, u32[]{:S(2)}, u32[]{:S(2)}) %collective-permute-start.5) | collective-permute-done | bytes 262176 | tf_op jit(solution)/shard_map/ppermute | solution.py:23
  59.3 1.0 fusion.186
  60.3 3.8 %collective-permute-done.11 = f32[2,256,1,128]{1,3,2,0:T(8,128)} collective-permute-done((f32[2,256,1,128]{1,3,2,0:T(8,128)}, f32[2,256,1,128]{1,3,2,0:T(8,128)}, u32[]{:S(2)}, u32[]{:S(2)}) %collective-permute-start.11) | collective-permute-done | bytes 262176 | tf_op jit(solution)/shard_map/ppermute | solution.py:23
  64.1 1.1 fusion.187
  65.4 1.0 maximum_select_fusion.7
  67.2 1.1 maximum_select_fusion.1
  68.3 1.4 collective-permute-start.6
  69.8 6.0 %collective-permute-done.12 = f32[2,256,1,128]{1,3,2,0:T(8,128)} collective-permute-done((f32[2,256,1,128]{1,3,2,0:T(8,128)S(1)}, f32[2,256,1,128]{1,3,2,0:T(8,128)}, u32[]{:S(2)}, u32[]{:S(2)}) %collective-permute-start.12) | collective-permute-done | bytes 262176 | tf_op jit(solution)/shard_map/ppermute | solution.py:23
  75.8 1.0 sub.170
  76.8 2.9 %collective-permute-done.6 = f32[2,256,1,128]{1,3,2,0:T(8,128)} collective-permute-done((f32[2,256,1,128]{1,3,2,0:T(8,128)S(1)}, f32[2,256,1,128]{1,3,2,0:T(8,128)}, u32[]{:S(2)}, u32[]{:S(2)}) %collective-permute-start.6) | collective-permute-done | bytes 262176 | tf_op jit(solution)/shard_map/ppermute | solution.py:23
  79.7 1.0 sub.155
  80.8 1.0 maximum_select_fusion.8
  83.0 1.0 maximum_select_fusion.2
  86.8 1.3 add_bitcast_fusion
  92.8 0.9 collective-permute-start.13
  93.7 1.3 collective-permute-start.7
  95.0 7.1 %collective-permute-done.13 = f32[2,256,1,128]{1,3,2,0:T(8,128)S(1)} collective-permute-done((f32[2,256,1,128]{1,3,2,0:T(8,128)S(1)}, f32[2,256,1,128]{1,3,2,0:T(8,128)S(1)}, u32[]{:S(2)}, u32[]{:S(2)}) %collective-permute-start.13) | collective-permute-done | bytes 262176 | tf_op jit(solution)/shard_map/ppermute | solution.py:23
  102.2 2.9 %collective-permute-done.7 = f32[2,256,1,128]{1,3,2,0:T(8,128)S(1)} collective-permute-done((f32[2,256,1,128]{1,3,2,0:T(8,128)S(1)}, f32[2,256,1,128]{1,3,2,0:T(8,128)S(1)}, u32[]{:S(2)}, u32[]{:S(2)}) %collective-permute-start.7) | collective-permute-done | bytes 262176 | tf_op jit(solution)/shard_map/ppermute | solution.py:23
  105.3 1.0 collective-permute-start.8
  107.0 1.1 collective-permute-start.14
  108.2 1.6 reverse_bitcast_fusion
  110.5 3.5 %collective-permute-done.8 = f32[2,256,1,128]{1,3,2,0:T(8,128)} collective-permute-done((f32[2,256,1,128]{1,3,2,0:T(8,128)S(1)}, f32[2,256,1,128]{1,3,2,0:T(8,128)}, u32[]{:S(2)}, u32[]{:S(2)}) %collective-permute-start.8) | collective-permute-done | bytes 262176 | tf_op jit(solution)/shard_map/ppermute | solution.py:23
  113.9 1.1 select_multiply_fusion.2
  115.1 1.7 %collective-permute-done.14 = f32[2,256,1,128]{1,3,2,0:T(8,128)} collective-permute-done((f32[2,256,1,128]{1,3,2,0:T(8,128)}, f32[2,256,1,128]{1,3,2,0:T(8,128)}, u32[]{:S(2)}, u32[]{:S(2)}) %collective-permute-start.14) | collective-permute-done | bytes 262176 | tf_op jit(solution)/shard_map/ppermute | solution.py:23
  116.7 1.0 select_multiply_fusion
  118.0 3.6 %collective-permute-start.15 = (f32[2,256,1,128]{1,3,2,0:T(8,128)S(1)}, f32[2,256,1,128]{1,3,2,0:T(8,128)}, u32[]{:S(2)}, u32[]{:S(2)}) collective-permute-start(f32[2,256,1,128]{1,3,2,0:T(8,128)S(1)} %maximum_select_fusion.11), channel_id=1, source_target_pairs={{0,4},{1,5},{2,6},{3,7},{4,0},{5,1},{6,2},{7,3},{8,12},{9,13},{10,... | collective-permute-start | bytes 786440 | tf_op jit(solution)/shard_map/ppermute | solution.py:23
  122.5 13.9 %collective-permute-done.15 = f32[2,256,1,128]{1,3,2,0:T(8,128)} collective-permute-done((f32[2,256,1,128]{1,3,2,0:T(8,128)S(1)}, f32[2,256,1,128]{1,3,2,0:T(8,128)}, u32[]{:S(2)}, u32[]{:S(2)}) %collective-permute-start.15) | collective-permute-done | bytes 262176 | tf_op jit(solution)/shard_map/ppermute | solution.py:23
  136.4 0.9 fusion.87
  137.3 1.5 collective-permute-start.16
  138.8 3.3 %collective-permute-start.17 = (f32[256,1,1]{0,2,1:T(1,128)S(1)}, f32[256,1,1]{0,2,1:T(1,128)S(1)}, u32[]{:S(2)}, u32[]{:S(2)}) collective-permute-start(f32[256,1,1]{0,2,1:T(1,128)S(1)} %get-tuple-element.47), channel_id=1, source_target_pairs={{1,0},{2,1},{3,2},{4,3},{5,4},{6,5},{7,6},{0,7},{9,8},{10,9},{11,1... | collective-permute-start | bytes 3080 | tf_op jit(solution)/shard_map/ppermute | solution.py:17
  142.1 1.2 fusion.19
  144.2 1.3 collective-permute-start.19
  145.5 3.0 %collective-permute-start.18 = (f32[256,1,130]{0,2,1:T(8,128)S(1)}, f32[256,1,130]{0,2,1:T(8,128)S(1)}, u32[]{:S(2)}, u32[]{:S(2)}) collective-permute-start(f32[256,1,130]{0,2,1:T(8,128)S(1)} %pad_maximum_fusion.1), channel_id=1, source_target_pairs={{0,8},{8,16},{16,24},{1,9},{9,17},{17,25},{2,10},{10,18},{18,26},{... | collective-permute-start | bytes 399368 | tf_op jit(solution)/shard_map/ppermute | solution.py:16
  151.7 1.7 %copy.23 = f32[2,256,128]{2,1,0:T(8,128)} copy(f32[2,256,128]{2,1,0:T(8,128)} %all-reduce.4.cloned.1.call-done) | data formatting | bytes 524288
  (110 shorter events, 24.7 us)
Async XLA Ops:
  7.2 20.3 %copy-start = (f32[3,3,256,256]{3,2,1,0:T(8,128)S(1)}, f32[3,3,256,256]{3,2,1,0:T(8,128)}, u32[]{:S(2)}) copy-start(f32[3,3,256,256]{3,2,1,0:T(8,128)} %param.6) | copy-start | bytes 7077892
  7.2 144.5 %all-reduce.4.cloned.1.call-start = ((), (), s32[]{:S(2)}) async-start(), calls=%async_computation | async-start | bytes 524288 | tf_op jit(solution)/shard_map/psum | solution.py:153
  8.7 9.8 %collective-permute-start = (f32[256,1,1]{2,1,0:T(1,128)S(1)}, f32[256,1,1]{2,1,0:T(1,128)S(1)}, u32[]{:S(2)}, u32[]{:S(2)}) collective-permute-start(f32[256,1,1]{2,1,0:T(1,128)S(1)} %get-tuple-element.54), channel_id=1, source_target_pairs={{0,1},{1,2},{2,3},{3,4},{4,5},{5,6},{6,7},{7,0},{8,9},{9,10},{10,1... | collective-permute-start | bytes 3080 | tf_op jit(solution)/shard_map/ppermute | solution.py:16
  11.7 7.8 %collective-permute-start.1 = (f32[256,1,1]{2,1,0:T(1,128)S(1)}, f32[256,1,1]{2,1,0:T(1,128)S(1)}, u32[]{:S(2)}, u32[]{:S(2)}) collective-permute-start(f32[256,1,1]{2,1,0:T(1,128)S(1)} %get-tuple-element.55), channel_id=1, source_target_pairs={{1,0},{2,1},{3,2},{4,3},{5,4},{6,5},{7,6},{0,7},{9,8},{10,9},{11,1... | collective-permute-start | bytes 3080 | tf_op jit(solution)/shard_map/ppermute | solution.py:17
  15.8 19.7 %collective-permute-start.10 = (f32[2,256,1,128]{1,3,2,0:T(8,128)S(1)}, f32[2,256,1,128]{1,3,2,0:T(8,128)S(1)}, u32[]{:S(2)}, u32[]{:S(2)}) collective-permute-start(f32[2,256,1,128]{1,3,2,0:T(8,128)S(1)} %stack.121), channel_id=1, source_target_pairs={{0,4},{1,5},{2,6},{3,7},{4,0},{5,1},{6,2},{7,3},{8,12},{9,13},{10,... | collective-permute-start | bytes 786440 | tf_op jit(solution)/shard_map/ppermute | solution.py:23
  21.2 6.6 %collective-permute-start.3 = (f32[256,1,130]{2,1,0:T(1,128)S(1)}, f32[256,1,130]{2,1,0:T(1,128)S(1)}, u32[]{:S(2)}, u32[]{:S(2)}) collective-permute-start(f32[256,1,130]{2,1,0:T(1,128)S(1)} %pad_maximum_fusion), channel_id=1, source_target_pairs={{8,0},{16,8},{24,16},{9,1},{17,9},{25,17},{10,2},{18,10},{26,18},{... | collective-permute-start | bytes 399368 | tf_op jit(solution)/shard_map/ppermute | solution.py:17
  22.5 6.4 %collective-permute-start.2 = (f32[256,1,130]{2,1,0:T(1,128)S(1)}, f32[256,1,130]{2,1,0:T(1,128)S(1)}, u32[]{:S(2)}, u32[]{:S(2)}) collective-permute-start(f32[256,1,130]{2,1,0:T(1,128)S(1)} %pad_maximum_fusion), channel_id=1, source_target_pairs={{0,8},{8,16},{16,24},{1,9},{9,17},{17,25},{2,10},{10,18},{18,26},{... | collective-permute-start | bytes 399368 | tf_op jit(solution)/shard_map/ppermute | solution.py:16
  27.4 3.3 %copy-start.2 = (f32[256,1,128]{2,1,0:T(1,128)S(1)}, f32[256,1,128]{2,1,0:T(1,128)}, u32[]{:S(2)}) copy-start(f32[256,1,128]{2,1,0:T(1,128)} %param.4) | copy-start | bytes 393220
  33.1 15.6 %collective-permute-start.4 = (f32[2,256,1,128]{1,3,2,0:T(8,128)}, f32[2,256,1,128]{1,3,2,0:T(8,128)S(1)}, u32[]{:S(2)}, u32[]{:S(2)}) collective-permute-start(f32[2,256,1,128]{1,3,2,0:T(8,128)} %stack.108), channel_id=1, source_target_pairs={{0,4},{1,5},{2,6},{3,7},{4,0},{5,1},{6,2},{7,3},{8,12},{9,13},{10,... | collective-permute-start | bytes 786440 | tf_op jit(solution)/shard_map/ppermute | solution.py:23
  48.9 1.6 copy-start.5
  48.9 2.3 %copy-start.7 = (f32[1,256,1,128]{1,3,2,0:T(8,128)}, f32[1,256,1,128]{1,3,2,0:T(8,128)S(1)}, u32[]{:S(2)}) copy-start(f32[1,256,1,128]{1,3,2,0:T(8,128)S(1)} %get-tuple-element.23) | copy-start | bytes 393220
  49.0 16.4 %copy-start.3 = (f32[1,256,1,128]{1,3,2,0:T(8,128)}, f32[1,256,1,128]{1,3,2,0:T(8,128)S(1)}, u32[]{:S(2)}) copy-start(f32[1,256,1,128]{1,3,2,0:T(8,128)S(1)} %get-tuple-element.68) | copy-start | bytes 393220
  49.0 16.4 %copy-start.4 = (f32[1,256,1,128]{1,3,2,0:T(8,128)}, f32[1,256,1,128]{1,3,2,0:T(8,128)S(1)}, u32[]{:S(2)}) copy-start(f32[1,256,1,128]{1,3,2,0:T(8,128)S(1)} %get-tuple-element.69) | copy-start | bytes 393220
  49.8 9.5 %collective-permute-start.5 = (f32[2,256,1,128]{1,3,2,0:T(8,128)}, f32[2,256,1,128]{1,3,2,0:T(8,128)}, u32[]{:S(2)}, u32[]{:S(2)}) collective-permute-start(f32[2,256,1,128]{1,3,2,0:T(8,128)} %maximum_select_fusion), channel_id=1, source_target_pairs={{0,2},{1,3},{2,0},{3,1},{4,6},{5,7},{6,4},{7,5},{8,10},{9,11},{10,... | collective-permute-start | bytes 786440 | tf_op jit(solution)/shard_map/ppermute | solution.py:23
  51.3 12.8 %collective-permute-start.11 = (f32[2,256,1,128]{1,3,2,0:T(8,128)}, f32[2,256,1,128]{1,3,2,0:T(8,128)}, u32[]{:S(2)}, u32[]{:S(2)}) collective-permute-start(f32[2,256,1,128]{1,3,2,0:T(8,128)} %maximum_select_fusion.6), channel_id=1, source_target_pairs={{0,2},{1,3},{2,0},{3,1},{4,6},{5,7},{6,4},{7,5},{8,10},{9,11},{10,... | collective-permute-start | bytes 786440 | tf_op jit(solution)/shard_map/ppermute | solution.py:23
  52.7 12.7 %copy-start.6 = (f32[1,256,1,128]{1,3,2,0:T(8,128)S(1)}, f32[1,256,1,128]{1,3,2,0:T(8,128)}, u32[]{:S(2)}) copy-start(f32[1,256,1,128]{1,3,2,0:T(8,128)} %copy-done.5) | copy-start | bytes 393220
  52.7 12.7 %copy-start.8 = (f32[1,256,1,128]{1,3,2,0:T(8,128)S(1)}, f32[1,256,1,128]{1,3,2,0:T(8,128)}, u32[]{:S(2)}) copy-start(f32[1,256,1,128]{1,3,2,0:T(8,128)} %copy-done.7) | copy-start | bytes 393220
  66.4 9.4 %collective-permute-start.12 = (f32[2,256,1,128]{1,3,2,0:T(8,128)S(1)}, f32[2,256,1,128]{1,3,2,0:T(8,128)}, u32[]{:S(2)}, u32[]{:S(2)}) collective-permute-start(f32[2,256,1,128]{1,3,2,0:T(8,128)S(1)} %maximum_select_fusion.7), channel_id=1, source_target_pairs={{0,1},{1,0},{2,3},{3,2},{4,5},{5,4},{6,7},{7,6},{8,9},{9,8},{10,11... | collective-permute-start | bytes 786440 | tf_op jit(solution)/shard_map/ppermute | solution.py:23
  68.3 11.4 %collective-permute-start.6 = (f32[2,256,1,128]{1,3,2,0:T(8,128)S(1)}, f32[2,256,1,128]{1,3,2,0:T(8,128)}, u32[]{:S(2)}, u32[]{:S(2)}) collective-permute-start(f32[2,256,1,128]{1,3,2,0:T(8,128)S(1)} %maximum_select_fusion.1), channel_id=1, source_target_pairs={{0,1},{1,0},{2,3},{3,2},{4,5},{5,4},{6,7},{7,6},{8,9},{9,8},{10,11... | collective-permute-start | bytes 786440 | tf_op jit(solution)/shard_map/ppermute | solution.py:23
  80.8 6.0 %copy-start.15 = (f32[2,256,128]{2,1,0:T(8,128)S(1)}, f32[2,256,128]{2,1,0:T(8,128)}, u32[]{:S(2)}) copy-start(f32[2,256,128]{2,1,0:T(8,128)} %param.7) | copy-start | bytes 786436
  92.8 9.3 %collective-permute-start.13 = (f32[2,256,1,128]{1,3,2,0:T(8,128)S(1)}, f32[2,256,1,128]{1,3,2,0:T(8,128)S(1)}, u32[]{:S(2)}, u32[]{:S(2)}) collective-permute-start(f32[2,256,1,128]{1,3,2,0:T(8,128)S(1)} %maximum_select_fusion.9), channel_id=1, source_target_pairs={{0,1},{1,0},{2,3},{3,2},{4,5},{5,4},{6,7},{7,6},{8,9},{9,8},{10,11... | collective-permute-start | bytes 786440 | tf_op jit(solution)/shard_map/ppermute | solution.py:23
  93.7 11.3 %collective-permute-start.7 = (f32[2,256,1,128]{1,3,2,0:T(8,128)S(1)}, f32[2,256,1,128]{1,3,2,0:T(8,128)S(1)}, u32[]{:S(2)}, u32[]{:S(2)}) collective-permute-start(f32[2,256,1,128]{1,3,2,0:T(8,128)S(1)} %maximum_select_fusion.3), channel_id=1, source_target_pairs={{0,1},{1,0},{2,3},{3,2},{4,5},{5,4},{6,7},{7,6},{8,9},{9,8},{10,11... | collective-permute-start | bytes 786440 | tf_op jit(solution)/shard_map/ppermute | solution.py:23
  105.2 1.1 copy-start.9
  105.3 1.8 %copy-start.10 = (f32[1,256,1,128]{1,3,2,0:T(8,128)}, f32[1,256,1,128]{1,3,2,0:T(8,128)S(1)}, u32[]{:S(2)}) copy-start(f32[1,256,1,128]{1,3,2,0:T(8,128)S(1)} %get-tuple-element.62) | copy-start | bytes 393220
  105.3 1.8 %copy-start.11 = (f32[1,256,1,128]{1,3,2,0:T(8,128)}, f32[1,256,1,128]{1,3,2,0:T(8,128)S(1)}, u32[]{:S(2)}) copy-start(f32[1,256,1,128]{1,3,2,0:T(8,128)S(1)} %get-tuple-element.63) | copy-start | bytes 393220
  105.3 8.6 %collective-permute-start.8 = (f32[2,256,1,128]{1,3,2,0:T(8,128)S(1)}, f32[2,256,1,128]{1,3,2,0:T(8,128)}, u32[]{:S(2)}, u32[]{:S(2)}) collective-permute-start(f32[2,256,1,128]{1,3,2,0:T(8,128)S(1)} %maximum_select_fusion.4), channel_id=1, source_target_pairs={{0,2},{1,3},{2,0},{3,1},{4,6},{5,7},{6,4},{7,5},{8,10},{9,11},{10,... | collective-permute-start | bytes 786440 | tf_op jit(solution)/shard_map/ppermute | solution.py:23
  107.0 9.7 %collective-permute-start.14 = (f32[2,256,1,128]{1,3,2,0:T(8,128)}, f32[2,256,1,128]{1,3,2,0:T(8,128)}, u32[]{:S(2)}, u32[]{:S(2)}) collective-permute-start(f32[2,256,1,128]{1,3,2,0:T(8,128)} %maximum_select_fusion.10), channel_id=1, source_target_pairs={{0,2},{1,3},{2,0},{3,1},{4,6},{5,7},{6,4},{7,5},{8,10},{9,11},{10,... | collective-permute-start | bytes 786440 | tf_op jit(solution)/shard_map/ppermute | solution.py:23
  110.5 11.2 %copy-start.13 = (f32[1,256,128]{2,1,0:T(8,128)S(1)}, f32[1,256,128]{2,1,0:T(8,128)}, u32[]{:S(2)}) copy-start(f32[1,256,128]{2,1,0:T(8,128)} %get-tuple-element.6) | copy-start | bytes 393220
  110.5 11.2 %copy-start.14 = (f32[1,256,128]{2,1,0:T(8,128)S(1)}, f32[1,256,128]{2,1,0:T(8,128)}, u32[]{:S(2)}) copy-start(f32[1,256,128]{2,1,0:T(8,128)} %get-tuple-element.7) | copy-start | bytes 393220
  115.0 27.1 %copy-start.1 = (f32[3,3,256,256]{2,3,1,0:T(8,128)S(1)}, f32[3,3,256,256]{2,3,1,0:T(8,128)}, u32[]{:S(2)}) copy-start(f32[3,3,256,256]{2,3,1,0:T(8,128)} %reverse_bitcast_fusion) | copy-start | bytes 7077892
  117.8 25.5 %copy-start.12 = (f32[256,1,128]{0,2,1:T(8,128)S(1)}, f32[256,1,128]{0,2,1:T(8,128)}, u32[]{:S(2)}) copy-start(f32[256,1,128]{0,2,1:T(8,128)} %copy.12) | copy-start | bytes 393220
  118.0 18.4 %collective-permute-start.15 = (f32[2,256,1,128]{1,3,2,0:T(8,128)S(1)}, f32[2,256,1,128]{1,3,2,0:T(8,128)}, u32[]{:S(2)}, u32[]{:S(2)}) collective-permute-start(f32[2,256,1,128]{1,3,2,0:T(8,128)S(1)} %maximum_select_fusion.11), channel_id=1, source_target_pairs={{0,4},{1,5},{2,6},{3,7},{4,0},{5,1},{6,2},{7,3},{8,12},{9,13},{10,... | collective-permute-start | bytes 786440 | tf_op jit(solution)/shard_map/ppermute | solution.py:23
  122.4 20.9 %collective-permute-start.9 = (f32[2,256,1,128]{1,3,2,0:T(8,128)S(1)}, f32[2,256,1,128]{1,3,2,0:T(8,128)S(1)}, u32[]{:S(2)}, u32[]{:S(2)}) collective-permute-start(f32[2,256,1,128]{1,3,2,0:T(8,128)S(1)} %maximum_select_fusion.5), channel_id=1, source_target_pairs={{0,4},{1,5},{2,6},{3,7},{4,0},{5,1},{6,2},{7,3},{8,12},{9,13},{10,... | collective-permute-start | bytes 786440 | tf_op jit(solution)/shard_map/ppermute | solution.py:23
  137.3 6.8 %collective-permute-start.16 = (f32[256,1,1]{0,2,1:T(1,128)S(1)}, f32[256,1,1]{0,2,1:T(1,128)S(1)}, u32[]{:S(2)}, u32[]{:S(2)}) collective-permute-start(f32[256,1,1]{0,2,1:T(1,128)S(1)} %get-tuple-element.46), channel_id=1, source_target_pairs={{0,1},{1,2},{2,3},{3,4},{4,5},{5,6},{6,7},{7,0},{8,9},{9,10},{10,1... | collective-permute-start | bytes 3080 | tf_op jit(solution)/shard_map/ppermute | solution.py:16
  138.8 5.3 %collective-permute-start.17 = (f32[256,1,1]{0,2,1:T(1,128)S(1)}, f32[256,1,1]{0,2,1:T(1,128)S(1)}, u32[]{:S(2)}, u32[]{:S(2)}) collective-permute-start(f32[256,1,1]{0,2,1:T(1,128)S(1)} %get-tuple-element.47), channel_id=1, source_target_pairs={{1,0},{2,1},{3,2},{4,3},{5,4},{6,5},{7,6},{0,7},{9,8},{10,9},{11,1... | collective-permute-start | bytes 3080 | tf_op jit(solution)/shard_map/ppermute | solution.py:17
  144.2 4.6 %collective-permute-start.19 = (f32[256,1,130]{0,2,1:T(8,128)S(1)}, f32[256,1,130]{0,2,1:T(8,128)S(1)}, u32[]{:S(2)}, u32[]{:S(2)}) collective-permute-start(f32[256,1,130]{0,2,1:T(8,128)S(1)} %pad_maximum_fusion.1), channel_id=1, source_target_pairs={{8,0},{16,8},{24,16},{9,1},{17,9},{25,17},{10,2},{18,10},{26,18},{... | collective-permute-start | bytes 399368 | tf_op jit(solution)/shard_map/ppermute | solution.py:17
  145.5 4.2 %collective-permute-start.18 = (f32[256,1,130]{0,2,1:T(8,128)S(1)}, f32[256,1,130]{0,2,1:T(8,128)S(1)}, u32[]{:S(2)}, u32[]{:S(2)}) collective-permute-start(f32[256,1,130]{0,2,1:T(8,128)S(1)} %pad_maximum_fusion.1), channel_id=1, source_target_pairs={{0,8},{8,16},{16,24},{1,9},{9,17},{17,25},{2,10},{10,18},{18,26},{... | collective-permute-start | bytes 399368 | tf_op jit(solution)/shard_map/ppermute | solution.py:16
Sparse Core Ops, SparseCore 0:
  122.5 29.1 all-reduce.3
where the time goes:
time: 161 us; the launch traced here: 160 us
  waiting for transfers between devices  64.3 us (40%)
  starting transfers between devices  35 us (22%)
  other arithmetic  19.2 us (12%)
  matrix products  16.9 us (10%)
  between operations  14.8 us (9%)
  local copies, waits for them, and re-layouts  10 us (6%)
    ppermute x12, waiting for transfers between devices, partner(): lax.ppermute(array, axis, [(i, i ^ 1 << stride) for i in range(lax.axis_s...  61.6 us
    ppermute x12, starting transfers between devices, partner(): lax.ppermute(array, axis, [(i, i ^ 1 << stride) for i in range(lax.axis_s...  15.4 us
    ppermute x4, starting transfers between devices, padded_2(): before = lax.ppermute(last, axis, up)  10.6 us
    ppermute x4, starting transfers between devices, padded_2(): after = lax.ppermute(leading, axis, down)  8.96 us
    dot_general x18, matrix products, apply_taps(): jnp.einsum('oi,iab->oab', taps[tap_row, tap_col], window, precision=precise)  7.13 us
    select_n x6, other arithmetic, forward_pairs(): data = jnp.where(upper, turned, data + other)  5.81 us
    unnamed x37, local copies, waits for them, and re-layouts  5.01 us
    sub x6, other arithmetic, forward_pairs(): differ = other - data  4.13 us
  transfers between devices with their start and end apart: 21, of which 12 were waited for; matrix products, arithmetic and copies ran while one was open for 16% of the time, Pallas kernels for 0%

commit v1 on v0

--- a/solution.py
+++ b/solution.py
@@ -1,9 +1,16 @@
+from functools import partial
+
 import jax
 import jax.numpy as jnp
+import numpy as np
 from jax import lax
+from jax.experimental import pallas as pl
+from jax.experimental.pallas import tpu as pltpu
 from jax.sharding import PartitionSpec as P
 
 precise = lax.Precision.HIGHEST
+three_pass = lax.Precision.HIGH
+ROOT_HALF = 0.5**0.5
 
 
 def padded_2(array, sides, width, wrap):
@@ -117,7 +124,7 @@
     return data[0]
 
 
-def on_device(field, cotangent, conv_weight, spectral_filter):
+def on_device_any_mesh(field, cotangent, conv_weight, spectral_filter):
     lat_rows = field.shape[1]
     columns = field.shape[2]
     total_len = columns * lax.axis_size("lon")
@@ -156,12 +163,316 @@
     return (output, input_grad, filter_grad)
 
 
+def reversed_bits(value, width):
+    return int(format(value, f"0{width}b")[::-1], 2)
+
+
+def iotas(rows, columns):
+    lane = lax.broadcasted_iota(jnp.int32, (rows, columns), 1)
+    row = lax.broadcasted_iota(jnp.int32, (rows, columns), 0)
+    return lane, row
+
+
+def conv_kernel(own_ref, other_ref, cot_ref, filter_ref, taps_ref, out_ref, taps, sems):
+    place = lax.axis_index("lat")
+    odd = lax.rem(place, 2)
+    side = 2 - 2 * odd
+    copies = [
+        pltpu.make_async_copy(taps_ref.at[1], taps.at[0], sems.at[0]),
+        pltpu.make_async_copy(taps_ref.at[side], taps.at[1], sems.at[1]),
+    ]
+    for copy in copies:
+        copy.start()
+    channels, columns = own_ref.shape
+    owners = channels // 8
+    out_ref[:, 0:8, :] = cot_ref[...].reshape(owners, 8, columns)
+    plane = filter_ref[place // 2].reshape(owners, 8, columns)
+    out_ref[:, 24:28, :] = jnp.where(odd == 0, plane[:, 0:4], plane[:, 4:8])
+    own = own_ref[...]
+    both = jnp.concatenate([own, other_ref[...]], axis=1)
+    for copy in copies:
+        copy.wait()
+    inner, outer = [], []
+    for tap_col in range(3):
+        side_part = jnp.dot(taps[1, tap_col], both, precision=three_pass)
+        inner.append(
+            jnp.dot(taps[0, tap_col], own, precision=three_pass) + side_part[:, columns:]
+        )
+        outer.append(side_part[:, :columns])
+    lane, row = iotas(channels, columns)
+    slot = lane - lax.rem(row, 8)
+    edges = jnp.zeros((channels, columns), jnp.float32)
+    for group, (left, middle, right) in enumerate((inner, outer)):
+        from_left = pltpu.roll(left, 1, 1)
+        from_right = pltpu.roll(right, columns - 1, 1)
+        main = (
+            middle
+            + jnp.where(lane == 0, 0.0, from_left)
+            + jnp.where(lane == columns - 1, 0.0, from_right)
+        )
+        out_ref[:, 8 + 8 * group : 16 + 8 * group, :] = main.reshape(owners, 8, columns)
+        edges = jnp.where(slot == 16 * group, left[:, columns - 1 :], edges)
+        edges = jnp.where(slot == 16 * group + 8, right[:, 0:1], edges)
+    edge_rows = jnp.sum(edges.reshape(owners, 8, columns), axis=1, keepdims=True)
+    out_ref[:, 28:32, :] = jnp.concatenate(
+        [edge_rows, jnp.zeros((owners, 3, columns), jnp.float32)], axis=1
+    )
+
+
+def transform_8(x):
+    s = [x[d] + x[d + 4] for d in range(4)]
+    t = [x[d] - x[d + 4] for d in range(4)]
+    plus, minus = ROOT_HALF * (t[1] + t[3]), ROOT_HALF * (t[1] - t[3])
+    return [
+        (s[0] + s[2] + (s[1] + s[3]), None),
+        (t[0] + minus, -t[2] - plus),
+        (s[0] - s[2], s[3] - s[1]),
+        (t[0] - minus, t[2] - plus),
+        (s[0] + s[2] - (s[1] + s[3]), None),
+    ]
+
+
+def spectral_kernel(in_ref, turn_ref, dft_ref, out_ref, work):
+    rows, lon = 4, 8
+    columns = in_ref.shape[-1]
+    lane, sub = iotas(8, columns)
+    me = lax.axis_index("lat") * lon + lax.axis_index("lon")
+    inward = {1: 2, 2: 1}
+
+    def edge(row, place, group):
+        picked = jnp.where(lane == sub + 8 * group, in_ref[row * lon + place, 28:29, :], 0.0)
+        if row in inward:
+            also = in_ref[inward[row] * lon + place, 28:29, :]
+            picked = picked + jnp.where(lane == sub + 8 * group + 16, also, 0.0)
+        return jnp.sum(picked, axis=1, keepdims=True)
+
+    grid = []
+    for place in range(lon):
+        mixed = []
+        for row in range(rows):
+            tile = in_ref[row * lon + place, 8:16, :]
+            if row in inward:
+                tile = tile + in_ref[inward[row] * lon + place, 16:24, :]
+            tile = tile + jnp.where(lane == 0, edge(row, (place - 1) % lon, 0), 0.0)
+            tile = tile + jnp.where(lane == columns - 1, edge(row, (place + 1) % lon, 1), 0.0)
+            mixed.append(tile)
+        cot = [in_ref[row * lon + place, 0:8, :] for row in range(rows)]
+        grid.append(jnp.concatenate(mixed + cot, axis=0))
+    pairs = transform_8(grid)
+    height = 16 * rows
+    for residue in range(lon):
+        real, imag = pairs[min(residue, lon - residue)]
+        cosine, sine = turn_ref[residue : residue + 1, :], turn_ref[8 + residue : 9 + residue, :]
+        if imag is None:
+            turned = (real * cosine, -real * sine)
+        elif residue < 4:
+            turned = (real * cosine + imag * sine, imag * cosine - real * sine)
+        else:
+            turned = (real * cosine - imag * sine, -imag * cosine - real * sine)
+        span = pl.ds(residue * height, height)
+        work[span, 0:columns] = turned[0]
+        work[span, columns:] = turned[1]
+    spectra = jnp.dot(work[...], dft_ref[...], precision=three_pass)
+    scale = 1.0 / (lon * columns)
+    half = 8 * rows
+    gradients = []
+    for residue in range(lon):
+        place = reversed_bits(residue, 3)
+        part = spectra[residue * height : (residue + 1) * height]
+        mix_re, mix_im = part[:half, :columns], part[:half, columns:]
+        cot_re, cot_im = part[half:, :columns], part[half:, columns:]
+        quarters = [in_ref[row * lon + place, 24:28, :] * scale for row in range(rows)]
+        gain_re = jnp.concatenate([jnp.concatenate(quarters[0:2], axis=0)] * rows, axis=0)
+        gain_im = jnp.concatenate([jnp.concatenate(quarters[2:4], axis=0)] * rows, axis=0)
+        top = pl.ds(residue * height, half)
+        bottom = pl.ds(residue * height + half, half)
+        work[top, 0:columns] = gain_re * mix_re - gain_im * mix_im
+        work[top, columns:] = -(gain_re * mix_im + gain_im * mix_re)
+        work[bottom, 0:columns] = gain_re * cot_re + gain_im * cot_im
+        work[bottom, columns:] = gain_im * cot_re - gain_re * cot_im
+        grad_re = (mix_re * cot_re + mix_im * cot_im) * scale
+        grad_im = (mix_re * cot_im - mix_im * cot_re) * scale
+        gradients.append(
+            [
+                grad[0:8] + grad[8:16] + (grad[16:24] + grad[24:32])
+                for grad in (grad_re, grad_im)
+            ]
+        )
+    back = jnp.dot(work[...], dft_ref[...], precision=three_pass)
+    turned = []
+    for residue in range(lon):
+        part = back[residue * height : (residue + 1) * height]
+        real, imag = part[:, :columns], part[:, columns:]
+        cosine, sine = turn_ref[residue : residue + 1, :], turn_ref[8 + residue : 9 + residue, :]
+        turned.append((real * cosine + imag * sine, real * sine - imag * cosine))
+    sums = [turned[r][0] + turned[lon - r][0] for r in (1, 2, 3)]
+    gaps = [turned[r][1] - turned[lon - r][1] for r in (1, 2, 3)]
+    first, fourth = turned[0][0], turned[4][0]
+    even = [
+        first + fourth + sums[1],
+        first - fourth - gaps[1],
+        first + fourth - sums[1],
+        first - fourth + gaps[1],
+    ]
+    swing = [
+        sums[0] + sums[2],
+        ROOT_HALF * (sums[0] - gaps[0] - sums[2] - gaps[2]),
+        gaps[2] - gaps[0],
+        ROOT_HALF * (sums[2] - gaps[2] - sums[0] - gaps[0]),
+    ]
+    series = [even[d] + swing[d] for d in range(4)] + [even[d] - swing[d] for d in range(4)]
+    base = 8 * lax.rem(me, 16)
+    left_slot = lane == base + sub
+    right_slot = lane == base + lax.rem(sub + 4, 8)
+    for place in range(lon):
+        residue = reversed_bits(place, 3)
+        before, after = series[(place - 1) % lon], series[(place + 1) % lon]
+        tiles, rims = [], []
+        for row in range(rows):
+            span = slice(half + 8 * row, half + 8 * row + 8)
+            tiles.append(series[place][span])
+            rims.append(
+                jnp.where(left_slot, before[span, columns - 1 :], 0.0)
+                + jnp.where(right_slot, after[span, 0:1], 0.0)
+            )
+        for row in range(rows):
+            owner = row * lon + place
+            part, start = row % 2, row // 2
+            out_ref[owner, 0:8, :] = series[place][8 * row : 8 * row + 8]
+            for step in range(3):
+                out_ref[owner, 8 + 4 * step : 12 + 4 * step, :] = tiles[start + step][
+                    4 * part : 4 * part + 4
+                ]
+            out_ref[owner, 20:28, :] = gradients[residue][part]
+            lines = [
+                jnp.sum(rims[start + step][4 * part : 4 * part + 4], axis=0, keepdims=True)
+                for step in range(3)
+            ]
+            lines.append(jnp.zeros((1, columns), jnp.float32))
+            out_ref[owner, 28:32, :] = jnp.concatenate(lines, axis=0)
+
+
+def adjoint_kernel(
+    mine_ref, other_ref, field_ref, cot_ref, taps_ref, out_ref, grad_ref, gain_ref, taps, rows_ref, sem
+):
+    copy = pltpu.make_async_copy(taps_ref, taps, sem)
+    copy.start()
+    channels, columns = field_ref.shape
+    owners = channels // 8
+    place = lax.axis_index("lat")
+    part = lax.rem(place, 2)
+    index = place - place // 2
+    out_ref[...] = field_ref[...] + mine_ref[:, 0:8, :].reshape(channels, columns)
+    mine, other = mine_ref[:, 20:28, :], other_ref[:, 20:28, :]
+    gain_ref[0] = jnp.where(part == 0, mine, other).reshape(channels, columns)
+    gain_ref[1] = jnp.where(part == 0, other, mine).reshape(channels, columns)
+    lane, _ = iotas(4, columns)
+    lower = lax.rem(lane // 4, 2) == 0
+    own_slot = lax.rem(lane // 4, 2) == part
+    lefts, rights = [], []
+    for first in (0, owners // 2):
+        mine = jnp.sum(mine_ref[first : first + owners // 2, 28:32, :], axis=0)
+        other = jnp.sum(other_ref[first : first + owners // 2, 28:32, :], axis=0)
+        lefts.append(jnp.where(own_slot, mine, other))
+        swapped = jnp.where(own_slot, other, mine)
+        rights.append(
+            jnp.where(lower, pltpu.roll(swapped, columns - 4, 1), pltpu.roll(swapped, 4, 1))
+        )
+    left = jnp.concatenate(lefts, axis=1)
+    right = jnp.concatenate(rights, axis=1)
+    rows_ref[0] = jnp.zeros(rows_ref.shape[1:], jnp.float32)
+    rows_ref[4] = jnp.zeros(rows_ref.shape[1:], jnp.float32)
+    for step in range(3):
+        span = slice(8 + 4 * step, 12 + 4 * step)
+        mine, other = mine_ref[:, span, :], other_ref[:, span, :]
+        tile = jnp.concatenate(
+            [jnp.where(part == 0, mine, other), jnp.where(part == 0, other, mine)], axis=1
+        )
+        rows_ref[1 + step, 8 : 8 + columns, :] = tile.reshape(channels, columns).T
+        rows_ref[1 + step, 7:8, :] = left[step : step + 1]
+        rows_ref[1 + step, 8 + columns : 9 + columns, :] = right[step : step + 1]
+    copy.wait()
+    total = jnp.zeros((columns, channels), jnp.float32)
+    for tap_row in range(3):
+        for tap_col in range(3):
+            window = rows_ref[index + 2 - tap_row, 9 - tap_col : 9 - tap_col + columns, :]
+            total = total + jnp.dot(window, taps[tap_row, tap_col], precision=three_pass)
+    grad_ref[...] = cot_ref[...] + total.T
+
+
+def transform_tables(columns, lon):
+    places = np.arange(columns)
+    turn = 2.0 * np.pi * (np.arange(lon)[:, None] * places[None, :]) / (lon * columns)
+    angle = 2.0 * np.pi * (places[:, None] * places[None, :] % columns) / columns
+    cosine, sine = np.cos(angle), np.sin(angle)
+    dft = np.block([[cosine, -sine], [sine, cosine]])
+    turns = np.concatenate([np.cos(turn), np.sin(turn)], axis=0)
+    return jnp.asarray(turns, jnp.float32), jnp.asarray(dft, jnp.float32)
+
+
+def on_device(field, cotangent, conv_weight, spectral_filter):
+    channels, _, columns = field.shape
+    lat, lon = lax.axis_size("lat"), lax.axis_size("lon")
+    owners = lat * lon
+    swap = [(i, i ^ 1) for i in range(lat)]
+    own = field.reshape(channels, columns)
+    cot = cotangent.reshape(channels, columns)
+    vmem = pl.BlockSpec(memory_space=pltpu.VMEM)
+    hbm = pl.BlockSpec(memory_space=pl.ANY)
+    params = pltpu.CompilerParams(vmem_limit_bytes=24 * 1024 * 1024)
+    message = jax.ShapeDtypeStruct((owners, 32, columns), jnp.float32)
+    outgoing = pl.pallas_call(
+        conv_kernel,
+        out_shape=message,
+        in_specs=[vmem, vmem, vmem, vmem, hbm],
+        out_specs=vmem,
+        scratch_shapes=[
+            pltpu.VMEM((2,) + conv_weight.shape[1:], jnp.float32),
+            pltpu.SemaphoreType.DMA((2,)),
+        ],
+        compiler_params=params,
+        name="conv",
+    )(own, lax.ppermute(own, "lat", swap), cot, spectral_filter, conv_weight)
+    owned = lax.all_to_all(outgoing, ("lat", "lon"), 0, 0, tiled=True)
+    turns, dft = transform_tables(columns, lon)
+    returned = pl.pallas_call(
+        spectral_kernel,
+        out_shape=message,
+        in_specs=[vmem] * 3,
+        out_specs=vmem,
+        scratch_shapes=[pltpu.VMEM((2 * 8 * lat * lon, 2 * columns), jnp.float32)],
+        compiler_params=params,
+        name="spectral",
+    )(owned, turns, dft)
+    mine = lax.all_to_all(returned, ("lat", "lon"), 0, 0, tiled=True)
+    other = lax.ppermute(mine, "lat", swap)
+    flat = jax.ShapeDtypeStruct((channels, columns), jnp.float32)
+    output, input_grad, filter_grad = pl.pallas_call(
+        adjoint_kernel,
+        out_shape=(flat, flat, jax.ShapeDtypeStruct(spectral_filter.shape, jnp.float32)),
+        in_specs=[vmem, vmem, vmem, vmem, hbm],
+        out_specs=(vmem, vmem, vmem),
+        scratch_shapes=[
+            pltpu.VMEM(conv_weight.shape, jnp.float32),
+            pltpu.VMEM((5, columns + 16, channels), jnp.float32),
+            pltpu.SemaphoreType.DMA,
+        ],
+        compiler_params=params,
+        name="adjoint",
+    )(mine, other, own, cot, conv_weight)
+    return (output.reshape(field.shape), input_grad.reshape(field.shape), filter_grad)
+
+
 def solution(mesh):
     placed = (P(None, "lat", "lon"), P(None, "lat", "lon"), P(), P(None, None, "lon"))
-    return jax.shard_map(
-        on_device,
-        mesh=mesh,
-        in_specs=placed,
-        out_specs=(P(None, "lat", "lon"), P(None, "lat", "lon"), P(None, None, "lon")),
-        check_vma=False,
-    )
+    specs = (P(None, "lat", "lon"), P(None, "lat", "lon"), P(None, None, "lon"))
+
+    def layer(field, cotangent, conv_weight, spectral_filter):
+        lat, lon = mesh.shape["lat"], mesh.shape["lon"]
+        channels, rows, length = field.shape
+        owned = rows == lat == 4 and lon == 8 and channels == 8 * lat * lon and length == 128 * lon
+        body = on_device if owned else on_device_any_mesh
+        mapped = jax.shard_map(body, mesh=mesh, in_specs=placed, out_specs=specs, check_vma=False)
+        return mapped(field, cotangent, conv_weight, spectral_filter)
+
+    return layer

time: 161 us -> 55.2 us (0.34)
  waiting for transfers between devices: 64.3 us -> 3.1 us
  blocking collectives: 0 us -> 41.8 us
  starting transfers between devices: 35 us -> 0.52 us
  other arithmetic: 19.2 us -> 0 us
  matrix products: 16.9 us -> 0 us
  between operations: 14.8 us -> 0.68 us
  local copies, waits for them, and re-layouts: 10 us -> 4.45 us
  Pallas kernels: 0 us -> 4.36 us
    ppermute x20 -> x2, waiting for transfers between devices: 64.2 us -> 3.1 us  [the longest x1 1.91 us: on_device(): other = lax.ppermute(mine, 'lat', swap)]
    all_to_all x0 -> x2, blocking collectives: none -> 41.8 us  [the longest x1 23.4 us: on_device(): owned = lax.all_to_all(outgoing, ('lat', 'lon'), 0, 0, tiled=True)]
    ppermute x20 -> x2, starting transfers between devices: 34.9 us -> 0.52 us  [the longest x1 0.52 us: on_device(): lax.ppermute(own, 'lat', swap)]
    dot_general x34 -> x0, matrix products: 16.9 us -> none  [the longest x18 7.13 us: apply_taps(): jnp.einsum('oi,iab->oab', taps[tap_row, tap_col], window, precision=precise)]
    select_n x12 -> x0, other arithmetic: 6.73 us -> none  [the longest x6 5.81 us: forward_pairs(): data = jnp.where(upper, turned, data + other)]
    sub x8 -> x0, other arithmetic: 4.4 us -> none  [the longest x6 4.13 us: forward_pairs(): differ = other - data]
    pallas_call x0 -> x3, Pallas kernels: none -> 4.36 us  [the longest x1 1.98 us: on_device(): pl.pallas_call(adjoint_kernel, out_shape=(flat, flat, jax.ShapeDtypeStruc...]
    concatenate x3 -> x0, other arithmetic: 3.65 us -> none  [padded_2(): array = jnp.concatenate([before, array, after], axis=dim)]
  transfers between devices with their start and end apart: 21 -> 2, of which waited for: 12 -> 2; matrix products, arithmetic and copies ran while one was open for 16% -> 0% of each run, Pallas kernels for 0% -> 0%
where the time goes in v1:
time: 55.2 us; the launch traced here: 54.9 us
  blocking collectives  41.8 us (76%)
  local copies, waits for them, and re-layouts  4.45 us (8%)
  Pallas kernels  4.36 us (8%)
  waiting for transfers between devices  3.1 us (6%)
  between operations  0.68 us (1%)
    all_to_all x1, blocking collectives, on_device(): owned = lax.all_to_all(outgoing, ('lat', 'lon'), 0, 0, tiled=True)  23.4 us
    all_to_all x1, blocking collectives, on_device(): mine = lax.all_to_all(returned, ('lat', 'lon'), 0, 0, tiled=True)  18.4 us
    unnamed x18, local copies, waits for them, and re-layouts  4.45 us
    pallas_call x1, Pallas kernels, on_device(): pl.pallas_call(adjoint_kernel, out_shape=(flat, flat, jax.ShapeDtypeStruc...  1.98 us
    ppermute x1, waiting for transfers between devices, on_device(): other = lax.ppermute(mine, 'lat', swap)  1.91 us
    pallas_call x1, Pallas kernels, on_device(): pl.pallas_call(spectral_kernel, out_shape=message, in_specs=[vmem] * 3, o...  1.28 us
    ppermute x1, waiting for transfers between devices, on_device(): lax.ppermute(own, 'lat', swap)  1.2 us
    pallas_call x1, Pallas kernels, on_device(): pl.pallas_call(conv_kernel, out_shape=message, in_specs=[vmem, vmem, vmem...  1.11 us
  transfers between devices with their start and end apart: 2, of which 2 were waited for; matrix products, arithmetic and copies ran while one was open for 0% of the time, Pallas kernels for 0%

profile of v1, /device:TPU:0, one launch (start us, length us, event | category | flops | bytes accessed | tf_op | source)
XLA Modules:
  0.0 54.9 jit_solution(17061087100096734272)
XLA Ops:
  0.6 0.5 collective-permute-start
  1.1 1.2 %collective-permute-done.other_ref = f32[256,128]{1,0:T(8,128)S(1)} collective-permute-done((f32[256,128]{1,0:T(8,128)}, f32[256,128]{1,0:T(8,128)S(1)}, u32[]{:S(2)}, u32[]{:S(2)}) %collective-permute-start) | collective-permute-done | bytes 131104 | tf_op jit(solution)/shard_map/ppermute | solution.py:435
  2.3 0.0 copy-start
  2.3 1.7 %copy-done = f32[3,3,256,256]{3,2,1,0:T(8,128)S(1)} copy-done((f32[3,3,256,256]{3,2,1,0:T(8,128)S(1)}, f32[3,3,256,256]{3,2,1,0:T(8,128)}, u32[]{:S(2)}) %copy-start) | copy-done | bytes 2359320
  4.0 0.0 copy-start.2
  4.0 0.9 %copy-done.2 = f32[256,1,128]{2,1,0:T(1,128)S(1)} copy-done((f32[256,1,128]{2,1,0:T(1,128)S(1)}, f32[256,1,128]{2,1,0:T(1,128)}, u32[]{:S(2)}) %copy-start.2) | copy-done | bytes 131096
  4.9 0.0 copy-start.4
  4.9 0.9 %copy-done.4 = f32[256,1,128]{2,1,0:T(1,128)S(1)} copy-done((f32[256,1,128]{2,1,0:T(1,128)S(1)}, f32[256,1,128]{2,1,0:T(1,128)}, u32[]{:S(2)}) %copy-start.4) | copy-done | bytes 131096
  5.8 0.0 copy-start.6
  5.8 0.9 %copy-done.6 = f32[2,256,128]{2,1,0:T(8,128)S(1)} copy-done((f32[2,256,128]{2,1,0:T(8,128)S(1)}, f32[2,256,128]{2,1,0:T(8,128)}, u32[]{:S(2)}) %copy-start.6) | copy-done | bytes 262168
  6.8 0.0 copy-start.7
  6.8 0.0 copy-start.8
  6.8 1.1 %conv.1 = f32[32,32,128]{2,1,0:T(8,128)S(1)} custom-call(f32[256,128]{1,0:T(8,128)S(1)} %bitcast.9, f32[256,128]{1,0:T(8,128)S(1)} %collective-permute-done.other_ref, f32[256,128]{1,0:T(8,128)S(1)} %bitcast.11, f32[2,256,128]{2,1,0:T(8,128)S(1)} %copy-done.6, f32[3,3,256,256]{3,2,1,0:T(8,128)S(1)} %copy-done), custom_call_target="tpu_custom_call" | custom-call | tf_op jit(solution)/shard_map/conv/pallas_call | solution.py:424
  7.9 0.0 copy-start.1
  7.9 0.0 copy-start.3
  7.9 0.0 copy-start.5
  7.9 23.4 %all_to_all.10.in_ref = f32[32,32,128]{2,1,0:T(8,128)S(1)} all-to-all(f32[32,32,128]{2,1,0:T(8,128)S(1)} %conv.1), channel_id=1, replica_groups=mesh['lat'=4,'lon'=8] {'lat','lon'}, dimensions={0} | all-to-all | bytes 1048576 | tf_op jit(solution)/shard_map/all_to_all | solution.py:436
  31.3 0.0 copy-done.7
  31.3 0.0 copy-done.8
  31.3 1.3 %spectral.1 = f32[32,32,128]{2,1,0:T(8,128)S(1)} custom-call(f32[32,32,128]{2,1,0:T(8,128)S(1)} %all_to_all.10.in_ref, f32[16,128]{1,0:T(8,128)S(1)} %copy-done.8, f32[256,256]{1,0:T(8,128)S(1)} %copy-done.7), custom_call_target="tpu_custom_call" | custom-call | tf_op jit(solution)/shard_map/spectral/pallas_call | solution.py:438
  32.6 18.4 %all_to_all.11.mine_ref = f32[32,32,128]{2,1,0:T(8,128)S(1)} all-to-all(f32[32,32,128]{2,1,0:T(8,128)S(1)} %spectral.1), channel_id=1, replica_groups=mesh['lat'=4,'lon'=8] {'lat','lon'}, dimensions={0} | all-to-all | bytes 1048576 | tf_op jit(solution)/shard_map/all_to_all | solution.py:447
  51.0 0.0 collective-permute-start.1
  51.0 1.9 %collective-permute-done.1.other_ref = f32[32,32,128]{2,1,0:T(8,128)S(1)} collective-permute-done((f32[32,32,128]{2,1,0:T(8,128)S(1)}, f32[32,32,128]{2,1,0:T(8,128)S(1)}, u32[]{:S(2)}, u32[]{:S(2)}) %collective-permute-start.1) | collective-permute-done | bytes 524320 | tf_op jit(solution)/shard_map/ppermute | solution.py:448
  52.9 0.0 copy-done.1
  52.9 0.0 copy-done.3
  52.9 0.0 copy-done.5
  52.9 2.0 %adjoint.1 = (f32[256,128]{1,0:T(8,128)}, f32[256,128]{1,0:T(8,128)}, f32[2,256,128]{2,1,0:T(8,128)}) custom-call(f32[32,32,128]{2,1,0:T(8,128)S(1)} %all_to_all.11.mine_ref, f32[32,32,128]{2,1,0:T(8,128)S(1)} %collective-permute-done.1.other_ref, f32[256,128]{1,0:T(8,128)S(1)} %bitcast.10, f32[256,128]{1,0:T(8,128)S(1)} %bitcast.12, ...), custom_call_target="tpu_custom_call" | custom-call | tf_op jit(solution)/shard_map/adjoint/pallas_call | solution.py:450
Async XLA Ops:
  0.6 1.7 %collective-permute-start = (f32[256,128]{1,0:T(8,128)}, f32[256,128]{1,0:T(8,128)S(1)}, u32[]{:S(2)}, u32[]{:S(2)}) collective-permute-start(f32[256,128]{1,0:T(8,128)} %bitcast.8), channel_id=1, source_target_pairs={{0,8},{8,0},{16,24},{24,16},{1,9},{9,1},{17,25},{25,17},{2,10},{10... | collective-permute-start | bytes 393224 | tf_op jit(solution)/shard_map/ppermute | solution.py:435
  2.3 1.7 %copy-start = (f32[3,3,256,256]{3,2,1,0:T(8,128)S(1)}, f32[3,3,256,256]{3,2,1,0:T(8,128)}, u32[]{:S(2)}) copy-start(f32[3,3,256,256]{3,2,1,0:T(8,128)} %taps_ref.3) | copy-start | bytes 7077892
  4.0 0.9 %copy-start.2 = (f32[256,1,128]{2,1,0:T(1,128)S(1)}, f32[256,1,128]{2,1,0:T(1,128)}, u32[]{:S(2)}) copy-start(f32[256,1,128]{2,1,0:T(1,128)} %param.6) | copy-start | bytes 393220
  4.9 0.9 %copy-start.4 = (f32[256,1,128]{2,1,0:T(1,128)S(1)}, f32[256,1,128]{2,1,0:T(1,128)}, u32[]{:S(2)}) copy-start(f32[256,1,128]{2,1,0:T(1,128)} %param.7) | copy-start | bytes 393220
  5.8 0.9 %copy-start.6 = (f32[2,256,128]{2,1,0:T(8,128)S(1)}, f32[2,256,128]{2,1,0:T(8,128)}, u32[]{:S(2)}) copy-start(f32[2,256,128]{2,1,0:T(8,128)} %filter_ref.1) | copy-start | bytes 786436
  6.8 24.5 %copy-start.7 = (f32[256,256]{1,0:T(8,128)S(1)}, f32[256,256]{1,0:T(8,128)}, u32[]{:S(2)}) copy-start(f32[256,256]{1,0:T(8,128)} %constant.5.clone.dft_ref) | copy-start | bytes 786436
  6.8 24.5 %copy-start.8 = (f32[16,128]{1,0:T(8,128)S(1)}, f32[16,128]{1,0:T(8,128)}, u32[]{:S(2)}) copy-start(f32[16,128]{1,0:T(8,128)} %constant.4.clone.turn_ref) | copy-start | bytes 24580
  7.9 45.0 %copy-start.1 = (f32[3,3,256,256]{3,2,1,0:T(8,128)S(1)}, f32[3,3,256,256]{3,2,1,0:T(8,128)}, u32[]{:S(2)}) copy-start(f32[3,3,256,256]{3,2,1,0:T(8,128)} %taps_ref.3) | copy-start | bytes 7077892
  7.9 45.0 %copy-start.3 = (f32[256,1,128]{2,1,0:T(1,128)S(1)}, f32[256,1,128]{2,1,0:T(1,128)}, u32[]{:S(2)}) copy-start(f32[256,1,128]{2,1,0:T(1,128)} %param.6) | copy-start | bytes 393220
  7.9 45.0 %copy-start.5 = (f32[256,1,128]{2,1,0:T(1,128)S(1)}, f32[256,1,128]{2,1,0:T(1,128)}, u32[]{:S(2)}) copy-start(f32[256,1,128]{2,1,0:T(1,128)} %param.7) | copy-start | bytes 393220
  51.0 1.9 %collective-permute-start.1 = (f32[32,32,128]{2,1,0:T(8,128)S(1)}, f32[32,32,128]{2,1,0:T(8,128)S(1)}, u32[]{:S(2)}, u32[]{:S(2)}) collective-permute-start(f32[32,32,128]{2,1,0:T(8,128)S(1)} %all_to_all.11.mine_ref), channel_id=1, source_target_pairs={{0,8},{8,0},{16,24},{24,16},{1,9},{9,1},{17,25},{25,17},{2,10},{10... | collective-permute-start | bytes 1572872 | tf_op jit(solution)/shard_map/ppermute | solution.py:448

commit v2 on v1

--- a/solution.py
+++ b/solution.py
@@ -163,6 +163,9 @@
     return (output, input_grad, filter_grad)
 
 
+FORTH, BACK = 25, 29
+
+
 def reversed_bits(value, width):
     return int(format(value, f"0{width}b")[::-1], 2)
 
@@ -173,50 +176,63 @@
     return lane, row
 
 
-def conv_kernel(own_ref, other_ref, cot_ref, filter_ref, taps_ref, out_ref, taps, sems):
+def fetch_kernel(own_ref, cot_ref, filter_ref, taps_ref, own_out, taps_out, out_ref, cot, gain, sems):
     place = lax.axis_index("lat")
-    odd = lax.rem(place, 2)
-    side = 2 - 2 * odd
+    half = gain.shape[0]
+    start = pl.multiple_of(lax.rem(place, 2) * half, half)
     copies = [
-        pltpu.make_async_copy(taps_ref.at[1], taps.at[0], sems.at[0]),
-        pltpu.make_async_copy(taps_ref.at[side], taps.at[1], sems.at[1]),
+        pltpu.make_async_copy(cot_ref, cot, sems.at[0]),
+        pltpu.make_async_copy(filter_ref.at[place // 2, pl.ds(start, half)], gain, sems.at[1]),
+        pltpu.make_async_copy(own_ref, own_out, sems.at[2]),
+        pltpu.make_async_copy(taps_ref, taps_out, sems.at[3]),
     ]
     for copy in copies:
         copy.start()
+    copies[0].wait()
+    copies[1].wait()
+    for owner in range(half // 4):
+        first, here = FORTH * owner, slice(4 * owner, 4 * owner + 4)
+        out_ref[first : first + 4, :] = cot[here]
+        out_ref[first + 4 : first + 8, :] = cot[half + 4 * owner : half + 4 * owner + 4]
+        out_ref[first + 20 : first + 24, :] = gain[here]
+    copies[2].wait()
+    copies[3].wait()
+
+
+def conv_kernel(own_ref, other_ref, taps_ref, packed_ref, out_ref):
+    place = lax.axis_index("lat")
+    odd = lax.rem(place, 2)
     channels, columns = own_ref.shape
-    owners = channels // 8
-    out_ref[:, 0:8, :] = cot_ref[...].reshape(owners, 8, columns)
-    plane = filter_ref[place // 2].reshape(owners, 8, columns)
-    out_ref[:, 24:28, :] = jnp.where(odd == 0, plane[:, 0:4], plane[:, 4:8])
-    own = own_ref[...]
-    both = jnp.concatenate([own, other_ref[...]], axis=1)
-    for copy in copies:
-        copy.wait()
-    inner, outer = [], []
+    half = channels // 2
+    side, cross = 2 - 2 * odd, 2 * (place // 2)
+    start = pl.multiple_of(odd * half, half)
+    own, other = own_ref[...], other_ref[...]
+    near = jnp.where(jnp.logical_or(place == 1, place == 2), own, other)
+    parts = []
     for tap_col in range(3):
-        side_part = jnp.dot(taps[1, tap_col], both, precision=three_pass)
-        inner.append(
-            jnp.dot(taps[0, tap_col], own, precision=three_pass) + side_part[:, columns:]
+        inner = jnp.dot(taps_ref[1, tap_col], own, precision=three_pass)
+        inner = inner + jnp.dot(taps_ref[side, tap_col], other, precision=three_pass)
+        outer = jnp.dot(taps_ref[cross, tap_col, pl.ds(start, half)], near, precision=three_pass)
+        parts.append(jnp.concatenate([inner, outer], axis=0))
+    lane, row = iotas(channels + half, columns)
+    left, middle, right = parts
+    main = (
+        middle
+        + jnp.where(lane == 0, 0.0, pltpu.roll(left, 1, 1))
+        + jnp.where(lane == columns - 1, 0.0, pltpu.roll(right, columns - 1, 1))
+    )
+    slot = lane - lax.rem(row, 4) - 4 * (row // half)
+    edges = jnp.where(slot == 0, left[:, columns - 1 :], 0.0)
+    edges = jnp.where(slot == 12, right[:, 0:1], edges)
+    edges = edges[:half] + edges[half:channels] + edges[channels:]
+    for owner in range(half // 4):
+        first = FORTH * owner
+        for part in range(3):
+            here = half * part + 4 * owner
+            out_ref[first + 8 + 4 * part : first + 12 + 4 * part, :] = main[here : here + 4]
+        out_ref[first + 24 : first + 25, :] = jnp.sum(
+            edges[4 * owner : 4 * owner + 4], axis=0, keepdims=True
         )
-        outer.append(side_part[:, :columns])
-    lane, row = iotas(channels, columns)
-    slot = lane - lax.rem(row, 8)
-    edges = jnp.zeros((channels, columns), jnp.float32)
-    for group, (left, middle, right) in enumerate((inner, outer)):
-        from_left = pltpu.roll(left, 1, 1)
-        from_right = pltpu.roll(right, columns - 1, 1)
-        main = (
-            middle
-            + jnp.where(lane == 0, 0.0, from_left)
-            + jnp.where(lane == columns - 1, 0.0, from_right)
-        )
-        out_ref[:, 8 + 8 * group : 16 + 8 * group, :] = main.reshape(owners, 8, columns)
-        edges = jnp.where(slot == 16 * group, left[:, columns - 1 :], edges)
-        edges = jnp.where(slot == 16 * group + 8, right[:, 0:1], edges)
-    edge_rows = jnp.sum(edges.reshape(owners, 8, columns), axis=1, keepdims=True)
-    out_ref[:, 28:32, :] = jnp.concatenate(
-        [edge_rows, jnp.zeros((owners, 3, columns), jnp.float32)], axis=1
-    )
 
 
 def transform_8(x):
@@ -237,26 +253,31 @@
     columns = in_ref.shape[-1]
     lane, sub = iotas(8, columns)
     me = lax.axis_index("lat") * lon + lax.axis_index("lon")
-    inward = {1: 2, 2: 1}
+    inward = {1: (2, 3), 2: (0, 1)}
+
+    def message(row, place, first, count):
+        start = FORTH * (row * lon + place) + first
+        return in_ref[start : start + count, :]
 
     def edge(row, place, group):
-        picked = jnp.where(lane == sub + 8 * group, in_ref[row * lon + place, 28:29, :], 0.0)
-        if row in inward:
-            also = in_ref[inward[row] * lon + place, 28:29, :]
-            picked = picked + jnp.where(lane == sub + 8 * group + 16, also, 0.0)
-        return jnp.sum(picked, axis=1, keepdims=True)
+        line = jnp.where(lane == sub + 12 * group, message(row, place, 24, 1), 0.0)
+        for part, giver in enumerate(inward.get(row, ())):
+            wanted = jnp.logical_and(lane == lax.rem(sub, 4) + 8 + 12 * group, sub // 4 == part)
+            line = line + jnp.where(wanted, message(giver, place, 24, 1), 0.0)
+        return jnp.sum(line, axis=1, keepdims=True)
 
     grid = []
     for place in range(lon):
         mixed = []
         for row in range(rows):
-            tile = in_ref[row * lon + place, 8:16, :]
+            tile = message(row, place, 8, 8)
             if row in inward:
-                tile = tile + in_ref[inward[row] * lon + place, 16:24, :]
+                pieces = [message(giver, place, 16, 4) for giver in inward[row]]
+                tile = tile + jnp.concatenate(pieces, axis=0)
             tile = tile + jnp.where(lane == 0, edge(row, (place - 1) % lon, 0), 0.0)
             tile = tile + jnp.where(lane == columns - 1, edge(row, (place + 1) % lon, 1), 0.0)
             mixed.append(tile)
-        cot = [in_ref[row * lon + place, 0:8, :] for row in range(rows)]
+        cot = [message(row, place, 0, 8) for row in range(rows)]
         grid.append(jnp.concatenate(mixed + cot, axis=0))
     pairs = transform_8(grid)
     height = 16 * rows
@@ -281,7 +302,7 @@
         part = spectra[residue * height : (residue + 1) * height]
         mix_re, mix_im = part[:half, :columns], part[:half, columns:]
         cot_re, cot_im = part[half:, :columns], part[half:, columns:]
-        quarters = [in_ref[row * lon + place, 24:28, :] * scale for row in range(rows)]
+        quarters = [message(row, place, 20, 4) * scale for row in range(rows)]
         gain_re = jnp.concatenate([jnp.concatenate(quarters[0:2], axis=0)] * rows, axis=0)
         gain_im = jnp.concatenate([jnp.concatenate(quarters[2:4], axis=0)] * rows, axis=0)
         top = pl.ds(residue * height, half)
@@ -321,83 +342,99 @@
         ROOT_HALF * (sums[2] - gaps[2] - sums[0] - gaps[0]),
     ]
     series = [even[d] + swing[d] for d in range(4)] + [even[d] - swing[d] for d in range(4)]
-    base = 8 * lax.rem(me, 16)
-    left_slot = lane == base + sub
-    right_slot = lane == base + lax.rem(sub + 4, 8)
+    slots = [lane == 4 * lax.rem(me + group, 32) + lax.rem(sub, 4) for group in range(6)]
     for place in range(lon):
         residue = reversed_bits(place, 3)
         before, after = series[(place - 1) % lon], series[(place + 1) % lon]
-        tiles, rims = [], []
-        for row in range(rows):
-            span = slice(half + 8 * row, half + 8 * row + 8)
-            tiles.append(series[place][span])
-            rims.append(
-                jnp.where(left_slot, before[span, columns - 1 :], 0.0)
-                + jnp.where(right_slot, after[span, 0:1], 0.0)
-            )
-        for row in range(rows):
-            owner = row * lon + place
-            part, start = row % 2, row // 2
-            out_ref[owner, 0:8, :] = series[place][8 * row : 8 * row + 8]
+        for chip in range(2):
+            rims = jnp.zeros((8, columns), jnp.float32)
             for step in range(3):
-                out_ref[owner, 8 + 4 * step : 12 + 4 * step, :] = tiles[start + step][
-                    4 * part : 4 * part + 4
-                ]
-            out_ref[owner, 20:28, :] = gradients[residue][part]
-            lines = [
-                jnp.sum(rims[start + step][4 * part : 4 * part + 4], axis=0, keepdims=True)
-                for step in range(3)
-            ]
-            lines.append(jnp.zeros((1, columns), jnp.float32))
-            out_ref[owner, 28:32, :] = jnp.concatenate(lines, axis=0)
-
-
-def adjoint_kernel(
-    mine_ref, other_ref, field_ref, cot_ref, taps_ref, out_ref, grad_ref, gain_ref, taps, rows_ref, sem
-):
-    copy = pltpu.make_async_copy(taps_ref, taps, sem)
-    copy.start()
-    channels, columns = field_ref.shape
-    owners = channels // 8
+                span = slice(half + 8 * (chip + step), half + 8 * (chip + step) + 8)
+                rims = jnp.where(slots[2 * step], before[span, columns - 1 :], rims)
+                rims = jnp.where(slots[2 * step + 1], after[span, 0:1], rims)
+            for part in range(2):
+                row = 2 * chip + part
+                start = BACK * (row * lon + place)
+                out_ref[start : start + 8, :] = series[place][8 * row : 8 * row + 8]
+                for step in range(3):
+                    here = half + 8 * (chip + step) + 4 * part
+                    out_ref[start + 8 + 4 * step : start + 12 + 4 * step, :] = series[place][
+                        here : here + 4
+                    ]
+                out_ref[start + 20 : start + 28, :] = gradients[residue][part]
+                out_ref[start + 28 : start + 29, :] = jnp.sum(
+                    rims[4 * part : 4 * part + 4], axis=0, keepdims=True
+                )
+
+
+def partial_adjoint(message_ref, taps_ref, rows_ref, part):
+    half, columns = rows_ref.shape[-1], message_ref.shape[-1]
     place = lax.axis_index("lat")
-    part = lax.rem(place, 2)
     index = place - place // 2
-    out_ref[...] = field_ref[...] + mine_ref[:, 0:8, :].reshape(channels, columns)
-    mine, other = mine_ref[:, 20:28, :], other_ref[:, 20:28, :]
-    gain_ref[0] = jnp.where(part == 0, mine, other).reshape(channels, columns)
-    gain_ref[1] = jnp.where(part == 0, other, mine).reshape(channels, columns)
-    lane, _ = iotas(4, columns)
-    lower = lax.rem(lane // 4, 2) == 0
-    own_slot = lax.rem(lane // 4, 2) == part
-    lefts, rights = [], []
-    for first in (0, owners // 2):
-        mine = jnp.sum(mine_ref[first : first + owners // 2, 28:32, :], axis=0)
-        other = jnp.sum(other_ref[first : first + owners // 2, 28:32, :], axis=0)
-        lefts.append(jnp.where(own_slot, mine, other))
-        swapped = jnp.where(own_slot, other, mine)
-        rights.append(
-            jnp.where(lower, pltpu.roll(swapped, columns - 4, 1), pltpu.roll(swapped, 4, 1))
-        )
-    left = jnp.concatenate(lefts, axis=1)
-    right = jnp.concatenate(rights, axis=1)
+    owners = half // 4
+    lines = message_ref[pl.ds(28, owners, stride=BACK), :]
+    lane, owner = iotas(owners, columns)
     rows_ref[0] = jnp.zeros(rows_ref.shape[1:], jnp.float32)
     rows_ref[4] = jnp.zeros(rows_ref.shape[1:], jnp.float32)
     for step in range(3):
-        span = slice(8 + 4 * step, 12 + 4 * step)
-        mine, other = mine_ref[:, span, :], other_ref[:, span, :]
-        tile = jnp.concatenate(
-            [jnp.where(part == 0, mine, other), jnp.where(part == 0, other, mine)], axis=1
-        )
-        rows_ref[1 + step, 8 : 8 + columns, :] = tile.reshape(channels, columns).T
-        rows_ref[1 + step, 7:8, :] = left[step : step + 1]
-        rows_ref[1 + step, 8 + columns : 9 + columns, :] = right[step : step + 1]
-    copy.wait()
-    total = jnp.zeros((columns, channels), jnp.float32)
+        pieces = [
+            message_ref[BACK * j + 8 + 4 * step : BACK * j + 12 + 4 * step, :] for j in range(owners)
+        ]
+        rows_ref[1 + step, 8 : 8 + columns, :] = jnp.concatenate(pieces, axis=0).T
+        for rim, target in ((2 * step, 7), (2 * step + 1, 8 + columns)):
+            wanted = lane // 4 == lax.rem(owner + rim, owners)
+            line = jnp.sum(jnp.where(wanted, lines, 0.0), axis=0, keepdims=True)
+            line = jnp.broadcast_to(line, (8, columns))
+            if rim:
+                line = pltpu.roll(line, columns - 4 * rim, 1)
+            rows_ref[1 + step, target : target + 1, :] = line[0:1]
+    span = pl.ds(pl.multiple_of(part * half, half), half)
+    windows, weights = [], []
     for tap_row in range(3):
         for tap_col in range(3):
-            window = rows_ref[index + 2 - tap_row, 9 - tap_col : 9 - tap_col + columns, :]
-            total = total + jnp.dot(window, taps[tap_row, tap_col], precision=three_pass)
+            first = 9 - tap_col
+            windows.append(rows_ref[index + 2 - tap_row, first : first + columns, :])
+            weights.append(taps_ref[tap_row, tap_col, span])
+    total = jnp.dot(windows[8], weights[8], precision=three_pass)
+    for pair in range(0, 8, 2):
+        total = total + jnp.dot(
+            jnp.concatenate(windows[pair : pair + 2], axis=1),
+            jnp.concatenate(weights[pair : pair + 2], axis=0),
+            precision=three_pass,
+        )
+    return total
+
+
+def adjoint_kernel(mine_ref, field_ref, taps_ref, out_ref, total_ref, rows_ref):
+    half = field_ref.shape[0] // 2
+    for owner in range(half // 4):
+        for part in range(2):
+            here, there = half * part + 4 * owner, BACK * owner + 4 * part
+            out_ref[here : here + 4, :] = field_ref[here : here + 4, :] + mine_ref[there : there + 4, :]
+    part = lax.rem(lax.axis_index("lat"), 2)
+    total_ref[...] = partial_adjoint(mine_ref, taps_ref, rows_ref, part)
+
+
+def last_kernel(
+    mine_ref, other_ref, cot_ref, taps_ref, total_ref, grad_ref, gain_ref, rows_ref, gain, sems
+):
+    half = cot_ref.shape[0] // 2
+    part = lax.rem(lax.axis_index("lat"), 2)
+    for owner in range(half // 4):
+        for piece in range(2):
+            here, there = half * piece + 4 * owner, BACK * owner + 20 + 4 * piece
+            gain[0, here : here + 4, :] = mine_ref[there : there + 4, :]
+            gain[1, here : here + 4, :] = other_ref[there : there + 4, :]
+    copies = [
+        pltpu.make_async_copy(gain.at[0], gain_ref.at[part], sems.at[0]),
+        pltpu.make_async_copy(gain.at[1], gain_ref.at[1 - part], sems.at[1]),
+    ]
+    for copy in copies:
+        copy.start()
+    total = total_ref[...] + partial_adjoint(other_ref, taps_ref, rows_ref, 1 - part)
     grad_ref[...] = cot_ref[...] + total.T
+    for copy in copies:
+        copy.wait()
 
 
 def transform_tables(columns, lon):
@@ -410,6 +447,12 @@
     return jnp.asarray(turns, jnp.float32), jnp.asarray(dft, jnp.float32)
 
 
+def exchanged(flat):
+    rows, columns = flat.shape
+    moved = lax.all_to_all(flat.reshape(rows, 1, columns), ("lat", "lon"), 0, 0, tiled=True)
+    return moved.reshape(rows, columns)
+
+
 def on_device(field, cotangent, conv_weight, spectral_filter):
     channels, _, columns = field.shape
     lat, lon = lax.axis_size("lat"), lax.axis_size("lon")
@@ -418,48 +461,70 @@
     own = field.reshape(channels, columns)
     cot = cotangent.reshape(channels, columns)
     vmem = pl.BlockSpec(memory_space=pltpu.VMEM)
-    hbm = pl.BlockSpec(memory_space=pl.ANY)
-    params = pltpu.CompilerParams(vmem_limit_bytes=24 * 1024 * 1024)
-    message = jax.ShapeDtypeStruct((owners, 32, columns), jnp.float32)
+    hbm = pl.BlockSpec(memory_space=pltpu.HBM)
+    params = pltpu.CompilerParams(vmem_limit_bytes=16 * 1024 * 1024)
+    flat = jax.ShapeDtypeStruct((channels, columns), jnp.float32)
+    taps_shape = jax.ShapeDtypeStruct(conv_weight.shape, jnp.float32)
+    forth = jax.ShapeDtypeStruct((owners * FORTH, columns), jnp.float32)
+    back = jax.ShapeDtypeStruct((owners * BACK, columns), jnp.float32)
+    other = lax.ppermute(own, "lat", swap)
+    own_here, taps, packed = pl.pallas_call(
+        fetch_kernel,
+        out_shape=(flat, taps_shape, forth),
+        in_specs=[hbm] * 4,
+        out_specs=(vmem, vmem, vmem),
+        scratch_shapes=[
+            pltpu.VMEM((channels, columns), jnp.float32),
+            pltpu.VMEM((channels // 2, columns), jnp.float32),
+            pltpu.SemaphoreType.DMA((4,)),
+        ],
+        compiler_params=params,
+        name="fetch",
+    )(*[pltpu.with_memory_space_constraint(x, pltpu.HBM) for x in (own, cot, spectral_filter, conv_weight)])
     outgoing = pl.pallas_call(
         conv_kernel,
-        out_shape=message,
-        in_specs=[vmem, vmem, vmem, vmem, hbm],
+        out_shape=forth,
+        in_specs=[vmem] * 4,
         out_specs=vmem,
-        scratch_shapes=[
-            pltpu.VMEM((2,) + conv_weight.shape[1:], jnp.float32),
-            pltpu.SemaphoreType.DMA((2,)),
-        ],
+        input_output_aliases={3: 0},
         compiler_params=params,
         name="conv",
-    )(own, lax.ppermute(own, "lat", swap), cot, spectral_filter, conv_weight)
-    owned = lax.all_to_all(outgoing, ("lat", "lon"), 0, 0, tiled=True)
+    )(own_here, other, taps, packed)
     turns, dft = transform_tables(columns, lon)
     returned = pl.pallas_call(
         spectral_kernel,
-        out_shape=message,
+        out_shape=back,
         in_specs=[vmem] * 3,
         out_specs=vmem,
         scratch_shapes=[pltpu.VMEM((2 * 8 * lat * lon, 2 * columns), jnp.float32)],
         compiler_params=params,
         name="spectral",
-    )(owned, turns, dft)
-    mine = lax.all_to_all(returned, ("lat", "lon"), 0, 0, tiled=True)
+    )(exchanged(outgoing), turns, dft)
+    mine = exchanged(returned)
     other = lax.ppermute(mine, "lat", swap)
-    flat = jax.ShapeDtypeStruct((channels, columns), jnp.float32)
-    output, input_grad, filter_grad = pl.pallas_call(
+    rows_scratch = pltpu.VMEM((5, columns + 16, channels // 2), jnp.float32)
+    output, total = pl.pallas_call(
         adjoint_kernel,
-        out_shape=(flat, flat, jax.ShapeDtypeStruct(spectral_filter.shape, jnp.float32)),
-        in_specs=[vmem, vmem, vmem, vmem, hbm],
-        out_specs=(vmem, vmem, vmem),
+        out_shape=(flat, jax.ShapeDtypeStruct((columns, channels), jnp.float32)),
+        in_specs=[vmem] * 3,
+        out_specs=(vmem, vmem),
+        scratch_shapes=[rows_scratch],
+        compiler_params=params,
+        name="adjoint",
+    )(mine, own, taps)
+    input_grad, filter_grad = pl.pallas_call(
+        last_kernel,
+        out_shape=(flat, jax.ShapeDtypeStruct(spectral_filter.shape, jnp.float32)),
+        in_specs=[vmem] * 5,
+        out_specs=(vmem, hbm),
         scratch_shapes=[
-            pltpu.VMEM(conv_weight.shape, jnp.float32),
-            pltpu.VMEM((5, columns + 16, channels), jnp.float32),
-            pltpu.SemaphoreType.DMA,
+            rows_scratch,
+            pltpu.VMEM(spectral_filter.shape, jnp.float32),
+            pltpu.SemaphoreType.DMA((2,)),
         ],
         compiler_params=params,
-        name="adjoint",
-    )(mine, other, own, cot, conv_weight)
+        name="last",
+    )(mine, other, cot, taps, total)
     return (output.reshape(field.shape), input_grad.reshape(field.shape), filter_grad)
 
 

time: 55.2 us -> 47.5 us (0.86)
  local copies, waits for them, and re-layouts: 4.45 us -> 0.02 us
  blocking collectives: 41.8 us -> 38 us
  Pallas kernels: 4.36 us -> 7.49 us
  waiting for transfers between devices: 3.1 us -> 0.6 us
    unnamed x18 -> x8, local copies, waits for them, and re-layouts: 4.45 us -> 0.02 us
    all_to_all x2, blocking collectives: 41.8 us -> 38 us  [exchanged(): lax.all_to_all(flat.reshape(rows, 1, columns), ('lat', 'lon'), 0, 0, tile...]
    pallas_call x3 -> x5, Pallas kernels: 4.36 us -> 7.49 us  [the longest x1 2.02 us: on_device(): pl.pallas_call(last_kernel, out_shape=(flat, jax.ShapeDtypeStruct(spectra...]
    ppermute x1, waiting for transfers between devices: 1.91 us -> 0.6 us  [on_device(): other = lax.ppermute(mine, 'lat', swap)]
    ppermute x1, waiting for transfers between devices: 1.2 us -> 0.01 us  [on_device(): other = lax.ppermute(own, 'lat', swap)]
  transfers between devices with their start and end apart: 2 -> 2, of which waited for: 2 -> 1; matrix products, arithmetic and copies ran while one was open for 0% -> 0% of each run, Pallas kernels for 0% -> 7%
where the time goes in v2:
time: 47.5 us; the launch traced here: 47.4 us
  blocking collectives  38 us (80%)
  Pallas kernels  7.49 us (16%)
  between operations  0.69 us (1%)
  waiting for transfers between devices  0.6 us (1%)
  starting transfers between devices  0.52 us (1%)
    all_to_all x2, blocking collectives, exchanged(): lax.all_to_all(flat.reshape(rows, 1, columns), ('lat', 'lon'), 0, 0, tile...  38 us
    pallas_call x1, Pallas kernels, on_device(): pl.pallas_call(last_kernel, out_shape=(flat, jax.ShapeDtypeStruct(spectra...  2.02 us
    pallas_call x1, Pallas kernels, on_device(): pl.pallas_call(fetch_kernel, out_shape=(flat, taps_shape, forth), in_spec...  1.88 us
    pallas_call x1, Pallas kernels, on_device(): pl.pallas_call(spectral_kernel, out_shape=back, in_specs=[vmem] * 3, out_...  1.26 us
    pallas_call x1, Pallas kernels, on_device(): pl.pallas_call(adjoint_kernel, out_shape=(flat, jax.ShapeDtypeStruct((col...  1.24 us
    pallas_call x1, Pallas kernels, on_device(): pl.pallas_call(conv_kernel, out_shape=forth, in_specs=[vmem] * 4, out_spe...  1.08 us
  transfers between devices with their start and end apart: 2, of which 1 were waited for; matrix products, arithmetic and copies ran while one was open for 0% of the time, Pallas kernels for 7%

profile of v2, /device:TPU:0, one launch (start us, length us, event | category | flops | bytes accessed | tf_op | source)
XLA Modules:
  0.0 47.4 jit_solution(4615190144408172124)
XLA Ops:
  0.6 0.5 %collective-permute-start = (f32[256,128]{1,0:T(8,128)}, f32[256,128]{1,0:T(8,128)S(1)}, u32[]{:S(2)}, u32[]{:S(2)}) collective-permute-start(f32[256,128]{1,0:T(8,128)} %bitcast.24), channel_id=1, source_target_pairs={{0,8},{8,0},{16,24},{24,16},{1,9},{9,1},{17,25},{25,17},{2,10},{10... | collective-permute-start | bytes 393224 | tf_op jit(solution)/shard_map/ppermute | solution.py:470
  1.1 1.9 %fetch.1 = (f32[256,128]{1,0:T(8,128)S(1)}, f32[3,3,256,256]{3,2,1,0:T(8,128)S(1)}, f32[800,128]{1,0:T(8,128)S(1)}) custom-call(f32[256,128]{1,0:T(8,128)} %bitcast.25, f32[256,128]{1,0:T(8,128)} %bitcast.22, f32[2,256,128]{2,1,0:T(8,128)} %filter_ref.1, f32[3,3,256,256]{3,2,1,0:T(8,128)} %taps_ref.1), custom_call_target="tpu_custom_call" | custom-call | tf_op jit(solution)/shard_map/fetch/pallas_call | solution.py:471
  3.0 0.0 copy-start.2
  3.1 0.0 copy-start.3
  3.1 0.0 collective-permute-done.other_ref
  3.1 0.0 copy-start.1
  3.1 1.1 %conv.1 = f32[800,128]{1,0:T(8,128)S(1)} custom-call(f32[256,128]{1,0:T(8,128)S(1)} %get-tuple-element.10.own_ref, f32[256,128]{1,0:T(8,128)S(1)} %collective-permute-done.other_ref, f32[3,3,256,256]{3,2,1,0:T(8,128)S(1)} %get-tuple-element.11.taps_ref, f32[800,128]{1,0:T(8,128)S(1)} %get-tuple-element.12.packed_ref), custom_call_target="tpu_custom_call", output_to_operand_aliasing={{}: (3, {})} | custom-call | tf_op jit(solution)/shard_map/conv/pallas_call | solution.py:484
  4.2 20.7 %all_to_all.10 = f32[800,1,128]{2,1,0:T(1,128)S(1)} all-to-all(f32[800,1,128]{2,1,0:T(1,128)S(1)} %bitcast.21), channel_id=1, replica_groups=mesh['lat'=4,'lon'=8] {'lat','lon'}, dimensions={0} | all-to-all | bytes 819200 | tf_op jit(solution)/shard_map/all_to_all | solution.py:452
  24.8 0.0 copy-done.2
  24.8 0.0 copy-done.3
  24.8 0.0 copy-start
  24.8 1.3 %spectral.1 = f32[928,128]{1,0:T(8,128)S(1)} custom-call(f32[800,128]{1,0:T(8,128)S(1)} %bitcast.20, f32[16,128]{1,0:T(8,128)S(1)} %copy-done.3, f32[256,256]{1,0:T(8,128)S(1)} %copy-done.2), custom_call_target="tpu_custom_call" | custom-call | tf_op jit(solution)/shard_map/spectral/pallas_call | solution.py:494
  26.1 17.4 %all_to_all.11 = f32[928,1,128]{2,1,0:T(1,128)S(1)} all-to-all(f32[928,1,128]{2,1,0:T(1,128)S(1)} %bitcast.19), channel_id=1, replica_groups=mesh['lat'=4,'lon'=8] {'lat','lon'}, dimensions={0} | all-to-all | bytes 950272 | tf_op jit(solution)/shard_map/all_to_all | solution.py:452
  43.5 0.0 collective-permute-start.1
  43.5 0.0 copy-done.1
  43.5 1.2 %adjoint.1 = (f32[256,128]{1,0:T(8,128)}, f32[128,256]{1,0:T(8,128)S(1)}) custom-call(f32[928,128]{1,0:T(8,128)S(1)} %bitcast.17, f32[256,128]{1,0:T(8,128)S(1)} %bitcast.26, f32[3,3,256,256]{3,2,1,0:T(8,128)S(1)} %get-tuple-element.11.taps_ref), custom_call_target="tpu_custom_call" | custom-call | tf_op jit(solution)/shard_map/adjoint/pallas_call | solution.py:506
  44.7 0.6 %collective-permute-done.1.other_ref = f32[928,128]{1,0:T(8,128)S(1)} collective-permute-done((f32[928,128]{1,0:T(8,128)S(1)}, f32[928,128]{1,0:T(8,128)S(1)}, u32[]{:S(2)}, u32[]{:S(2)}) %collective-permute-start.1) | collective-permute-done | bytes 475168 | tf_op jit(solution)/shard_map/ppermute | solution.py:504
  45.3 0.0 copy-done
  45.3 2.0 %last.1 = (f32[256,128]{1,0:T(8,128)}, f32[2,256,128]{2,1,0:T(8,128)}) custom-call(f32[928,128]{1,0:T(8,128)S(1)} %bitcast.18, f32[928,128]{1,0:T(8,128)S(1)} %collective-permute-done.1.other_ref, f32[256,128]{1,0:T(8,128)S(1)} %bitcast.23, f32[3,3,256,256]{3,2,1,0:T(8,128)S(1)} %get-tuple-element.11.taps_ref, f32[128,256]{1,0:T(8,128)S(1)} %get-tuple-element.14.total_ref), custom_call_target="tpu_custom_call" | custom-call | tf_op jit(solution)/shard_map/last/pallas_call | solution.py:515
Async XLA Ops:
  0.6 2.4 %collective-permute-start = (f32[256,128]{1,0:T(8,128)}, f32[256,128]{1,0:T(8,128)S(1)}, u32[]{:S(2)}, u32[]{:S(2)}) collective-permute-start(f32[256,128]{1,0:T(8,128)} %bitcast.24), channel_id=1, source_target_pairs={{0,8},{8,0},{16,24},{24,16},{1,9},{9,1},{17,25},{25,17},{2,10},{10... | collective-permute-start | bytes 393224 | tf_op jit(solution)/shard_map/ppermute | solution.py:470
  3.0 21.8 %copy-start.2 = (f32[256,256]{1,0:T(8,128)S(1)}, f32[256,256]{1,0:T(8,128)}, u32[]{:S(2)}) copy-start(f32[256,256]{1,0:T(8,128)} %constant.5.clone.dft_ref) | copy-start | bytes 786436
  3.1 21.8 %copy-start.3 = (f32[16,128]{1,0:T(8,128)S(1)}, f32[16,128]{1,0:T(8,128)}, u32[]{:S(2)}) copy-start(f32[16,128]{1,0:T(8,128)} %constant.4.clone.turn_ref) | copy-start | bytes 24580
  3.1 40.4 %copy-start.1 = (f32[256,1,128]{2,1,0:T(1,128)S(1)}, f32[256,1,128]{2,1,0:T(1,128)}, u32[]{:S(2)}) copy-start(f32[256,1,128]{2,1,0:T(1,128)} %param.6) | copy-start | bytes 393220
  24.8 20.5 %copy-start = (f32[256,1,128]{2,1,0:T(1,128)S(1)}, f32[256,1,128]{2,1,0:T(1,128)}, u32[]{:S(2)}) copy-start(f32[256,1,128]{2,1,0:T(1,128)} %param.7) | copy-start | bytes 393220
  43.5 1.8 %collective-permute-start.1 = (f32[928,128]{1,0:T(8,128)S(1)}, f32[928,128]{1,0:T(8,128)S(1)}, u32[]{:S(2)}, u32[]{:S(2)}) collective-permute-start(f32[928,128]{1,0:T(8,128)S(1)} %bitcast.16), channel_id=1, source_target_pairs={{0,8},{8,0},{16,24},{24,16},{1,9},{9,1},{17,25},{25,17},{2,10},{10... | collective-permute-start | bytes 1425416 | tf_op jit(solution)/shard_map/ppermute | solution.py:504

commit v3 on v2

--- a/solution.py
+++ b/solution.py
@@ -176,16 +176,23 @@
     return lane, row
 
 
-def fetch_kernel(own_ref, cot_ref, filter_ref, taps_ref, own_out, taps_out, out_ref, cot, gain, sems):
+def fetch_kernel(
+    own_ref, cot_ref, filter_ref, taps_ref, own_out, middle, side, cross, out_ref, cot, gain, sems
+):
     place = lax.axis_index("lat")
-    half = gain.shape[0]
-    start = pl.multiple_of(lax.rem(place, 2) * half, half)
+    odd, half = lax.rem(place, 2), gain.shape[0]
+    span = pl.ds(pl.multiple_of(odd * half, half), half)
+    cross_row = 2 * (place // 2)
     copies = [
         pltpu.make_async_copy(cot_ref, cot, sems.at[0]),
-        pltpu.make_async_copy(filter_ref.at[place // 2, pl.ds(start, half)], gain, sems.at[1]),
+        pltpu.make_async_copy(filter_ref.at[place // 2, span], gain, sems.at[1]),
         pltpu.make_async_copy(own_ref, own_out, sems.at[2]),
-        pltpu.make_async_copy(taps_ref, taps_out, sems.at[3]),
+        pltpu.make_async_copy(taps_ref.at[1], middle, sems.at[3]),
+        pltpu.make_async_copy(taps_ref.at[2 - 2 * odd], side, sems.at[4]),
     ]
+    for tap_col in range(3):
+        piece = taps_ref.at[cross_row, tap_col, span]
+        copies.append(pltpu.make_async_copy(piece, cross.at[tap_col], sems.at[5 + tap_col]))
     for copy in copies:
         copy.start()
     copies[0].wait()
@@ -195,24 +202,47 @@
         out_ref[first : first + 4, :] = cot[here]
         out_ref[first + 4 : first + 8, :] = cot[half + 4 * owner : half + 4 * owner + 4]
         out_ref[first + 20 : first + 24, :] = gain[here]
-    copies[2].wait()
-    copies[3].wait()
-
-
-def conv_kernel(own_ref, other_ref, taps_ref, packed_ref, out_ref):
+    for copy in copies[2:]:
+        copy.wait()
+
+
+def high_low(x):
+    high = x.astype(jnp.bfloat16)
+    return high, (x - high.astype(jnp.float32)).astype(jnp.bfloat16)
+
+
+def both_parts(x):
+    return jnp.concatenate(high_low(x), axis=1)
+
+
+def product(weights, parts):
+    columns = parts.shape[1] // 2
+    high, low = high_low(weights)
+    wide = jnp.dot(high, parts, preferred_element_type=jnp.float32)
+    rest = jnp.dot(low, parts[:, :columns], preferred_element_type=jnp.float32)
+    return wide[:, :columns] + (wide[:, columns:] + rest)
+
+
+def tall_product(x, high, low):
+    rows = x.shape[0]
+    x_high, x_low = high_low(x)
+    both = jnp.concatenate([x_high, x_low], axis=0)
+    both = jnp.dot(both, high, preferred_element_type=jnp.float32)
+    rest = jnp.dot(x_high, low, preferred_element_type=jnp.float32)
+    return both[:rows] + (both[rows:] + rest)
+
+
+def conv_kernel(own_ref, other_ref, middle_ref, side_ref, cross_ref, packed_ref, out_ref):
     place = lax.axis_index("lat")
-    odd = lax.rem(place, 2)
     channels, columns = own_ref.shape
     half = channels // 2
-    side, cross = 2 - 2 * odd, 2 * (place // 2)
-    start = pl.multiple_of(odd * half, half)
     own, other = own_ref[...], other_ref[...]
     near = jnp.where(jnp.logical_or(place == 1, place == 2), own, other)
+    own, other, near = both_parts(own), both_parts(other), both_parts(near)
     parts = []
     for tap_col in range(3):
-        inner = jnp.dot(taps_ref[1, tap_col], own, precision=three_pass)
-        inner = inner + jnp.dot(taps_ref[side, tap_col], other, precision=three_pass)
-        outer = jnp.dot(taps_ref[cross, tap_col, pl.ds(start, half)], near, precision=three_pass)
+        inner = product(middle_ref[tap_col], own) + product(side_ref[tap_col], other)
+        outer = product(cross_ref[tap_col], near)
         parts.append(jnp.concatenate([inner, outer], axis=0))
     lane, row = iotas(channels + half, columns)
     left, middle, right = parts
@@ -293,7 +323,12 @@
         span = pl.ds(residue * height, height)
         work[span, 0:columns] = turned[0]
         work[span, columns:] = turned[1]
-    spectra = jnp.dot(work[...], dft_ref[...], precision=three_pass)
+    chunk = lon * height // 4
+    pieces = [pl.ds(first, chunk) for first in range(0, lon * height, chunk)]
+    table = high_low(dft_ref[...])
+    spectra = jnp.concatenate(
+        [tall_product(work[piece], *table) for piece in pieces], axis=0
+    )
     scale = 1.0 / (lon * columns)
     half = 8 * rows
     gradients = []
@@ -319,7 +354,9 @@
                 for grad in (grad_re, grad_im)
             ]
         )
-    back = jnp.dot(work[...], dft_ref[...], precision=three_pass)
+    back = jnp.concatenate(
+        [tall_product(work[piece], *table) for piece in pieces], axis=0
+    )
     turned = []
     for residue in range(lon):
         part = back[residue * height : (residue + 1) * height]
@@ -395,13 +432,11 @@
             first = 9 - tap_col
             windows.append(rows_ref[index + 2 - tap_row, first : first + columns, :])
             weights.append(taps_ref[tap_row, tap_col, span])
-    total = jnp.dot(windows[8], weights[8], precision=three_pass)
-    for pair in range(0, 8, 2):
-        total = total + jnp.dot(
-            jnp.concatenate(windows[pair : pair + 2], axis=1),
-            jnp.concatenate(weights[pair : pair + 2], axis=0),
-            precision=three_pass,
-        )
+    total = 0.0
+    for pair in range(0, 9, 2):
+        window = jnp.concatenate(windows[pair : pair + 2], axis=1)
+        weight = jnp.concatenate(weights[pair : pair + 2], axis=0)
+        total = total + tall_product(window, *high_low(weight))
     return total
 
 
@@ -415,26 +450,16 @@
     total_ref[...] = partial_adjoint(mine_ref, taps_ref, rows_ref, part)
 
 
-def last_kernel(
-    mine_ref, other_ref, cot_ref, taps_ref, total_ref, grad_ref, gain_ref, rows_ref, gain, sems
-):
+def last_kernel(mine_ref, other_ref, cot_ref, taps_ref, total_ref, grad_ref, gain_ref, rows_ref):
     half = cot_ref.shape[0] // 2
     part = lax.rem(lax.axis_index("lat"), 2)
     for owner in range(half // 4):
         for piece in range(2):
             here, there = half * piece + 4 * owner, BACK * owner + 20 + 4 * piece
-            gain[0, here : here + 4, :] = mine_ref[there : there + 4, :]
-            gain[1, here : here + 4, :] = other_ref[there : there + 4, :]
-    copies = [
-        pltpu.make_async_copy(gain.at[0], gain_ref.at[part], sems.at[0]),
-        pltpu.make_async_copy(gain.at[1], gain_ref.at[1 - part], sems.at[1]),
-    ]
-    for copy in copies:
-        copy.start()
+            gain_ref[part, here : here + 4, :] = mine_ref[there : there + 4, :]
+            gain_ref[1 - part, here : here + 4, :] = other_ref[there : there + 4, :]
     total = total_ref[...] + partial_adjoint(other_ref, taps_ref, rows_ref, 1 - part)
     grad_ref[...] = cot_ref[...] + total.T
-    for copy in copies:
-        copy.wait()
 
 
 def transform_tables(columns, lon):
@@ -464,19 +489,20 @@
     hbm = pl.BlockSpec(memory_space=pltpu.HBM)
     params = pltpu.CompilerParams(vmem_limit_bytes=16 * 1024 * 1024)
     flat = jax.ShapeDtypeStruct((channels, columns), jnp.float32)
-    taps_shape = jax.ShapeDtypeStruct(conv_weight.shape, jnp.float32)
     forth = jax.ShapeDtypeStruct((owners * FORTH, columns), jnp.float32)
     back = jax.ShapeDtypeStruct((owners * BACK, columns), jnp.float32)
     other = lax.ppermute(own, "lat", swap)
-    own_here, taps, packed = pl.pallas_call(
+    row_shape = jax.ShapeDtypeStruct(conv_weight.shape[1:], jnp.float32)
+    half_shape = jax.ShapeDtypeStruct((3, channels // 2, channels), jnp.float32)
+    *fetched, packed = pl.pallas_call(
         fetch_kernel,
-        out_shape=(flat, taps_shape, forth),
+        out_shape=(flat, row_shape, row_shape, half_shape, forth),
         in_specs=[hbm] * 4,
-        out_specs=(vmem, vmem, vmem),
+        out_specs=(vmem,) * 5,
         scratch_shapes=[
             pltpu.VMEM((channels, columns), jnp.float32),
             pltpu.VMEM((channels // 2, columns), jnp.float32),
-            pltpu.SemaphoreType.DMA((4,)),
+            pltpu.SemaphoreType.DMA((8,)),
         ],
         compiler_params=params,
         name="fetch",
@@ -484,12 +510,12 @@
     outgoing = pl.pallas_call(
         conv_kernel,
         out_shape=forth,
-        in_specs=[vmem] * 4,
+        in_specs=[vmem] * 6,
         out_specs=vmem,
-        input_output_aliases={3: 0},
+        input_output_aliases={5: 0},
         compiler_params=params,
         name="conv",
-    )(own_here, other, taps, packed)
+    )(fetched[0], other, *fetched[1:], packed)
     turns, dft = transform_tables(columns, lon)
     returned = pl.pallas_call(
         spectral_kernel,
@@ -511,20 +537,16 @@
         scratch_shapes=[rows_scratch],
         compiler_params=params,
         name="adjoint",
-    )(mine, own, taps)
+    )(mine, own, conv_weight)
     input_grad, filter_grad = pl.pallas_call(
         last_kernel,
         out_shape=(flat, jax.ShapeDtypeStruct(spectral_filter.shape, jnp.float32)),
         in_specs=[vmem] * 5,
-        out_specs=(vmem, hbm),
-        scratch_shapes=[
-            rows_scratch,
-            pltpu.VMEM(spectral_filter.shape, jnp.float32),
-            pltpu.SemaphoreType.DMA((2,)),
-        ],
+        out_specs=(vmem, vmem),
+        scratch_shapes=[rows_scratch],
         compiler_params=params,
         name="last",
-    )(mine, other, cot, taps, total)
+    )(mine, other, cot, conv_weight, total)
     return (output.reshape(field.shape), input_grad.reshape(field.shape), filter_grad)
 
 

time: 47.5 us -> 46.1 us (0.971)
  Pallas kernels: 7.49 us -> 5.97 us
    pallas_call x1, Pallas kernels: 2.02 us -> 1.35 us  [on_device(): pl.pallas_call(last_kernel, out_shape=(flat, jax.ShapeDtypeStruct(spectra...]
    pallas_call x2, Pallas kernels: 2.96 us -> 2.46 us  [the longest x1 1.69 us: on_device(): pl.pallas_call(fetch_kernel, out_shape=(flat, row_shape, row_shape, half_...]
  transfers between devices with their start and end apart: 2 -> 2, of which waited for: 1 -> 1; matrix products, arithmetic and copies ran while one was open for 0% -> 0% of each run, Pallas kernels for 7% -> 6%
where the time goes in v3:
time: 46.1 us; the launch traced here: 45.9 us
  blocking collectives  38 us (82%)
  Pallas kernels  5.97 us (13%)
  between operations  0.7 us (2%)
  waiting for transfers between devices  0.63 us (1%)
  starting transfers between devices  0.52 us (1%)
    all_to_all x2, blocking collectives, exchanged(): lax.all_to_all(flat.reshape(rows, 1, columns), ('lat', 'lon'), 0, 0, tile...  38 us
    pallas_call x1, Pallas kernels, on_device(): pl.pallas_call(fetch_kernel, out_shape=(flat, row_shape, row_shape, half_...  1.69 us
    pallas_call x1, Pallas kernels, on_device(): pl.pallas_call(last_kernel, out_shape=(flat, jax.ShapeDtypeStruct(spectra...  1.35 us
    pallas_call x1, Pallas kernels, on_device(): pl.pallas_call(adjoint_kernel, out_shape=(flat, jax.ShapeDtypeStruct((col...  1.2 us
    pallas_call x1, Pallas kernels, on_device(): pl.pallas_call(spectral_kernel, out_shape=back, in_specs=[vmem] * 3, out_...  0.96 us
  transfers between devices with their start and end apart: 2, of which 1 were waited for; matrix products, arithmetic and copies ran while one was open for 0% of the time, Pallas kernels for 6%

profile of v3, /device:TPU:0, one launch (start us, length us, event | category | flops | bytes accessed | tf_op | source)
XLA Modules:
  0.0 45.9 jit_solution(7178295695946999450)
XLA Ops:
  0.6 0.5 %collective-permute-start = (f32[256,128]{1,0:T(8,128)}, f32[256,128]{1,0:T(8,128)S(1)}, u32[]{:S(2)}, u32[]{:S(2)}) collective-permute-start(f32[256,128]{1,0:T(8,128)} %bitcast.24), channel_id=1, source_target_pairs={{0,8},{8,0},{16,24},{24,16},{1,9},{9,1},{17,25},{25,17},{2,10},{10... | collective-permute-start | bytes 393224 | tf_op jit(solution)/shard_map/ppermute | solution.py:494
  1.1 1.7 %fetch.1 = (f32[256,128]{1,0:T(8,128)S(1)}, f32[3,256,256]{2,1,0:T(8,128)S(1)}, f32[3,256,256]{2,1,0:T(8,128)S(1)}, f32[3,128,256]{2,1,0:T(8,128)S(1)}, f32[800,128]{1,0:T(8,128)S(1)}) custom-call(f32[256,128]{1,0:T(8,128)} %bitcast.25, f32[256,128]{1,0:T(8,128)} %bitcast.22, f32[2,256,128]{2,1,0:T(8,128)} %filter_ref.1, f32[3,3,256,256]{3,2,1,0:T(8,128)} %taps_ref.5), custom_call_target="tpu_custom_call" | custom-call | tf_op jit(solution)/shard_map/fetch/pallas_call | solution.py:497
  2.8 0.0 copy-start.3
  2.9 0.0 copy-start.4
  2.9 0.0 collective-permute-done.other_ref
  2.9 0.0 copy-start
  2.9 0.0 copy-start.2
  2.9 0.8 %conv.1 = f32[800,128]{1,0:T(8,128)S(1)} custom-call(f32[256,128]{1,0:T(8,128)S(1)} %get-tuple-element.12.own_ref, f32[256,128]{1,0:T(8,128)S(1)} %collective-permute-done.other_ref, f32[3,256,256]{2,1,0:T(8,128)S(1)} %get-tuple-element.13.middle_ref, f32[3,256,256]{2,1,0:T(8,128)S(1)} %get-tuple-element.14.side_ref, ...), custom_call_target="tpu_custom_call", output_to_operand_aliasing={{}: (5, {})} | custom-call | tf_op jit(solution)/shard_map/conv/pallas_call | solution.py:510
  3.7 20.7 %all_to_all.10 = f32[800,1,128]{2,1,0:T(1,128)S(1)} all-to-all(f32[800,1,128]{2,1,0:T(1,128)S(1)} %bitcast.21), channel_id=1, replica_groups=mesh['lat'=4,'lon'=8] {'lat','lon'}, dimensions={0} | all-to-all | bytes 819200 | tf_op jit(solution)/shard_map/all_to_all | solution.py:477
  24.3 0.0 copy-done.3
  24.4 0.0 copy-done.4
  24.4 0.0 copy-start.1
  24.4 1.0 %spectral.1 = f32[928,128]{1,0:T(8,128)S(1)} custom-call(f32[800,128]{1,0:T(8,128)S(1)} %bitcast.20, f32[16,128]{1,0:T(8,128)S(1)} %copy-done.4, f32[256,256]{1,0:T(8,128)S(1)} %copy-done.3), custom_call_target="tpu_custom_call" | custom-call | tf_op jit(solution)/shard_map/spectral/pallas_call | solution.py:520
  25.3 17.4 %all_to_all.11 = f32[928,1,128]{2,1,0:T(1,128)S(1)} all-to-all(f32[928,1,128]{2,1,0:T(1,128)S(1)} %bitcast.19), channel_id=1, replica_groups=mesh['lat'=4,'lon'=8] {'lat','lon'}, dimensions={0} | all-to-all | bytes 950272 | tf_op jit(solution)/shard_map/all_to_all | solution.py:477
  42.7 0.0 collective-permute-start.1
  42.7 0.0 copy-done
  42.7 0.0 copy-done.2
  42.7 1.2 %adjoint.1 = (f32[256,128]{1,0:T(8,128)}, f32[128,256]{1,0:T(8,128)S(1)}) custom-call(f32[928,128]{1,0:T(8,128)S(1)} %bitcast.17, f32[256,128]{1,0:T(8,128)S(1)} %bitcast.26, f32[3,3,256,256]{3,2,1,0:T(8,128)S(1)} %copy-done), custom_call_target="tpu_custom_call" | custom-call | tf_op jit(solution)/shard_map/adjoint/pallas_call | solution.py:532
  43.9 0.6 %collective-permute-done.1.other_ref = f32[928,128]{1,0:T(8,128)S(1)} collective-permute-done((f32[928,128]{1,0:T(8,128)S(1)}, f32[928,128]{1,0:T(8,128)S(1)}, u32[]{:S(2)}, u32[]{:S(2)}) %collective-permute-start.1) | collective-permute-done | bytes 475168 | tf_op jit(solution)/shard_map/ppermute | solution.py:530
  44.5 0.0 copy-done.1
  44.5 1.4 %last.1 = (f32[256,128]{1,0:T(8,128)}, f32[2,256,128]{2,1,0:T(8,128)}) custom-call(f32[928,128]{1,0:T(8,128)S(1)} %bitcast.18, f32[928,128]{1,0:T(8,128)S(1)} %collective-permute-done.1.other_ref, f32[256,128]{1,0:T(8,128)S(1)} %bitcast.23, f32[3,3,256,256]{3,2,1,0:T(8,128)S(1)} %copy-done, f32[128,256]{1,0:T(8,128)S(1)} %get-tuple-element.18.total_ref), custom_call_target="tpu_custom_call" | custom-call | tf_op jit(solution)/shard_map/last/pallas_call | solution.py:541
Async XLA Ops:
  0.6 2.2 %collective-permute-start = (f32[256,128]{1,0:T(8,128)}, f32[256,128]{1,0:T(8,128)S(1)}, u32[]{:S(2)}, u32[]{:S(2)}) collective-permute-start(f32[256,128]{1,0:T(8,128)} %bitcast.24), channel_id=1, source_target_pairs={{0,8},{8,0},{16,24},{24,16},{1,9},{9,1},{17,25},{25,17},{2,10},{10... | collective-permute-start | bytes 393224 | tf_op jit(solution)/shard_map/ppermute | solution.py:494
  2.8 21.5 %copy-start.3 = (f32[256,256]{1,0:T(8,128)S(1)}, f32[256,256]{1,0:T(8,128)}, u32[]{:S(2)}) copy-start(f32[256,256]{1,0:T(8,128)} %constant.5.clone.dft_ref) | copy-start | bytes 786436
  2.9 21.5 %copy-start.4 = (f32[16,128]{1,0:T(8,128)S(1)}, f32[16,128]{1,0:T(8,128)}, u32[]{:S(2)}) copy-start(f32[16,128]{1,0:T(8,128)} %constant.4.clone.turn_ref) | copy-start | bytes 24580
  2.9 39.8 %copy-start = (f32[3,3,256,256]{3,2,1,0:T(8,128)S(1)}, f32[3,3,256,256]{3,2,1,0:T(8,128)}, u32[]{:S(2)}) copy-start(f32[3,3,256,256]{3,2,1,0:T(8,128)} %taps_ref.5) | copy-start | bytes 7077892
  2.9 39.8 %copy-start.2 = (f32[256,1,128]{2,1,0:T(1,128)S(1)}, f32[256,1,128]{2,1,0:T(1,128)}, u32[]{:S(2)}) copy-start(f32[256,1,128]{2,1,0:T(1,128)} %param.6) | copy-start | bytes 393220
  24.4 20.2 %copy-start.1 = (f32[256,1,128]{2,1,0:T(1,128)S(1)}, f32[256,1,128]{2,1,0:T(1,128)}, u32[]{:S(2)}) copy-start(f32[256,1,128]{2,1,0:T(1,128)} %param.7) | copy-start | bytes 393220
  42.7 1.8 %collective-permute-start.1 = (f32[928,128]{1,0:T(8,128)S(1)}, f32[928,128]{1,0:T(8,128)S(1)}, u32[]{:S(2)}, u32[]{:S(2)}) collective-permute-start(f32[928,128]{1,0:T(8,128)S(1)} %bitcast.16), channel_id=1, source_target_pairs={{0,8},{8,0},{16,24},{24,16},{1,9},{9,1},{17,25},{25,17},{2,10},{10... | collective-permute-start | bytes 1425416 | tf_op jit(solution)/shard_map/ppermute | solution.py:530

commit v4 on v3

--- a/solution.py
+++ b/solution.py
@@ -163,7 +163,8 @@
     return (output, input_grad, filter_grad)
 
 
-FORTH, BACK = 25, 29
+FORTH, BACK = 49, 57
+FIRST_COPIES, IN_FLIGHT = 5, 2
 
 
 def reversed_bits(value, width):
@@ -177,50 +178,36 @@
 
 
 def fetch_kernel(
-    own_ref, cot_ref, filter_ref, taps_ref, own_out, middle, side, cross, out_ref, cot, gain, sems
+    own_ref, cot_ref, filter_ref, taps_ref, own_out, cot_out, gain_out, taps_out, sems
 ):
     place = lax.axis_index("lat")
-    odd, half = lax.rem(place, 2), gain.shape[0]
+    odd, half = lax.rem(place, 2), gain_out.shape[0]
     span = pl.ds(pl.multiple_of(odd * half, half), half)
-    cross_row = 2 * (place // 2)
     copies = [
-        pltpu.make_async_copy(cot_ref, cot, sems.at[0]),
-        pltpu.make_async_copy(filter_ref.at[place // 2, span], gain, sems.at[1]),
-        pltpu.make_async_copy(own_ref, own_out, sems.at[2]),
-        pltpu.make_async_copy(taps_ref.at[1], middle, sems.at[3]),
-        pltpu.make_async_copy(taps_ref.at[2 - 2 * odd], side, sems.at[4]),
+        pltpu.make_async_copy(own_ref, own_out, sems.at[0]),
+        pltpu.make_async_copy(cot_ref, cot_out, sems.at[1]),
+        pltpu.make_async_copy(filter_ref.at[place // 2, span], gain_out, sems.at[2]),
     ]
-    for tap_col in range(3):
-        piece = taps_ref.at[cross_row, tap_col, span]
-        copies.append(pltpu.make_async_copy(piece, cross.at[tap_col], sems.at[5 + tap_col]))
-    for copy in copies:
-        copy.start()
-    copies[0].wait()
-    copies[1].wait()
-    for owner in range(half // 4):
-        first, here = FORTH * owner, slice(4 * owner, 4 * owner + 4)
-        out_ref[first : first + 4, :] = cot[here]
-        out_ref[first + 4 : first + 8, :] = cot[half + 4 * owner : half + 4 * owner + 4]
-        out_ref[first + 20 : first + 24, :] = gain[here]
-    for copy in copies[2:]:
-        copy.wait()
+
+    @pl.when(odd == 1)
+    def _():
+        half_taps = pltpu.make_async_copy(taps_ref.at[:, :, half:], taps_out, sems.at[3])
+        for copy in [half_taps] + copies:
+            copy.start()
+        for copy in [half_taps] + copies:
+            copy.wait()
+
+    @pl.when(odd == 0)
+    def _():
+        for copy in copies:
+            copy.start()
+        for copy in copies:
+            copy.wait()
 
 
 def high_low(x):
     high = x.astype(jnp.bfloat16)
     return high, (x - high.astype(jnp.float32)).astype(jnp.bfloat16)
-
-
-def both_parts(x):
-    return jnp.concatenate(high_low(x), axis=1)
-
-
-def product(weights, parts):
-    columns = parts.shape[1] // 2
-    high, low = high_low(weights)
-    wide = jnp.dot(high, parts, preferred_element_type=jnp.float32)
-    rest = jnp.dot(low, parts[:, :columns], preferred_element_type=jnp.float32)
-    return wide[:, :columns] + (wide[:, columns:] + rest)
 
 
 def tall_product(x, high, low):
@@ -232,36 +219,91 @@
     return both[:rows] + (both[rows:] + rest)
 
 
-def conv_kernel(own_ref, other_ref, middle_ref, side_ref, cross_ref, packed_ref, out_ref):
-    place = lax.axis_index("lat")
-    channels, columns = own_ref.shape
-    half = channels // 2
-    own, other = own_ref[...], other_ref[...]
-    near = jnp.where(jnp.logical_or(place == 1, place == 2), own, other)
-    own, other, near = both_parts(own), both_parts(other), both_parts(near)
+def conv_kernel(
+    own_ref, other_ref, cot_ref, other_cot_ref, gain_ref, half_ref, taps_ref, out_ref, taps, sems
+):
+    odd, upper = lax.rem(lax.axis_index("lat"), 2), lax.axis_index("lat") // 2
+    half = gain_ref.shape[0]
+    order = [(row, col) for col in range(3) for row in (1, 2 * upper, 2 - 2 * upper)]
+
+    @pl.when(odd == 0)
+    def _():
+        copies = [
+            pltpu.make_async_copy(taps_ref.at[row, col, :half], taps.at[index], sems.at[index])
+            for index, (row, col) in enumerate(order)
+        ]
+        for copy in copies[:FIRST_COPIES]:
+            copy.start()
+
+        def weights(index):
+            copies[index].wait()
+            if FIRST_COPIES <= index + IN_FLIGHT < len(copies):
+                copies[index + IN_FLIGHT].start()
+            return high_low(taps[index])
+
+        pack((own_ref, other_ref), (cot_ref, other_cot_ref), gain_ref, weights, 0, out_ref)
+
+    @pl.when(odd == 1)
+    def _():
+        def weights(index):
+            return high_low(half_ref[order[index]])
+
+        pack((other_ref, own_ref), (other_cot_ref, cot_ref), gain_ref, weights, 1, out_ref)
+
+
+def pack(fields, cots, gain_ref, weights, core, out_ref):
+    upper = lax.axis_index("lat") // 2
+    half, columns = gain_ref.shape
+    for owner in range(half // 8):
+        first, here = FORTH * owner, half * core + 8 * owner
+        out_ref[first : first + 8, :] = cots[0][here : here + 8, :]
+        out_ref[first + 8 : first + 16, :] = cots[1][here : here + 8, :]
+        out_ref[first + 40 : first + 48, :] = gain_ref[8 * owner : 8 * owner + 8, :]
+    row_0, row_1 = fields[0][...], fields[1][...]
+    near = jnp.concatenate(high_low(jnp.where(upper == 0, row_1, row_0)), axis=1)
+    both_high, both_low = high_low(jnp.concatenate([row_0, row_1], axis=1))
+
+    def times(weights, values):
+        return jnp.dot(weights, values, preferred_element_type=jnp.float32)
+
     parts = []
     for tap_col in range(3):
-        inner = product(middle_ref[tap_col], own) + product(side_ref[tap_col], other)
-        outer = product(cross_ref[tap_col], near)
-        parts.append(jnp.concatenate([inner, outer], axis=0))
-    lane, row = iotas(channels + half, columns)
+        high, low = weights(3 * tap_col)
+        middle = times(high, both_high) + (times(high, both_low) + times(low, both_high))
+        high, low = weights(3 * tap_col + 1)
+        outer = times(high, both_high) + (times(high, both_low) + times(low, both_high))
+        high, low = weights(3 * tap_col + 2)
+        wide = times(high, near)
+        inner = wide[:, :columns] + (wide[:, columns:] + times(low, near[:, :columns]))
+        on_0, on_1 = outer[:, :columns], outer[:, columns:]
+        parts.append(
+            jnp.concatenate(
+                [
+                    middle[:, :columns] + jnp.where(upper == 0, inner, on_1),
+                    middle[:, columns:] + jnp.where(upper == 0, on_0, inner),
+                    jnp.where(upper == 0, on_1, on_0),
+                ],
+                axis=0,
+            )
+        )
+    lane, row = iotas(3 * half, columns)
     left, middle, right = parts
     main = (
         middle
         + jnp.where(lane == 0, 0.0, pltpu.roll(left, 1, 1))
         + jnp.where(lane == columns - 1, 0.0, pltpu.roll(right, columns - 1, 1))
     )
-    slot = lane - lax.rem(row, 4) - 4 * (row // half)
+    slot = lane - lax.rem(row, 8) - 8 * (row // half)
     edges = jnp.where(slot == 0, left[:, columns - 1 :], 0.0)
-    edges = jnp.where(slot == 12, right[:, 0:1], edges)
-    edges = edges[:half] + edges[half:channels] + edges[channels:]
-    for owner in range(half // 4):
+    edges = jnp.where(slot == 24, right[:, 0:1], edges)
+    edges = edges[:half] + edges[half : 2 * half] + edges[2 * half :]
+    for owner in range(half // 8):
         first = FORTH * owner
         for part in range(3):
-            here = half * part + 4 * owner
-            out_ref[first + 8 + 4 * part : first + 12 + 4 * part, :] = main[here : here + 4]
-        out_ref[first + 24 : first + 25, :] = jnp.sum(
-            edges[4 * owner : 4 * owner + 4], axis=0, keepdims=True
+            here = half * part + 8 * owner
+            out_ref[first + 16 + 8 * part : first + 24 + 8 * part, :] = main[here : here + 8]
+        out_ref[first + 48 : first + 49, :] = jnp.sum(
+            edges[8 * owner : 8 * owner + 8], axis=0, keepdims=True
         )
 
 
@@ -282,32 +324,32 @@
     rows, lon = 4, 8
     columns = in_ref.shape[-1]
     lane, sub = iotas(8, columns)
-    me = lax.axis_index("lat") * lon + lax.axis_index("lon")
-    inward = {1: (2, 3), 2: (0, 1)}
-
-    def message(row, place, first, count):
-        start = FORTH * (row * lon + place) + first
+    me = lax.axis_index("lat") // 2 * lon + lax.axis_index("lon")
+
+    def message(chip, place, first, count):
+        start = FORTH * (chip * lon + place) + first
         return in_ref[start : start + count, :]
 
     def edge(row, place, group):
-        line = jnp.where(lane == sub + 12 * group, message(row, place, 24, 1), 0.0)
-        for part, giver in enumerate(inward.get(row, ())):
-            wanted = jnp.logical_and(lane == lax.rem(sub, 4) + 8 + 12 * group, sub // 4 == part)
-            line = line + jnp.where(wanted, message(giver, place, 24, 1), 0.0)
+        chip, part = row // 2, row % 2
+        wanted = lane == sub + 8 * part + 24 * group
+        line = jnp.where(wanted, message(chip, place, 48, 1), 0.0)
+        if row in (1, 2):
+            wanted = lane == sub + 16 + 24 * group
+            line = line + jnp.where(wanted, message(1 - chip, place, 48, 1), 0.0)
         return jnp.sum(line, axis=1, keepdims=True)
 
     grid = []
     for place in range(lon):
         mixed = []
         for row in range(rows):
-            tile = message(row, place, 8, 8)
-            if row in inward:
-                pieces = [message(giver, place, 16, 4) for giver in inward[row]]
-                tile = tile + jnp.concatenate(pieces, axis=0)
+            tile = message(row // 2, place, 16 + 8 * (row % 2), 8)
+            if row in (1, 2):
+                tile = tile + message(1 - row // 2, place, 32, 8)
             tile = tile + jnp.where(lane == 0, edge(row, (place - 1) % lon, 0), 0.0)
             tile = tile + jnp.where(lane == columns - 1, edge(row, (place + 1) % lon, 1), 0.0)
             mixed.append(tile)
-        cot = [message(row, place, 0, 8) for row in range(rows)]
+        cot = [message(row // 2, place, 8 * (row % 2), 8) for row in range(rows)]
         grid.append(jnp.concatenate(mixed + cot, axis=0))
     pairs = transform_8(grid)
     height = 16 * rows
@@ -337,9 +379,8 @@
         part = spectra[residue * height : (residue + 1) * height]
         mix_re, mix_im = part[:half, :columns], part[:half, columns:]
         cot_re, cot_im = part[half:, :columns], part[half:, columns:]
-        quarters = [message(row, place, 20, 4) * scale for row in range(rows)]
-        gain_re = jnp.concatenate([jnp.concatenate(quarters[0:2], axis=0)] * rows, axis=0)
-        gain_im = jnp.concatenate([jnp.concatenate(quarters[2:4], axis=0)] * rows, axis=0)
+        gain_re = jnp.concatenate([message(0, place, 40, 8) * scale] * rows, axis=0)
+        gain_im = jnp.concatenate([message(1, place, 40, 8) * scale] * rows, axis=0)
         top = pl.ds(residue * height, half)
         bottom = pl.ds(residue * height + half, half)
         work[top, 0:columns] = gain_re * mix_re - gain_im * mix_im
@@ -379,51 +420,47 @@
         ROOT_HALF * (sums[2] - gaps[2] - sums[0] - gaps[0]),
     ]
     series = [even[d] + swing[d] for d in range(4)] + [even[d] - swing[d] for d in range(4)]
-    slots = [lane == 4 * lax.rem(me + group, 32) + lax.rem(sub, 4) for group in range(6)]
+    slots = [lane == 8 * lax.rem(me + group, 16) + sub for group in range(6)]
     for place in range(lon):
         residue = reversed_bits(place, 3)
         before, after = series[(place - 1) % lon], series[(place + 1) % lon]
         for chip in range(2):
+            start = BACK * (chip * lon + place)
             rims = jnp.zeros((8, columns), jnp.float32)
             for step in range(3):
-                span = slice(half + 8 * (chip + step), half + 8 * (chip + step) + 8)
+                here = half + 8 * (chip + step)
+                span = slice(here, here + 8)
                 rims = jnp.where(slots[2 * step], before[span, columns - 1 :], rims)
                 rims = jnp.where(slots[2 * step + 1], after[span, 0:1], rims)
+                first = start + 16 + 8 * step
+                out_ref[first : first + 8, :] = series[place][span]
+            out_ref[start : start + 16, :] = series[place][16 * chip : 16 * chip + 16]
             for part in range(2):
-                row = 2 * chip + part
-                start = BACK * (row * lon + place)
-                out_ref[start : start + 8, :] = series[place][8 * row : 8 * row + 8]
-                for step in range(3):
-                    here = half + 8 * (chip + step) + 4 * part
-                    out_ref[start + 8 + 4 * step : start + 12 + 4 * step, :] = series[place][
-                        here : here + 4
-                    ]
-                out_ref[start + 20 : start + 28, :] = gradients[residue][part]
-                out_ref[start + 28 : start + 29, :] = jnp.sum(
-                    rims[4 * part : 4 * part + 4], axis=0, keepdims=True
-                )
+                first = start + 40 + 8 * part
+                out_ref[first : first + 8, :] = gradients[residue][part]
+            out_ref[start + 56 : start + 57, :] = jnp.sum(rims, axis=0, keepdims=True)
 
 
 def partial_adjoint(message_ref, taps_ref, rows_ref, part):
     half, columns = rows_ref.shape[-1], message_ref.shape[-1]
     place = lax.axis_index("lat")
     index = place - place // 2
-    owners = half // 4
-    lines = message_ref[pl.ds(28, owners, stride=BACK), :]
+    owners = half // 8
+    lines = message_ref[pl.ds(56, owners, stride=BACK), :]
     lane, owner = iotas(owners, columns)
     rows_ref[0] = jnp.zeros(rows_ref.shape[1:], jnp.float32)
     rows_ref[4] = jnp.zeros(rows_ref.shape[1:], jnp.float32)
     for step in range(3):
         pieces = [
-            message_ref[BACK * j + 8 + 4 * step : BACK * j + 12 + 4 * step, :] for j in range(owners)
+            message_ref[BACK * j + 16 + 8 * step : BACK * j + 24 + 8 * step, :] for j in range(owners)
         ]
         rows_ref[1 + step, 8 : 8 + columns, :] = jnp.concatenate(pieces, axis=0).T
         for rim, target in ((2 * step, 7), (2 * step + 1, 8 + columns)):
-            wanted = lane // 4 == lax.rem(owner + rim, owners)
+            wanted = lane // 8 == lax.rem(owner + rim, owners)
             line = jnp.sum(jnp.where(wanted, lines, 0.0), axis=0, keepdims=True)
             line = jnp.broadcast_to(line, (8, columns))
             if rim:
-                line = pltpu.roll(line, columns - 4 * rim, 1)
+                line = pltpu.roll(line, columns - 8 * rim, 1)
             rows_ref[1 + step, target : target + 1, :] = line[0:1]
     span = pl.ds(pl.multiple_of(part * half, half), half)
     windows, weights = [], []
@@ -440,24 +477,24 @@
     return total
 
 
-def adjoint_kernel(mine_ref, field_ref, taps_ref, out_ref, total_ref, rows_ref):
-    half = field_ref.shape[0] // 2
-    for owner in range(half // 4):
-        for part in range(2):
-            here, there = half * part + 4 * owner, BACK * owner + 4 * part
-            out_ref[here : here + 4, :] = field_ref[here : here + 4, :] + mine_ref[there : there + 4, :]
+def adjoint_kernel(mine_ref, taps_ref, total_ref, rows_ref):
     part = lax.rem(lax.axis_index("lat"), 2)
     total_ref[...] = partial_adjoint(mine_ref, taps_ref, rows_ref, part)
 
 
-def last_kernel(mine_ref, other_ref, cot_ref, taps_ref, total_ref, grad_ref, gain_ref, rows_ref):
+def last_kernel(
+    mine_ref, other_ref, field_ref, cot_ref, taps_ref, total_ref, out_ref, grad_ref, gain_ref, rows_ref
+):
     half = cot_ref.shape[0] // 2
     part = lax.rem(lax.axis_index("lat"), 2)
-    for owner in range(half // 4):
-        for piece in range(2):
-            here, there = half * piece + 4 * owner, BACK * owner + 20 + 4 * piece
-            gain_ref[part, here : here + 4, :] = mine_ref[there : there + 4, :]
-            gain_ref[1 - part, here : here + 4, :] = other_ref[there : there + 4, :]
+    for message_ref, side in ((mine_ref, part), (other_ref, 1 - part)):
+        for owner in range(half // 8):
+            here = pl.ds(pl.multiple_of(half * side + 8 * owner, 8), 8)
+            start = BACK * owner
+            first, second = message_ref[start : start + 8, :], message_ref[start + 8 : start + 16, :]
+            out_ref[here, :] = field_ref[here, :] + jnp.where(part == 0, first, second)
+            gain_ref[0, here, :] = message_ref[start + 40 : start + 48, :]
+            gain_ref[1, here, :] = message_ref[start + 48 : start + 56, :]
     total = total_ref[...] + partial_adjoint(other_ref, taps_ref, rows_ref, 1 - part)
     grad_ref[...] = cot_ref[...] + total.T
 
@@ -472,16 +509,31 @@
     return jnp.asarray(turns, jnp.float32), jnp.asarray(dft, jnp.float32)
 
 
-def exchanged(flat):
+def exchanged(flat, lat, lon):
     rows, columns = flat.shape
-    moved = lax.all_to_all(flat.reshape(rows, 1, columns), ("lat", "lon"), 0, 0, tiled=True)
+    groups = [
+        [(2 * chip + core) * lon + place for chip in range(lat // 2) for place in range(lon)]
+        for core in range(2)
+    ]
+    moved = lax.all_to_all(
+        flat.reshape(rows, 1, columns),
+        ("lat", "lon"),
+        0,
+        0,
+        tiled=True,
+        axis_index_groups=groups,
+    )
     return moved.reshape(rows, columns)
+
+
+def in_hbm(x):
+    return pltpu.with_memory_space_constraint(x, pltpu.HBM)
 
 
 def on_device(field, cotangent, conv_weight, spectral_filter):
     channels, _, columns = field.shape
     lat, lon = lax.axis_size("lat"), lax.axis_size("lon")
-    owners = lat * lon
+    owners = lat * lon // 2
     swap = [(i, i ^ 1) for i in range(lat)]
     own = field.reshape(channels, columns)
     cot = cotangent.reshape(channels, columns)
@@ -489,33 +541,32 @@
     hbm = pl.BlockSpec(memory_space=pltpu.HBM)
     params = pltpu.CompilerParams(vmem_limit_bytes=16 * 1024 * 1024)
     flat = jax.ShapeDtypeStruct((channels, columns), jnp.float32)
+    half_taps = jax.ShapeDtypeStruct((3, 3, channels // 2, channels), jnp.float32)
     forth = jax.ShapeDtypeStruct((owners * FORTH, columns), jnp.float32)
     back = jax.ShapeDtypeStruct((owners * BACK, columns), jnp.float32)
-    other = lax.ppermute(own, "lat", swap)
-    row_shape = jax.ShapeDtypeStruct(conv_weight.shape[1:], jnp.float32)
-    half_shape = jax.ShapeDtypeStruct((3, channels // 2, channels), jnp.float32)
-    *fetched, packed = pl.pallas_call(
+    other, other_cot = lax.ppermute((own, cot), "lat", swap)
+    gain_half = jax.ShapeDtypeStruct((channels // 2, columns), jnp.float32)
+    own_here, cot_here, gain, taps = pl.pallas_call(
         fetch_kernel,
-        out_shape=(flat, row_shape, row_shape, half_shape, forth),
+        out_shape=(flat, flat, gain_half, half_taps),
         in_specs=[hbm] * 4,
-        out_specs=(vmem,) * 5,
-        scratch_shapes=[
-            pltpu.VMEM((channels, columns), jnp.float32),
-            pltpu.VMEM((channels // 2, columns), jnp.float32),
-            pltpu.SemaphoreType.DMA((8,)),
-        ],
+        out_specs=(vmem,) * 4,
+        scratch_shapes=[pltpu.SemaphoreType.DMA((4,))],
         compiler_params=params,
         name="fetch",
-    )(*[pltpu.with_memory_space_constraint(x, pltpu.HBM) for x in (own, cot, spectral_filter, conv_weight)])
+    )(*map(in_hbm, (own, cot, spectral_filter, conv_weight)))
     outgoing = pl.pallas_call(
         conv_kernel,
         out_shape=forth,
-        in_specs=[vmem] * 6,
+        in_specs=[vmem] * 6 + [hbm],
         out_specs=vmem,
-        input_output_aliases={5: 0},
+        scratch_shapes=[
+            pltpu.VMEM((9, channels // 2, channels), jnp.float32),
+            pltpu.SemaphoreType.DMA((9,)),
+        ],
         compiler_params=params,
         name="conv",
-    )(fetched[0], other, *fetched[1:], packed)
+    )(own_here, other, cot_here, other_cot, gain, taps, in_hbm(conv_weight))
     turns, dft = transform_tables(columns, lon)
     returned = pl.pallas_call(
         spectral_kernel,
@@ -525,28 +576,28 @@
         scratch_shapes=[pltpu.VMEM((2 * 8 * lat * lon, 2 * columns), jnp.float32)],
         compiler_params=params,
         name="spectral",
-    )(exchanged(outgoing), turns, dft)
-    mine = exchanged(returned)
+    )(exchanged(outgoing, lat, lon), turns, dft)
+    mine = exchanged(returned, lat, lon)
     other = lax.ppermute(mine, "lat", swap)
     rows_scratch = pltpu.VMEM((5, columns + 16, channels // 2), jnp.float32)
-    output, total = pl.pallas_call(
+    total = pl.pallas_call(
         adjoint_kernel,
-        out_shape=(flat, jax.ShapeDtypeStruct((columns, channels), jnp.float32)),
-        in_specs=[vmem] * 3,
-        out_specs=(vmem, vmem),
+        out_shape=jax.ShapeDtypeStruct((columns, channels), jnp.float32),
+        in_specs=[vmem] * 2,
+        out_specs=vmem,
         scratch_shapes=[rows_scratch],
         compiler_params=params,
         name="adjoint",
-    )(mine, own, conv_weight)
-    input_grad, filter_grad = pl.pallas_call(
+    )(mine, conv_weight)
+    output, input_grad, filter_grad = pl.pallas_call(
         last_kernel,
-        out_shape=(flat, jax.ShapeDtypeStruct(spectral_filter.shape, jnp.float32)),
-        in_specs=[vmem] * 5,
-        out_specs=(vmem, vmem),
+        out_shape=(flat, flat, jax.ShapeDtypeStruct(spectral_filter.shape, jnp.float32)),
+        in_specs=[vmem] * 6,
+        out_specs=(vmem, vmem, vmem),
         scratch_shapes=[rows_scratch],
         compiler_params=params,
         name="last",
-    )(mine, other, cot, conv_weight, total)
+    )(mine, other, own, cot, conv_weight, total)
     return (output.reshape(field.shape), input_grad.reshape(field.shape), filter_grad)
 
 

time: 46.1 us -> 42.6 us (0.924)
  blocking collectives: 38 us -> 31.2 us
  Pallas kernels: 5.97 us -> 8.06 us
  waiting for transfers between devices: 0.63 us -> 1.72 us
    all_to_all x2, blocking collectives: 38 us -> 31.2 us  [exchanged(): lax.all_to_all(flat.reshape(rows, 1, columns), ('lat', 'lon'), 0, 0, tile...]
    pallas_call x4, Pallas kernels: 5.02 us -> 7.09 us  [the longest x1 4.13 us: on_device(): pl.pallas_call(conv_kernel, out_shape=forth, in_specs=[vmem] * 6 + [hbm],...]
    ppermute x1, waiting for transfers between devices: 0.63 us -> 1.25 us  [on_device(): other = lax.ppermute(mine, 'lat', swap)]
    ppermute x1 -> x2, waiting for transfers between devices: 0.01 us -> 0.47 us  [on_device(): other, other_cot = lax.ppermute((own, cot), 'lat', swap)]
  transfers between devices with their start and end apart: 2 -> 3, of which waited for: 1 -> 3; matrix products, arithmetic and copies ran while one was open for 0% -> 0% of each run, Pallas kernels for 6% -> 4%
where the time goes in v4:
time: 42.6 us; the launch traced here: 42.3 us
  blocking collectives  31.2 us (73%)
  Pallas kernels  8.06 us (19%)
  waiting for transfers between devices  1.72 us (4%)
  between operations  0.68 us (2%)
  starting transfers between devices  0.6 us (1%)
    all_to_all x2, blocking collectives, exchanged(): lax.all_to_all(flat.reshape(rows, 1, columns), ('lat', 'lon'), 0, 0, tile...  31.2 us
    pallas_call x1, Pallas kernels, on_device(): pl.pallas_call(conv_kernel, out_shape=forth, in_specs=[vmem] * 6 + [hbm],...  4.13 us
    pallas_call x1, Pallas kernels, on_device(): pl.pallas_call(last_kernel, out_shape=(flat, flat, jax.ShapeDtypeStruct(s...  1.4 us
    ppermute x1, waiting for transfers between devices, on_device(): other = lax.ppermute(mine, 'lat', swap)  1.25 us
    pallas_call x1, Pallas kernels, on_device(): pl.pallas_call(fetch_kernel, out_shape=(flat, flat, gain_half, half_taps)...  1 us
    pallas_call x1, Pallas kernels, on_device(): pl.pallas_call(spectral_kernel, out_shape=back, in_specs=[vmem] * 3, out_...  0.96 us
  transfers between devices with their start and end apart: 3, of which 3 were waited for; matrix products, arithmetic and copies ran while one was open for 0% of the time, Pallas kernels for 4%

profile of v4, /device:TPU:0, one launch (start us, length us, event | category | flops | bytes accessed | tf_op | source)
XLA Modules:
  0.0 42.3 jit_solution(16548786565167120163)
XLA Ops:
  0.6 0.5 %collective-permute-start = (f32[256,128]{1,0:T(8,128)}, f32[256,128]{1,0:T(8,128)S(1)}, u32[]{:S(2)}, u32[]{:S(2)}) collective-permute-start(f32[256,128]{1,0:T(8,128)} %bitcast.22), channel_id=1, source_target_pairs={{0,8},{8,0},{16,24},{24,16},{1,9},{9,1},{17,25},{25,17},{2,10},{10... | collective-permute-start | bytes 393224 | tf_op jit(solution)/shard_map/ppermute | solution.py:547
  1.1 0.1 collective-permute-start.1
  1.2 1.0 %fetch.1 = (f32[256,128]{1,0:T(8,128)S(1)}, f32[256,128]{1,0:T(8,128)S(1)}, f32[128,128]{1,0:T(8,128)S(1)}, f32[3,3,128,256]{3,2,1,0:T(8,128)S(1)}) custom-call(f32[256,128]{1,0:T(8,128)} %bitcast.23, f32[256,128]{1,0:T(8,128)} %bitcast.26, f32[2,256,128]{2,1,0:T(8,128)} %filter_ref.1, f32[3,3,256,256]{3,2,1,0:T(8,128)} %taps_ref.7), custom_call_target="tpu_custom_call" | custom-call | tf_op jit(solution)/shard_map/fetch/pallas_call | solution.py:549
  2.2 0.1 collective-permute-done.other_ref
  2.3 0.4 collective-permute-done.1.other_cot_ref
  2.7 0.0 copy-start.3
  2.7 0.0 copy-start.4
  2.7 4.1 %conv.1 = f32[784,128]{1,0:T(8,128)S(1)} custom-call(f32[256,128]{1,0:T(8,128)S(1)} %get-tuple-element.10.own_ref, f32[256,128]{1,0:T(8,128)S(1)} %collective-permute-done.other_ref, f32[256,128]{1,0:T(8,128)S(1)} %get-tuple-element.11.cot_ref, f32[256,128]{1,0:T(8,128)S(1)} %collective-permute-done.1.other_cot_ref, ...), custom_call_target="tpu_custom_call" | custom-call | tf_op jit(solution)/shard_map/conv/pallas_call | solution.py:558
  6.8 0.0 copy-start
  6.9 17.6 %all_to_all.10 = f32[784,1,128]{2,1,0:T(1,128)S(1)} all-to-all(f32[784,1,128]{2,1,0:T(1,128)S(1)} %bitcast.20), channel_id=1, replica_groups={{0,1,2,3,4,5,6,7,16,17,18,19,20,21,22,23},{8,9,10,11,12,13,14,15,24,25,..., dimensions={0} | all-to-all | bytes 802816 | tf_op jit(solution)/shard_map/all_to_all | solution.py:518
  24.4 0.0 copy-done.3
  24.4 0.0 copy-done.4
  24.4 0.0 copy-start.1
  24.4 0.0 copy-start.2
  24.5 1.0 %spectral.1 = f32[912,128]{1,0:T(8,128)S(1)} custom-call(f32[784,128]{1,0:T(8,128)S(1)} %bitcast.21, f32[16,128]{1,0:T(8,128)S(1)} %copy-done.4, f32[256,256]{1,0:T(8,128)S(1)} %copy-done.3), custom_call_target="tpu_custom_call" | custom-call | tf_op jit(solution)/shard_map/spectral/pallas_call | solution.py:571
  25.4 13.7 %all_to_all.11 = f32[912,1,128]{2,1,0:T(1,128)S(1)} all-to-all(f32[912,1,128]{2,1,0:T(1,128)S(1)} %bitcast.19), channel_id=1, replica_groups={{0,1,2,3,4,5,6,7,16,17,18,19,20,21,22,23},{8,9,10,11,12,13,14,15,24,25,..., dimensions={0} | all-to-all | bytes 933888 | tf_op jit(solution)/shard_map/all_to_all | solution.py:518
  39.1 0.0 collective-permute-start.2
  39.1 0.0 copy-done
  39.1 0.6 %adjoint.1.total_ref = f32[128,256]{1,0:T(8,128)S(1)} custom-call(f32[912,128]{1,0:T(8,128)S(1)} %bitcast.17, f32[3,3,256,256]{3,2,1,0:T(8,128)S(1)} %copy-done), custom_call_target="tpu_custom_call" | custom-call | tf_op jit(solution)/shard_map/adjoint/pallas_call | solution.py:583
  39.7 1.3 %collective-permute-done.2.other_ref = f32[912,128]{1,0:T(8,128)S(1)} collective-permute-done((f32[912,128]{1,0:T(8,128)S(1)}, f32[912,128]{1,0:T(8,128)S(1)}, u32[]{:S(2)}, u32[]{:S(2)}) %collective-permute-start.2) | collective-permute-done | bytes 466976 | tf_op jit(solution)/shard_map/ppermute | solution.py:581
  40.9 0.0 copy-done.1
  40.9 0.0 copy-done.2
  40.9 1.4 %last.1 = (f32[256,128]{1,0:T(8,128)}, f32[256,128]{1,0:T(8,128)}, f32[2,256,128]{2,1,0:T(8,128)}) custom-call(f32[912,128]{1,0:T(8,128)S(1)} %bitcast.18, f32[912,128]{1,0:T(8,128)S(1)} %collective-permute-done.2.other_ref, f32[256,128]{1,0:T(8,128)S(1)} %bitcast.24, f32[256,128]{1,0:T(8,128)S(1)} %bitcast.27, f32[3,3,256,256]{3,2,1,0:T(8,128)S(1)} %copy-done, ...), custom_call_target="tpu_custom_call" | custom-call | tf_op jit(solution)/shard_map/last/pallas_call | solution.py:592
Async XLA Ops:
  0.6 1.7 %collective-permute-start = (f32[256,128]{1,0:T(8,128)}, f32[256,128]{1,0:T(8,128)S(1)}, u32[]{:S(2)}, u32[]{:S(2)}) collective-permute-start(f32[256,128]{1,0:T(8,128)} %bitcast.22), channel_id=1, source_target_pairs={{0,8},{8,0},{16,24},{24,16},{1,9},{9,1},{17,25},{25,17},{2,10},{10... | collective-permute-start | bytes 393224 | tf_op jit(solution)/shard_map/ppermute | solution.py:547
  1.1 1.6 %collective-permute-start.1 = (f32[256,128]{1,0:T(8,128)}, f32[256,128]{1,0:T(8,128)S(1)}, u32[]{:S(2)}, u32[]{:S(2)}) collective-permute-start(f32[256,128]{1,0:T(8,128)} %bitcast.25), channel_id=1, source_target_pairs={{0,8},{8,0},{16,24},{24,16},{1,9},{9,1},{17,25},{25,17},{2,10},{10... | collective-permute-start | bytes 393224 | tf_op jit(solution)/shard_map/ppermute | solution.py:547
  2.7 21.7 %copy-start.3 = (f32[256,256]{1,0:T(8,128)S(1)}, f32[256,256]{1,0:T(8,128)}, u32[]{:S(2)}) copy-start(f32[256,256]{1,0:T(8,128)} %constant.5.clone.dft_ref) | copy-start | bytes 786436
  2.7 21.7 %copy-start.4 = (f32[16,128]{1,0:T(8,128)S(1)}, f32[16,128]{1,0:T(8,128)}, u32[]{:S(2)}) copy-start(f32[16,128]{1,0:T(8,128)} %constant.4.clone.turn_ref) | copy-start | bytes 24580
  6.8 32.2 %copy-start = (f32[3,3,256,256]{3,2,1,0:T(8,128)S(1)}, f32[3,3,256,256]{3,2,1,0:T(8,128)}, u32[]{:S(2)}) copy-start(f32[3,3,256,256]{3,2,1,0:T(8,128)} %taps_ref.7) | copy-start | bytes 7077892
  24.4 16.5 %copy-start.1 = (f32[256,1,128]{2,1,0:T(1,128)S(1)}, f32[256,1,128]{2,1,0:T(1,128)}, u32[]{:S(2)}) copy-start(f32[256,1,128]{2,1,0:T(1,128)} %param.6) | copy-start | bytes 393220
  24.4 16.5 %copy-start.2 = (f32[256,1,128]{2,1,0:T(1,128)S(1)}, f32[256,1,128]{2,1,0:T(1,128)}, u32[]{:S(2)}) copy-start(f32[256,1,128]{2,1,0:T(1,128)} %param.7) | copy-start | bytes 393220
  39.1 1.8 %collective-permute-start.2 = (f32[912,128]{1,0:T(8,128)S(1)}, f32[912,128]{1,0:T(8,128)S(1)}, u32[]{:S(2)}, u32[]{:S(2)}) collective-permute-start(f32[912,128]{1,0:T(8,128)S(1)} %bitcast.16), channel_id=1, source_target_pairs={{0,8},{8,0},{16,24},{24,16},{1,9},{9,1},{17,25},{25,17},{2,10},{10... | collective-permute-start | bytes 1400840 | tf_op jit(solution)/shard_map/ppermute | solution.py:581

commit v5 on v4

--- a/solution.py
+++ b/solution.py
@@ -165,6 +165,10 @@
 
 FORTH, BACK = 49, 57
 FIRST_COPIES, IN_FLIGHT = 5, 2
+
+
+def rank(chip, place):
+    return 8 * (place % 2) + 4 * chip + 2 * (place // 2 % 2) + place // 4
 
 
 def reversed_bits(value, width):
@@ -324,10 +328,10 @@
     rows, lon = 4, 8
     columns = in_ref.shape[-1]
     lane, sub = iotas(8, columns)
-    me = lax.axis_index("lat") // 2 * lon + lax.axis_index("lon")
+    me = rank(lax.axis_index("lat") // 2, lax.axis_index("lon"))
 
     def message(chip, place, first, count):
-        start = FORTH * (chip * lon + place) + first
+        start = FORTH * rank(chip, place) + first
         return in_ref[start : start + count, :]
 
     def edge(row, place, group):
@@ -425,7 +429,7 @@
         residue = reversed_bits(place, 3)
         before, after = series[(place - 1) % lon], series[(place + 1) % lon]
         for chip in range(2):
-            start = BACK * (chip * lon + place)
+            start = BACK * rank(chip, place)
             rims = jnp.zeros((8, columns), jnp.float32)
             for step in range(3):
                 here = half + 8 * (chip + step)
@@ -511,10 +515,9 @@
 
 def exchanged(flat, lat, lon):
     rows, columns = flat.shape
-    groups = [
-        [(2 * chip + core) * lon + place for chip in range(lat // 2) for place in range(lon)]
-        for core in range(2)
-    ]
+    members = [(chip, place) for chip in range(lat // 2) for place in range(lon)]
+    members.sort(key=lambda member: rank(*member))
+    groups = [[(2 * chip + core) * lon + place for chip, place in members] for core in range(2)]
     moved = lax.all_to_all(
         flat.reshape(rows, 1, columns),
         ("lat", "lon"),

time: 42.6 us -> 42 us (0.986)
  blocking collectives: 31.2 us -> 30.7 us
    all_to_all x2, blocking collectives: 31.2 us -> 30.7 us  [exchanged(): lax.all_to_all(flat.reshape(rows, 1, columns), ('lat', 'lon'), 0, 0, tile...]
where the time goes in v5:
time: 42 us; the launch traced here: 41.7 us
  blocking collectives  30.7 us (73%)
  Pallas kernels  8.06 us (19%)
  waiting for transfers between devices  1.71 us (4%)
  between operations  0.68 us (2%)
  starting transfers between devices  0.6 us (1%)
    all_to_all x2, blocking collectives, exchanged(): lax.all_to_all(flat.reshape(rows, 1, columns), ('lat', 'lon'), 0, 0, tile...  30.7 us
    pallas_call x1, Pallas kernels, on_device(): pl.pallas_call(conv_kernel, out_shape=forth, in_specs=[vmem] * 6 + [hbm],...  4.13 us
    pallas_call x1, Pallas kernels, on_device(): pl.pallas_call(last_kernel, out_shape=(flat, flat, jax.ShapeDtypeStruct(s...  1.39 us
    ppermute x1, waiting for transfers between devices, on_device(): other = lax.ppermute(mine, 'lat', swap)  1.25 us
    pallas_call x1, Pallas kernels, on_device(): pl.pallas_call(fetch_kernel, out_shape=(flat, flat, gain_half, half_taps)...  1 us
    pallas_call x1, Pallas kernels, on_device(): pl.pallas_call(spectral_kernel, out_shape=back, in_specs=[vmem] * 3, out_...  0.96 us
  transfers between devices with their start and end apart: 3, of which 3 were waited for; matrix products, arithmetic and copies ran while one was open for 0% of the time, Pallas kernels for 4%

profile of v5, /device:TPU:0, one launch (start us, length us, event | category | flops | bytes accessed | tf_op | source)
XLA Modules:
  0.0 41.7 jit_solution(10013155377118501448)
XLA Ops:
  0.6 0.5 %collective-permute-start = (f32[256,128]{1,0:T(8,128)}, f32[256,128]{1,0:T(8,128)S(1)}, u32[]{:S(2)}, u32[]{:S(2)}) collective-permute-start(f32[256,128]{1,0:T(8,128)} %bitcast.22), channel_id=1, source_target_pairs={{0,8},{8,0},{16,24},{24,16},{1,9},{9,1},{17,25},{25,17},{2,10},{10... | collective-permute-start | bytes 393224 | tf_op jit(solution)/shard_map/ppermute | solution.py:550
  1.1 0.1 collective-permute-start.1
  1.2 1.0 %fetch.1 = (f32[256,128]{1,0:T(8,128)S(1)}, f32[256,128]{1,0:T(8,128)S(1)}, f32[128,128]{1,0:T(8,128)S(1)}, f32[3,3,128,256]{3,2,1,0:T(8,128)S(1)}) custom-call(f32[256,128]{1,0:T(8,128)} %bitcast.23, f32[256,128]{1,0:T(8,128)} %bitcast.26, f32[2,256,128]{2,1,0:T(8,128)} %filter_ref.1, f32[3,3,256,256]{3,2,1,0:T(8,128)} %taps_ref.7), custom_call_target="tpu_custom_call" | custom-call | tf_op jit(solution)/shard_map/fetch/pallas_call | solution.py:552
  2.2 0.1 collective-permute-done.other_ref
  2.3 0.4 collective-permute-done.1.other_cot_ref
  2.7 0.0 copy-start.3
  2.7 0.0 copy-start.4
  2.7 4.1 %conv.1 = f32[784,128]{1,0:T(8,128)S(1)} custom-call(f32[256,128]{1,0:T(8,128)S(1)} %get-tuple-element.10.own_ref, f32[256,128]{1,0:T(8,128)S(1)} %collective-permute-done.other_ref, f32[256,128]{1,0:T(8,128)S(1)} %get-tuple-element.11.cot_ref, f32[256,128]{1,0:T(8,128)S(1)} %collective-permute-done.1.other_cot_ref, ...), custom_call_target="tpu_custom_call" | custom-call | tf_op jit(solution)/shard_map/conv/pallas_call | solution.py:561
  6.8 0.0 copy-start
  6.9 16.9 %all_to_all.10 = f32[784,1,128]{2,1,0:T(1,128)S(1)} all-to-all(f32[784,1,128]{2,1,0:T(1,128)S(1)} %bitcast.20), channel_id=1, replica_groups={{0,4,2,6,16,20,18,22,1,5,3,7,17,21,19,23},{8,12,10,14,24,28,26,30,9,13,..., dimensions={0} | all-to-all | bytes 802816 | tf_op jit(solution)/shard_map/all_to_all | solution.py:521
  23.8 0.0 copy-done.3
  23.8 0.0 copy-done.4
  23.8 0.0 copy-start.1
  23.8 0.0 copy-start.2
  23.8 1.0 %spectral.1 = f32[912,128]{1,0:T(8,128)S(1)} custom-call(f32[784,128]{1,0:T(8,128)S(1)} %bitcast.21, f32[16,128]{1,0:T(8,128)S(1)} %copy-done.4, f32[256,256]{1,0:T(8,128)S(1)} %copy-done.3), custom_call_target="tpu_custom_call" | custom-call | tf_op jit(solution)/shard_map/spectral/pallas_call | solution.py:574
  24.8 13.8 %all_to_all.11 = f32[912,1,128]{2,1,0:T(1,128)S(1)} all-to-all(f32[912,1,128]{2,1,0:T(1,128)S(1)} %bitcast.19), channel_id=1, replica_groups={{0,4,2,6,16,20,18,22,1,5,3,7,17,21,19,23},{8,12,10,14,24,28,26,30,9,13,..., dimensions={0} | all-to-all | bytes 933888 | tf_op jit(solution)/shard_map/all_to_all | solution.py:521
  38.5 0.0 collective-permute-start.2
  38.5 0.0 copy-done
  38.5 0.6 %adjoint.1.total_ref = f32[128,256]{1,0:T(8,128)S(1)} custom-call(f32[912,128]{1,0:T(8,128)S(1)} %bitcast.17, f32[3,3,256,256]{3,2,1,0:T(8,128)S(1)} %copy-done), custom_call_target="tpu_custom_call" | custom-call | tf_op jit(solution)/shard_map/adjoint/pallas_call | solution.py:586
  39.1 1.2 %collective-permute-done.2.other_ref = f32[912,128]{1,0:T(8,128)S(1)} collective-permute-done((f32[912,128]{1,0:T(8,128)S(1)}, f32[912,128]{1,0:T(8,128)S(1)}, u32[]{:S(2)}, u32[]{:S(2)}) %collective-permute-start.2) | collective-permute-done | bytes 466976 | tf_op jit(solution)/shard_map/ppermute | solution.py:584
  40.3 0.0 copy-done.1
  40.3 0.0 copy-done.2
  40.3 1.4 %last.1 = (f32[256,128]{1,0:T(8,128)}, f32[256,128]{1,0:T(8,128)}, f32[2,256,128]{2,1,0:T(8,128)}) custom-call(f32[912,128]{1,0:T(8,128)S(1)} %bitcast.18, f32[912,128]{1,0:T(8,128)S(1)} %collective-permute-done.2.other_ref, f32[256,128]{1,0:T(8,128)S(1)} %bitcast.24, f32[256,128]{1,0:T(8,128)S(1)} %bitcast.27, f32[3,3,256,256]{3,2,1,0:T(8,128)S(1)} %copy-done, ...), custom_call_target="tpu_custom_call" | custom-call | tf_op jit(solution)/shard_map/last/pallas_call | solution.py:595
Async XLA Ops:
  0.6 1.7 %collective-permute-start = (f32[256,128]{1,0:T(8,128)}, f32[256,128]{1,0:T(8,128)S(1)}, u32[]{:S(2)}, u32[]{:S(2)}) collective-permute-start(f32[256,128]{1,0:T(8,128)} %bitcast.22), channel_id=1, source_target_pairs={{0,8},{8,0},{16,24},{24,16},{1,9},{9,1},{17,25},{25,17},{2,10},{10... | collective-permute-start | bytes 393224 | tf_op jit(solution)/shard_map/ppermute | solution.py:550
  1.1 1.6 %collective-permute-start.1 = (f32[256,128]{1,0:T(8,128)}, f32[256,128]{1,0:T(8,128)S(1)}, u32[]{:S(2)}, u32[]{:S(2)}) collective-permute-start(f32[256,128]{1,0:T(8,128)} %bitcast.25), channel_id=1, source_target_pairs={{0,8},{8,0},{16,24},{24,16},{1,9},{9,1},{17,25},{25,17},{2,10},{10... | collective-permute-start | bytes 393224 | tf_op jit(solution)/shard_map/ppermute | solution.py:550
  2.7 21.1 %copy-start.3 = (f32[256,256]{1,0:T(8,128)S(1)}, f32[256,256]{1,0:T(8,128)}, u32[]{:S(2)}) copy-start(f32[256,256]{1,0:T(8,128)} %constant.5.clone.dft_ref) | copy-start | bytes 786436
  2.7 21.1 %copy-start.4 = (f32[16,128]{1,0:T(8,128)S(1)}, f32[16,128]{1,0:T(8,128)}, u32[]{:S(2)}) copy-start(f32[16,128]{1,0:T(8,128)} %constant.4.clone.turn_ref) | copy-start | bytes 24580
  6.8 31.7 %copy-start = (f32[3,3,256,256]{3,2,1,0:T(8,128)S(1)}, f32[3,3,256,256]{3,2,1,0:T(8,128)}, u32[]{:S(2)}) copy-start(f32[3,3,256,256]{3,2,1,0:T(8,128)} %taps_ref.7) | copy-start | bytes 7077892
  23.8 16.6 %copy-start.1 = (f32[256,1,128]{2,1,0:T(1,128)S(1)}, f32[256,1,128]{2,1,0:T(1,128)}, u32[]{:S(2)}) copy-start(f32[256,1,128]{2,1,0:T(1,128)} %param.6) | copy-start | bytes 393220
  23.8 16.6 %copy-start.2 = (f32[256,1,128]{2,1,0:T(1,128)S(1)}, f32[256,1,128]{2,1,0:T(1,128)}, u32[]{:S(2)}) copy-start(f32[256,1,128]{2,1,0:T(1,128)} %param.7) | copy-start | bytes 393220
  38.5 1.8 %collective-permute-start.2 = (f32[912,128]{1,0:T(8,128)S(1)}, f32[912,128]{1,0:T(8,128)S(1)}, u32[]{:S(2)}, u32[]{:S(2)}) collective-permute-start(f32[912,128]{1,0:T(8,128)S(1)} %bitcast.16), channel_id=1, source_target_pairs={{0,8},{8,0},{16,24},{24,16},{1,9},{9,1},{17,25},{25,17},{2,10},{10... | collective-permute-start | bytes 1400840 | tf_op jit(solution)/shard_map/ppermute | solution.py:584

commit v6 on v5

--- a/solution.py
+++ b/solution.py
@@ -168,7 +168,8 @@
 
 
 def rank(chip, place):
-    return 8 * (place % 2) + 4 * chip + 2 * (place // 2 % 2) + place // 4
+    upper, odd, x = place // 4, place // 2 % 2, place % 2
+    return 8 * ((upper + odd + 1) % 2) + 4 * (1 - chip) + 2 * (1 - x) + 1 - upper
 
 
 def reversed_bits(value, width):

time: 42 us -> 38.6 us (0.919)
  blocking collectives: 30.7 us -> 27.3 us
    all_to_all x2, blocking collectives: 30.7 us -> 27.3 us  [exchanged(): lax.all_to_all(flat.reshape(rows, 1, columns), ('lat', 'lon'), 0, 0, tile...]
where the time goes in v6:
time: 38.6 us; the launch traced here: 38.4 us
  blocking collectives  27.3 us (71%)
  Pallas kernels  8.05 us (21%)
  waiting for transfers between devices  1.71 us (4%)
  between operations  0.68 us (2%)
  starting transfers between devices  0.6 us (2%)
    all_to_all x2, blocking collectives, exchanged(): lax.all_to_all(flat.reshape(rows, 1, columns), ('lat', 'lon'), 0, 0, tile...  27.3 us
    pallas_call x1, Pallas kernels, on_device(): pl.pallas_call(conv_kernel, out_shape=forth, in_specs=[vmem] * 6 + [hbm],...  4.13 us
    pallas_call x1, Pallas kernels, on_device(): pl.pallas_call(last_kernel, out_shape=(flat, flat, jax.ShapeDtypeStruct(s...  1.39 us
    ppermute x1, waiting for transfers between devices, on_device(): other = lax.ppermute(mine, 'lat', swap)  1.25 us
    pallas_call x1, Pallas kernels, on_device(): pl.pallas_call(fetch_kernel, out_shape=(flat, flat, gain_half, half_taps)...  1 us
    pallas_call x1, Pallas kernels, on_device(): pl.pallas_call(spectral_kernel, out_shape=back, in_specs=[vmem] * 3, out_...  0.96 us
  transfers between devices with their start and end apart: 3, of which 3 were waited for; matrix products, arithmetic and copies ran while one was open for 0% of the time, Pallas kernels for 4%

profile of v6, /device:TPU:0, one launch (start us, length us, event | category | flops | bytes accessed | tf_op | source)
XLA Modules:
  0.0 38.4 jit_solution(15608069159478713463)
XLA Ops:
  0.6 0.5 %collective-permute-start = (f32[256,128]{1,0:T(8,128)}, f32[256,128]{1,0:T(8,128)S(1)}, u32[]{:S(2)}, u32[]{:S(2)}) collective-permute-start(f32[256,128]{1,0:T(8,128)} %bitcast.22), channel_id=1, source_target_pairs={{0,8},{8,0},{16,24},{24,16},{1,9},{9,1},{17,25},{25,17},{2,10},{10... | collective-permute-start | bytes 393224 | tf_op jit(solution)/shard_map/ppermute | solution.py:551
  1.1 0.1 collective-permute-start.1
  1.2 1.0 %fetch.1 = (f32[256,128]{1,0:T(8,128)S(1)}, f32[256,128]{1,0:T(8,128)S(1)}, f32[128,128]{1,0:T(8,128)S(1)}, f32[3,3,128,256]{3,2,1,0:T(8,128)S(1)}) custom-call(f32[256,128]{1,0:T(8,128)} %bitcast.23, f32[256,128]{1,0:T(8,128)} %bitcast.26, f32[2,256,128]{2,1,0:T(8,128)} %filter_ref.1, f32[3,3,256,256]{3,2,1,0:T(8,128)} %taps_ref.7), custom_call_target="tpu_custom_call" | custom-call | tf_op jit(solution)/shard_map/fetch/pallas_call | solution.py:553
  2.2 0.1 collective-permute-done.other_ref
  2.3 0.4 collective-permute-done.1.other_cot_ref
  2.7 0.0 copy-start.3
  2.7 0.0 copy-start.4
  2.7 4.1 %conv.1 = f32[784,128]{1,0:T(8,128)S(1)} custom-call(f32[256,128]{1,0:T(8,128)S(1)} %get-tuple-element.10.own_ref, f32[256,128]{1,0:T(8,128)S(1)} %collective-permute-done.other_ref, f32[256,128]{1,0:T(8,128)S(1)} %get-tuple-element.11.cot_ref, f32[256,128]{1,0:T(8,128)S(1)} %collective-permute-done.1.other_cot_ref, ...), custom_call_target="tpu_custom_call" | custom-call | tf_op jit(solution)/shard_map/conv/pallas_call | solution.py:562
  6.8 0.0 copy-start
  6.9 15.1 %all_to_all.10 = f32[784,1,128]{2,1,0:T(1,128)S(1)} all-to-all(f32[784,1,128]{2,1,0:T(1,128)S(1)} %bitcast.20), channel_id=1, replica_groups={{21,19,20,18,5,3,4,2,23,17,22,16,7,1,6,0},{29,27,28,26,13,11,12,10,31,2..., dimensions={0} | all-to-all | bytes 802816 | tf_op jit(solution)/shard_map/all_to_all | solution.py:522
  22.0 0.0 copy-done.3
  22.0 0.0 copy-done.4
  22.0 0.0 copy-start.1
  22.0 0.0 copy-start.2
  22.0 1.0 %spectral.1 = f32[912,128]{1,0:T(8,128)S(1)} custom-call(f32[784,128]{1,0:T(8,128)S(1)} %bitcast.21, f32[16,128]{1,0:T(8,128)S(1)} %copy-done.4, f32[256,256]{1,0:T(8,128)S(1)} %copy-done.3), custom_call_target="tpu_custom_call" | custom-call | tf_op jit(solution)/shard_map/spectral/pallas_call | solution.py:575
  22.9 12.2 %all_to_all.11 = f32[912,1,128]{2,1,0:T(1,128)S(1)} all-to-all(f32[912,1,128]{2,1,0:T(1,128)S(1)} %bitcast.19), channel_id=1, replica_groups={{21,19,20,18,5,3,4,2,23,17,22,16,7,1,6,0},{29,27,28,26,13,11,12,10,31,2..., dimensions={0} | all-to-all | bytes 933888 | tf_op jit(solution)/shard_map/all_to_all | solution.py:522
  35.1 0.0 collective-permute-start.2
  35.1 0.0 copy-done
  35.1 0.6 %adjoint.1.total_ref = f32[128,256]{1,0:T(8,128)S(1)} custom-call(f32[912,128]{1,0:T(8,128)S(1)} %bitcast.17, f32[3,3,256,256]{3,2,1,0:T(8,128)S(1)} %copy-done), custom_call_target="tpu_custom_call" | custom-call | tf_op jit(solution)/shard_map/adjoint/pallas_call | solution.py:587
  35.7 1.2 %collective-permute-done.2.other_ref = f32[912,128]{1,0:T(8,128)S(1)} collective-permute-done((f32[912,128]{1,0:T(8,128)S(1)}, f32[912,128]{1,0:T(8,128)S(1)}, u32[]{:S(2)}, u32[]{:S(2)}) %collective-permute-start.2) | collective-permute-done | bytes 466976 | tf_op jit(solution)/shard_map/ppermute | solution.py:585
  37.0 0.0 copy-done.1
  37.0 0.0 copy-done.2
  37.0 1.4 %last.1 = (f32[256,128]{1,0:T(8,128)}, f32[256,128]{1,0:T(8,128)}, f32[2,256,128]{2,1,0:T(8,128)}) custom-call(f32[912,128]{1,0:T(8,128)S(1)} %bitcast.18, f32[912,128]{1,0:T(8,128)S(1)} %collective-permute-done.2.other_ref, f32[256,128]{1,0:T(8,128)S(1)} %bitcast.24, f32[256,128]{1,0:T(8,128)S(1)} %bitcast.27, f32[3,3,256,256]{3,2,1,0:T(8,128)S(1)} %copy-done, ...), custom_call_target="tpu_custom_call" | custom-call | tf_op jit(solution)/shard_map/last/pallas_call | solution.py:596
Async XLA Ops:
  0.6 1.7 %collective-permute-start = (f32[256,128]{1,0:T(8,128)}, f32[256,128]{1,0:T(8,128)S(1)}, u32[]{:S(2)}, u32[]{:S(2)}) collective-permute-start(f32[256,128]{1,0:T(8,128)} %bitcast.22), channel_id=1, source_target_pairs={{0,8},{8,0},{16,24},{24,16},{1,9},{9,1},{17,25},{25,17},{2,10},{10... | collective-permute-start | bytes 393224 | tf_op jit(solution)/shard_map/ppermute | solution.py:551
  1.1 1.6 %collective-permute-start.1 = (f32[256,128]{1,0:T(8,128)}, f32[256,128]{1,0:T(8,128)S(1)}, u32[]{:S(2)}, u32[]{:S(2)}) collective-permute-start(f32[256,128]{1,0:T(8,128)} %bitcast.25), channel_id=1, source_target_pairs={{0,8},{8,0},{16,24},{24,16},{1,9},{9,1},{17,25},{25,17},{2,10},{10... | collective-permute-start | bytes 393224 | tf_op jit(solution)/shard_map/ppermute | solution.py:551
  2.7 19.3 %copy-start.3 = (f32[256,256]{1,0:T(8,128)S(1)}, f32[256,256]{1,0:T(8,128)}, u32[]{:S(2)}) copy-start(f32[256,256]{1,0:T(8,128)} %constant.5.clone.dft_ref) | copy-start | bytes 786436
  2.7 19.3 %copy-start.4 = (f32[16,128]{1,0:T(8,128)S(1)}, f32[16,128]{1,0:T(8,128)}, u32[]{:S(2)}) copy-start(f32[16,128]{1,0:T(8,128)} %constant.4.clone.turn_ref) | copy-start | bytes 24580
  6.8 28.3 %copy-start = (f32[3,3,256,256]{3,2,1,0:T(8,128)S(1)}, f32[3,3,256,256]{3,2,1,0:T(8,128)}, u32[]{:S(2)}) copy-start(f32[3,3,256,256]{3,2,1,0:T(8,128)} %taps_ref.7) | copy-start | bytes 7077892
  22.0 15.0 %copy-start.1 = (f32[256,1,128]{2,1,0:T(1,128)S(1)}, f32[256,1,128]{2,1,0:T(1,128)}, u32[]{:S(2)}) copy-start(f32[256,1,128]{2,1,0:T(1,128)} %param.6) | copy-start | bytes 393220
  22.0 15.0 %copy-start.2 = (f32[256,1,128]{2,1,0:T(1,128)S(1)}, f32[256,1,128]{2,1,0:T(1,128)}, u32[]{:S(2)}) copy-start(f32[256,1,128]{2,1,0:T(1,128)} %param.7) | copy-start | bytes 393220
  35.1 1.8 %collective-permute-start.2 = (f32[912,128]{1,0:T(8,128)S(1)}, f32[912,128]{1,0:T(8,128)S(1)}, u32[]{:S(2)}, u32[]{:S(2)}) collective-permute-start(f32[912,128]{1,0:T(8,128)S(1)} %bitcast.16), channel_id=1, source_target_pairs={{0,8},{8,0},{16,24},{24,16},{1,9},{9,1},{17,25},{25,17},{2,10},{10... | collective-permute-start | bytes 1400840 | tf_op jit(solution)/shard_map/ppermute | solution.py:585

commit v7 on v6

--- a/solution.py
+++ b/solution.py
@@ -164,12 +164,11 @@
 
 
 FORTH, BACK = 49, 57
-FIRST_COPIES, IN_FLIGHT = 5, 2
 
 
 def rank(chip, place):
     upper, odd, x = place // 4, place // 2 % 2, place % 2
-    return 8 * ((upper + odd + 1) % 2) + 4 * (1 - chip) + 2 * (1 - x) + 1 - upper
+    return 8 * ((upper + odd + 1) % 2) + 4 * (1 - x) + 2 * (1 - chip) + 1 - upper
 
 
 def reversed_bits(value, width):
@@ -237,13 +236,11 @@
             pltpu.make_async_copy(taps_ref.at[row, col, :half], taps.at[index], sems.at[index])
             for index, (row, col) in enumerate(order)
         ]
-        for copy in copies[:FIRST_COPIES]:
+        for copy in copies:
             copy.start()
 
         def weights(index):
             copies[index].wait()
-            if FIRST_COPIES <= index + IN_FLIGHT < len(copies):
-                copies[index + IN_FLIGHT].start()
             return high_low(taps[index])
 
         pack((own_ref, other_ref), (cot_ref, other_cot_ref), gain_ref, weights, 0, out_ref)

time: 38.6 us -> 38.3 us (level)
  Pallas kernels: 8.05 us -> 7.16 us
  blocking collectives: 27.3 us -> 27.9 us
    pallas_call x1, Pallas kernels: 4.13 us -> 3.23 us  [on_device(): pl.pallas_call(conv_kernel, out_shape=forth, in_specs=[vmem] * 6 + [hbm],...]
    all_to_all x2, blocking collectives: 27.3 us -> 27.9 us  [exchanged(): lax.all_to_all(flat.reshape(rows, 1, columns), ('lat', 'lon'), 0, 0, tile...]
where the time goes in v7:
time: 38.3 us; the launch traced here: 38 us
  blocking collectives  27.9 us (73%)
  Pallas kernels  7.16 us (19%)
  waiting for transfers between devices  1.72 us (4%)
  between operations  0.68 us (2%)
  starting transfers between devices  0.6 us (2%)
    all_to_all x2, blocking collectives, exchanged(): lax.all_to_all(flat.reshape(rows, 1, columns), ('lat', 'lon'), 0, 0, tile...  27.9 us
    pallas_call x1, Pallas kernels, on_device(): pl.pallas_call(conv_kernel, out_shape=forth, in_specs=[vmem] * 6 + [hbm],...  3.23 us
    pallas_call x1, Pallas kernels, on_device(): pl.pallas_call(last_kernel, out_shape=(flat, flat, jax.ShapeDtypeStruct(s...  1.4 us
    ppermute x1, waiting for transfers between devices, on_device(): other = lax.ppermute(mine, 'lat', swap)  1.25 us
    pallas_call x1, Pallas kernels, on_device(): pl.pallas_call(fetch_kernel, out_shape=(flat, flat, gain_half, half_taps)...  1 us
    pallas_call x1, Pallas kernels, on_device(): pl.pallas_call(spectral_kernel, out_shape=back, in_specs=[vmem] * 3, out_...  0.97 us
  transfers between devices with their start and end apart: 3, of which 3 were waited for; matrix products, arithmetic and copies ran while one was open for 0% of the time, Pallas kernels for 4%

profile of v7, /device:TPU:0, one launch (start us, length us, event | category | flops | bytes accessed | tf_op | source)
XLA Modules:
  0.0 38.0 jit_solution(9992144030326945629)
XLA Ops:
  0.6 0.5 %collective-permute-start = (f32[256,128]{1,0:T(8,128)}, f32[256,128]{1,0:T(8,128)S(1)}, u32[]{:S(2)}, u32[]{:S(2)}) collective-permute-start(f32[256,128]{1,0:T(8,128)} %bitcast.22), channel_id=1, source_target_pairs={{0,8},{8,0},{16,24},{24,16},{1,9},{9,1},{17,25},{25,17},{2,10},{10... | collective-permute-start | bytes 393224 | tf_op jit(solution)/shard_map/ppermute | solution.py:548
  1.1 0.1 collective-permute-start.1
  1.2 1.0 %fetch.1 = (f32[256,128]{1,0:T(8,128)S(1)}, f32[256,128]{1,0:T(8,128)S(1)}, f32[128,128]{1,0:T(8,128)S(1)}, f32[3,3,128,256]{3,2,1,0:T(8,128)S(1)}) custom-call(f32[256,128]{1,0:T(8,128)} %bitcast.23, f32[256,128]{1,0:T(8,128)} %bitcast.26, f32[2,256,128]{2,1,0:T(8,128)} %filter_ref.1, f32[3,3,256,256]{3,2,1,0:T(8,128)} %taps_ref.7), custom_call_target="tpu_custom_call" | custom-call | tf_op jit(solution)/shard_map/fetch/pallas_call | solution.py:550
  2.2 0.1 collective-permute-done.other_ref
  2.3 0.4 collective-permute-done.1.other_cot_ref
  2.7 0.0 copy-start.3
  2.7 0.0 copy-start.4
  2.7 3.2 %conv.1 = f32[784,128]{1,0:T(8,128)S(1)} custom-call(f32[256,128]{1,0:T(8,128)S(1)} %get-tuple-element.10.own_ref, f32[256,128]{1,0:T(8,128)S(1)} %collective-permute-done.other_ref, f32[256,128]{1,0:T(8,128)S(1)} %get-tuple-element.11.cot_ref, f32[256,128]{1,0:T(8,128)S(1)} %collective-permute-done.1.other_cot_ref, ...), custom_call_target="tpu_custom_call" | custom-call | tf_op jit(solution)/shard_map/conv/pallas_call | solution.py:559
  6.0 0.0 copy-start
  6.0 16.0 %all_to_all.10 = f32[784,1,128]{2,1,0:T(1,128)S(1)} all-to-all(f32[784,1,128]{2,1,0:T(1,128)S(1)} %bitcast.20), channel_id=1, replica_groups={{21,19,5,3,20,18,4,2,23,17,7,1,22,16,6,0},{29,27,13,11,28,26,12,10,31,2..., dimensions={0} | all-to-all | bytes 802816 | tf_op jit(solution)/shard_map/all_to_all | solution.py:519
  22.0 0.0 copy-done.3
  22.0 0.0 copy-done.4
  22.0 0.0 copy-start.1
  22.0 0.0 copy-start.2
  22.0 1.0 %spectral.1 = f32[912,128]{1,0:T(8,128)S(1)} custom-call(f32[784,128]{1,0:T(8,128)S(1)} %bitcast.21, f32[16,128]{1,0:T(8,128)S(1)} %copy-done.4, f32[256,256]{1,0:T(8,128)S(1)} %copy-done.3), custom_call_target="tpu_custom_call" | custom-call | tf_op jit(solution)/shard_map/spectral/pallas_call | solution.py:572
  22.9 11.9 %all_to_all.11 = f32[912,1,128]{2,1,0:T(1,128)S(1)} all-to-all(f32[912,1,128]{2,1,0:T(1,128)S(1)} %bitcast.19), channel_id=1, replica_groups={{21,19,5,3,20,18,4,2,23,17,7,1,22,16,6,0},{29,27,13,11,28,26,12,10,31,2..., dimensions={0} | all-to-all | bytes 933888 | tf_op jit(solution)/shard_map/all_to_all | solution.py:519
  34.8 0.0 collective-permute-start.2
  34.8 0.0 copy-done
  34.8 0.6 %adjoint.1.total_ref = f32[128,256]{1,0:T(8,128)S(1)} custom-call(f32[912,128]{1,0:T(8,128)S(1)} %bitcast.17, f32[3,3,256,256]{3,2,1,0:T(8,128)S(1)} %copy-done), custom_call_target="tpu_custom_call" | custom-call | tf_op jit(solution)/shard_map/adjoint/pallas_call | solution.py:584
  35.4 1.3 %collective-permute-done.2.other_ref = f32[912,128]{1,0:T(8,128)S(1)} collective-permute-done((f32[912,128]{1,0:T(8,128)S(1)}, f32[912,128]{1,0:T(8,128)S(1)}, u32[]{:S(2)}, u32[]{:S(2)}) %collective-permute-start.2) | collective-permute-done | bytes 466976 | tf_op jit(solution)/shard_map/ppermute | solution.py:582
  36.6 0.0 copy-done.1
  36.6 0.0 copy-done.2
  36.6 1.4 %last.1 = (f32[256,128]{1,0:T(8,128)}, f32[256,128]{1,0:T(8,128)}, f32[2,256,128]{2,1,0:T(8,128)}) custom-call(f32[912,128]{1,0:T(8,128)S(1)} %bitcast.18, f32[912,128]{1,0:T(8,128)S(1)} %collective-permute-done.2.other_ref, f32[256,128]{1,0:T(8,128)S(1)} %bitcast.24, f32[256,128]{1,0:T(8,128)S(1)} %bitcast.27, f32[3,3,256,256]{3,2,1,0:T(8,128)S(1)} %copy-done, ...), custom_call_target="tpu_custom_call" | custom-call | tf_op jit(solution)/shard_map/last/pallas_call | solution.py:593
Async XLA Ops:
  0.6 1.7 %collective-permute-start = (f32[256,128]{1,0:T(8,128)}, f32[256,128]{1,0:T(8,128)S(1)}, u32[]{:S(2)}, u32[]{:S(2)}) collective-permute-start(f32[256,128]{1,0:T(8,128)} %bitcast.22), channel_id=1, source_target_pairs={{0,8},{8,0},{16,24},{24,16},{1,9},{9,1},{17,25},{25,17},{2,10},{10... | collective-permute-start | bytes 393224 | tf_op jit(solution)/shard_map/ppermute | solution.py:548
  1.1 1.6 %collective-permute-start.1 = (f32[256,128]{1,0:T(8,128)}, f32[256,128]{1,0:T(8,128)S(1)}, u32[]{:S(2)}, u32[]{:S(2)}) collective-permute-start(f32[256,128]{1,0:T(8,128)} %bitcast.25), channel_id=1, source_target_pairs={{0,8},{8,0},{16,24},{24,16},{1,9},{9,1},{17,25},{25,17},{2,10},{10... | collective-permute-start | bytes 393224 | tf_op jit(solution)/shard_map/ppermute | solution.py:548
  2.7 19.3 %copy-start.3 = (f32[256,256]{1,0:T(8,128)S(1)}, f32[256,256]{1,0:T(8,128)}, u32[]{:S(2)}) copy-start(f32[256,256]{1,0:T(8,128)} %constant.5.clone.dft_ref) | copy-start | bytes 786436
  2.7 19.3 %copy-start.4 = (f32[16,128]{1,0:T(8,128)S(1)}, f32[16,128]{1,0:T(8,128)}, u32[]{:S(2)}) copy-start(f32[16,128]{1,0:T(8,128)} %constant.4.clone.turn_ref) | copy-start | bytes 24580
  6.0 28.9 %copy-start = (f32[3,3,256,256]{3,2,1,0:T(8,128)S(1)}, f32[3,3,256,256]{3,2,1,0:T(8,128)}, u32[]{:S(2)}) copy-start(f32[3,3,256,256]{3,2,1,0:T(8,128)} %taps_ref.7) | copy-start | bytes 7077892
  22.0 14.7 %copy-start.1 = (f32[256,1,128]{2,1,0:T(1,128)S(1)}, f32[256,1,128]{2,1,0:T(1,128)}, u32[]{:S(2)}) copy-start(f32[256,1,128]{2,1,0:T(1,128)} %param.6) | copy-start | bytes 393220
  22.0 14.7 %copy-start.2 = (f32[256,1,128]{2,1,0:T(1,128)S(1)}, f32[256,1,128]{2,1,0:T(1,128)}, u32[]{:S(2)}) copy-start(f32[256,1,128]{2,1,0:T(1,128)} %param.7) | copy-start | bytes 393220
  34.8 1.8 %collective-permute-start.2 = (f32[912,128]{1,0:T(8,128)S(1)}, f32[912,128]{1,0:T(8,128)S(1)}, u32[]{:S(2)}, u32[]{:S(2)}) collective-permute-start(f32[912,128]{1,0:T(8,128)S(1)} %bitcast.16), channel_id=1, source_target_pairs={{0,8},{8,0},{16,24},{24,16},{1,9},{9,1},{17,25},{25,17},{2,10},{10... | collective-permute-start | bytes 1400840 | tf_op jit(solution)/shard_map/ppermute | solution.py:582

commit v8 on v7

--- a/solution.py
+++ b/solution.py
@@ -256,11 +256,6 @@
 def pack(fields, cots, gain_ref, weights, core, out_ref):
     upper = lax.axis_index("lat") // 2
     half, columns = gain_ref.shape
-    for owner in range(half // 8):
-        first, here = FORTH * owner, half * core + 8 * owner
-        out_ref[first : first + 8, :] = cots[0][here : here + 8, :]
-        out_ref[first + 8 : first + 16, :] = cots[1][here : here + 8, :]
-        out_ref[first + 40 : first + 48, :] = gain_ref[8 * owner : 8 * owner + 8, :]
     row_0, row_1 = fields[0][...], fields[1][...]
     near = jnp.concatenate(high_low(jnp.where(upper == 0, row_1, row_0)), axis=1)
     both_high, both_low = high_low(jnp.concatenate([row_0, row_1], axis=1))
@@ -307,6 +302,11 @@
         out_ref[first + 48 : first + 49, :] = jnp.sum(
             edges[8 * owner : 8 * owner + 8], axis=0, keepdims=True
         )
+    for owner in range(half // 8):
+        first, here = FORTH * owner, half * core + 8 * owner
+        out_ref[first : first + 8, :] = cots[0][here : here + 8, :]
+        out_ref[first + 8 : first + 16, :] = cots[1][here : here + 8, :]
+        out_ref[first + 40 : first + 48, :] = gain_ref[8 * owner : 8 * owner + 8, :]
 
 
 def transform_8(x):
@@ -348,9 +348,9 @@
             tile = message(row // 2, place, 16 + 8 * (row % 2), 8)
             if row in (1, 2):
                 tile = tile + message(1 - row // 2, place, 32, 8)
-            tile = tile + jnp.where(lane == 0, edge(row, (place - 1) % lon, 0), 0.0)
-            tile = tile + jnp.where(lane == columns - 1, edge(row, (place + 1) % lon, 1), 0.0)
-            mixed.append(tile)
+            left, right = edge(row, (place - 1) % lon, 0), edge(row, (place + 1) % lon, 1)
+            outer = jnp.where(lane == columns - 1, right, 0.0)
+            mixed.append(tile + jnp.where(lane == 0, left, outer))
         cot = [message(row // 2, place, 8 * (row % 2), 8) for row in range(rows)]
         grid.append(jnp.concatenate(mixed + cot, axis=0))
     pairs = transform_8(grid)

time: 38.3 us -> 38.3 us (level)
  no operation moved by 1% of the time
where the time goes in v8:
time: 38.3 us; the launch traced here: 38 us
  blocking collectives  27.8 us (73%)
  Pallas kernels  7.17 us (19%)
  waiting for transfers between devices  1.71 us (4%)
  between operations  0.68 us (2%)
  starting transfers between devices  0.6 us (2%)
    all_to_all x2, blocking collectives, exchanged(): lax.all_to_all(flat.reshape(rows, 1, columns), ('lat', 'lon'), 0, 0, tile...  27.8 us
    pallas_call x1, Pallas kernels, on_device(): pl.pallas_call(conv_kernel, out_shape=forth, in_specs=[vmem] * 6 + [hbm],...  3.24 us
    pallas_call x1, Pallas kernels, on_device(): pl.pallas_call(last_kernel, out_shape=(flat, flat, jax.ShapeDtypeStruct(s...  1.39 us
    ppermute x1, waiting for transfers between devices, on_device(): other = lax.ppermute(mine, 'lat', swap)  1.25 us
    pallas_call x1, Pallas kernels, on_device(): pl.pallas_call(fetch_kernel, out_shape=(flat, flat, gain_half, half_taps)...  1 us
    pallas_call x1, Pallas kernels, on_device(): pl.pallas_call(spectral_kernel, out_shape=back, in_specs=[vmem] * 3, out_...  0.96 us
  transfers between devices with their start and end apart: 3, of which 3 were waited for; matrix products, arithmetic and copies ran while one was open for 0% of the time, Pallas kernels for 4%

profile of v8, /device:TPU:0, one launch (start us, length us, event | category | flops | bytes accessed | tf_op | source)
XLA Modules:
  0.0 38.0 jit_solution(7565149541867706443)
XLA Ops:
  0.6 0.5 %collective-permute-start = (f32[256,128]{1,0:T(8,128)}, f32[256,128]{1,0:T(8,128)S(1)}, u32[]{:S(2)}, u32[]{:S(2)}) collective-permute-start(f32[256,128]{1,0:T(8,128)} %bitcast.22), channel_id=1, source_target_pairs={{0,8},{8,0},{16,24},{24,16},{1,9},{9,1},{17,25},{25,17},{2,10},{10... | collective-permute-start | bytes 393224 | tf_op jit(solution)/shard_map/ppermute | solution.py:548
  1.1 0.1 collective-permute-start.1
  1.2 1.0 %fetch.1 = (f32[256,128]{1,0:T(8,128)S(1)}, f32[256,128]{1,0:T(8,128)S(1)}, f32[128,128]{1,0:T(8,128)S(1)}, f32[3,3,128,256]{3,2,1,0:T(8,128)S(1)}) custom-call(f32[256,128]{1,0:T(8,128)} %bitcast.23, f32[256,128]{1,0:T(8,128)} %bitcast.26, f32[2,256,128]{2,1,0:T(8,128)} %filter_ref.1, f32[3,3,256,256]{3,2,1,0:T(8,128)} %taps_ref.7), custom_call_target="tpu_custom_call" | custom-call | tf_op jit(solution)/shard_map/fetch/pallas_call | solution.py:550
  2.2 0.1 collective-permute-done.other_ref
  2.3 0.4 collective-permute-done.1.other_cot_ref
  2.7 0.0 copy-start.3
  2.7 0.0 copy-start.4
  2.7 3.2 %conv.1 = f32[784,128]{1,0:T(8,128)S(1)} custom-call(f32[256,128]{1,0:T(8,128)S(1)} %get-tuple-element.10.own_ref, f32[256,128]{1,0:T(8,128)S(1)} %collective-permute-done.other_ref, f32[256,128]{1,0:T(8,128)S(1)} %get-tuple-element.11.cot_ref, f32[256,128]{1,0:T(8,128)S(1)} %collective-permute-done.1.other_cot_ref, ...), custom_call_target="tpu_custom_call" | custom-call | tf_op jit(solution)/shard_map/conv/pallas_call | solution.py:559
  6.0 0.0 copy-start
  6.0 16.0 %all_to_all.10 = f32[784,1,128]{2,1,0:T(1,128)S(1)} all-to-all(f32[784,1,128]{2,1,0:T(1,128)S(1)} %bitcast.20), channel_id=1, replica_groups={{21,19,5,3,20,18,4,2,23,17,7,1,22,16,6,0},{29,27,13,11,28,26,12,10,31,2..., dimensions={0} | all-to-all | bytes 802816 | tf_op jit(solution)/shard_map/all_to_all | solution.py:519
  21.9 0.0 copy-done.3
  21.9 0.0 copy-done.4
  21.9 0.0 copy-start.1
  22.0 0.0 copy-start.2
  22.0 1.0 %spectral.1 = f32[912,128]{1,0:T(8,128)S(1)} custom-call(f32[784,128]{1,0:T(8,128)S(1)} %bitcast.21, f32[16,128]{1,0:T(8,128)S(1)} %copy-done.4, f32[256,256]{1,0:T(8,128)S(1)} %copy-done.3), custom_call_target="tpu_custom_call" | custom-call | tf_op jit(solution)/shard_map/spectral/pallas_call | solution.py:572
  22.9 11.9 %all_to_all.11 = f32[912,1,128]{2,1,0:T(1,128)S(1)} all-to-all(f32[912,1,128]{2,1,0:T(1,128)S(1)} %bitcast.19), channel_id=1, replica_groups={{21,19,5,3,20,18,4,2,23,17,7,1,22,16,6,0},{29,27,13,11,28,26,12,10,31,2..., dimensions={0} | all-to-all | bytes 933888 | tf_op jit(solution)/shard_map/all_to_all | solution.py:519
  34.8 0.0 collective-permute-start.2
  34.8 0.0 copy-done
  34.8 0.6 %adjoint.1.total_ref = f32[128,256]{1,0:T(8,128)S(1)} custom-call(f32[912,128]{1,0:T(8,128)S(1)} %bitcast.17, f32[3,3,256,256]{3,2,1,0:T(8,128)S(1)} %copy-done), custom_call_target="tpu_custom_call" | custom-call | tf_op jit(solution)/shard_map/adjoint/pallas_call | solution.py:584
  35.4 1.2 %collective-permute-done.2.other_ref = f32[912,128]{1,0:T(8,128)S(1)} collective-permute-done((f32[912,128]{1,0:T(8,128)S(1)}, f32[912,128]{1,0:T(8,128)S(1)}, u32[]{:S(2)}, u32[]{:S(2)}) %collective-permute-start.2) | collective-permute-done | bytes 466976 | tf_op jit(solution)/shard_map/ppermute | solution.py:582
  36.6 0.0 copy-done.1
  36.6 0.0 copy-done.2
  36.6 1.4 %last.1 = (f32[256,128]{1,0:T(8,128)}, f32[256,128]{1,0:T(8,128)}, f32[2,256,128]{2,1,0:T(8,128)}) custom-call(f32[912,128]{1,0:T(8,128)S(1)} %bitcast.18, f32[912,128]{1,0:T(8,128)S(1)} %collective-permute-done.2.other_ref, f32[256,128]{1,0:T(8,128)S(1)} %bitcast.24, f32[256,128]{1,0:T(8,128)S(1)} %bitcast.27, f32[3,3,256,256]{3,2,1,0:T(8,128)S(1)} %copy-done, ...), custom_call_target="tpu_custom_call" | custom-call | tf_op jit(solution)/shard_map/last/pallas_call | solution.py:593
Async XLA Ops:
  0.6 1.7 %collective-permute-start = (f32[256,128]{1,0:T(8,128)}, f32[256,128]{1,0:T(8,128)S(1)}, u32[]{:S(2)}, u32[]{:S(2)}) collective-permute-start(f32[256,128]{1,0:T(8,128)} %bitcast.22), channel_id=1, source_target_pairs={{0,8},{8,0},{16,24},{24,16},{1,9},{9,1},{17,25},{25,17},{2,10},{10... | collective-permute-start | bytes 393224 | tf_op jit(solution)/shard_map/ppermute | solution.py:548
  1.1 1.6 %collective-permute-start.1 = (f32[256,128]{1,0:T(8,128)}, f32[256,128]{1,0:T(8,128)S(1)}, u32[]{:S(2)}, u32[]{:S(2)}) collective-permute-start(f32[256,128]{1,0:T(8,128)} %bitcast.25), channel_id=1, source_target_pairs={{0,8},{8,0},{16,24},{24,16},{1,9},{9,1},{17,25},{25,17},{2,10},{10... | collective-permute-start | bytes 393224 | tf_op jit(solution)/shard_map/ppermute | solution.py:548
  2.7 19.2 %copy-start.3 = (f32[256,256]{1,0:T(8,128)S(1)}, f32[256,256]{1,0:T(8,128)}, u32[]{:S(2)}) copy-start(f32[256,256]{1,0:T(8,128)} %constant.5.clone.dft_ref) | copy-start | bytes 786436
  2.7 19.2 %copy-start.4 = (f32[16,128]{1,0:T(8,128)S(1)}, f32[16,128]{1,0:T(8,128)}, u32[]{:S(2)}) copy-start(f32[16,128]{1,0:T(8,128)} %constant.4.clone.turn_ref) | copy-start | bytes 24580
  6.0 28.8 %copy-start = (f32[3,3,256,256]{3,2,1,0:T(8,128)S(1)}, f32[3,3,256,256]{3,2,1,0:T(8,128)}, u32[]{:S(2)}) copy-start(f32[3,3,256,256]{3,2,1,0:T(8,128)} %taps_ref.7) | copy-start | bytes 7077892
  21.9 14.7 %copy-start.1 = (f32[256,1,128]{2,1,0:T(1,128)S(1)}, f32[256,1,128]{2,1,0:T(1,128)}, u32[]{:S(2)}) copy-start(f32[256,1,128]{2,1,0:T(1,128)} %param.6) | copy-start | bytes 393220
  22.0 14.7 %copy-start.2 = (f32[256,1,128]{2,1,0:T(1,128)S(1)}, f32[256,1,128]{2,1,0:T(1,128)}, u32[]{:S(2)}) copy-start(f32[256,1,128]{2,1,0:T(1,128)} %param.7) | copy-start | bytes 393220
  34.8 1.8 %collective-permute-start.2 = (f32[912,128]{1,0:T(8,128)S(1)}, f32[912,128]{1,0:T(8,128)S(1)}, u32[]{:S(2)}, u32[]{:S(2)}) collective-permute-start(f32[912,128]{1,0:T(8,128)S(1)} %bitcast.16), channel_id=1, source_target_pairs={{0,8},{8,0},{16,24},{24,16},{1,9},{9,1},{17,25},{25,17},{2,10},{10... | collective-permute-start | bytes 1400840 | tf_op jit(solution)/shard_map/ppermute | solution.py:582

commit v9 on v7

--- a/solution.py
+++ b/solution.py
@@ -195,10 +195,13 @@
 
     @pl.when(odd == 1)
     def _():
-        half_taps = pltpu.make_async_copy(taps_ref.at[:, :, half:], taps_out, sems.at[3])
-        for copy in [half_taps] + copies:
+        all_taps = [
+            pltpu.make_async_copy(taps_ref.at[row, :, half:], taps_out.at[row], sems.at[3 + row])
+            for row in range(3)
+        ]
+        for copy in all_taps + copies:
             copy.start()
-        for copy in [half_taps] + copies:
+        for copy in copies + all_taps:
             copy.wait()
 
     @pl.when(odd == 0)
@@ -471,11 +474,9 @@
             first = 9 - tap_col
             windows.append(rows_ref[index + 2 - tap_row, first : first + columns, :])
             weights.append(taps_ref[tap_row, tap_col, span])
-    total = 0.0
-    for pair in range(0, 9, 2):
-        window = jnp.concatenate(windows[pair : pair + 2], axis=1)
-        weight = jnp.concatenate(weights[pair : pair + 2], axis=0)
-        total = total + tall_product(window, *high_low(weight))
+    window = jnp.concatenate(windows, axis=1)
+    weight = jnp.concatenate(weights, axis=0)
+    total = tall_product(window, *high_low(weight))
     return total
 
 
@@ -552,7 +553,7 @@
         out_shape=(flat, flat, gain_half, half_taps),
         in_specs=[hbm] * 4,
         out_specs=(vmem,) * 4,
-        scratch_shapes=[pltpu.SemaphoreType.DMA((4,))],
+        scratch_shapes=[pltpu.SemaphoreType.DMA((6,))],
         compiler_params=params,
         name="fetch",
     )(*map(in_hbm, (own, cot, spectral_filter, conv_weight)))

time: 38.3 us -> 38.3 us (level)
  no operation moved by 1% of the time
where the time goes in v9:
time: 38.3 us; the launch traced here: 38 us
  blocking collectives  27.9 us (73%)
  Pallas kernels  7.19 us (19%)
  waiting for transfers between devices  1.69 us (4%)
  between operations  0.68 us (2%)
  starting transfers between devices  0.6 us (2%)
    all_to_all x2, blocking collectives, exchanged(): lax.all_to_all(flat.reshape(rows, 1, columns), ('lat', 'lon'), 0, 0, tile...  27.9 us
    pallas_call x1, Pallas kernels, on_device(): pl.pallas_call(conv_kernel, out_shape=forth, in_specs=[vmem] * 6 + [hbm],...  3.23 us
    pallas_call x1, Pallas kernels, on_device(): pl.pallas_call(last_kernel, out_shape=(flat, flat, jax.ShapeDtypeStruct(s...  1.39 us
    ppermute x1, waiting for transfers between devices, on_device(): other = lax.ppermute(mine, 'lat', swap)  1.24 us
    pallas_call x1, Pallas kernels, on_device(): pl.pallas_call(fetch_kernel, out_shape=(flat, flat, gain_half, half_taps)...  1.02 us
    pallas_call x1, Pallas kernels, on_device(): pl.pallas_call(spectral_kernel, out_shape=back, in_specs=[vmem] * 3, out_...  0.97 us
  transfers between devices with their start and end apart: 3, of which 3 were waited for; matrix products, arithmetic and copies ran while one was open for 0% of the time, Pallas kernels for 4%

profile of v9, /device:TPU:0, one launch (start us, length us, event | category | flops | bytes accessed | tf_op | source)
XLA Modules:
  0.0 38.0 jit_solution(3541277372037782429)
XLA Ops:
  0.6 0.5 %collective-permute-start = (f32[256,128]{1,0:T(8,128)}, f32[256,128]{1,0:T(8,128)S(1)}, u32[]{:S(2)}, u32[]{:S(2)}) collective-permute-start(f32[256,128]{1,0:T(8,128)} %bitcast.22), channel_id=1, source_target_pairs={{0,8},{8,0},{16,24},{24,16},{1,9},{9,1},{17,25},{25,17},{2,10},{10... | collective-permute-start | bytes 393224 | tf_op jit(solution)/shard_map/ppermute | solution.py:549
  1.1 0.1 collective-permute-start.1
  1.2 1.0 %fetch.1 = (f32[256,128]{1,0:T(8,128)S(1)}, f32[256,128]{1,0:T(8,128)S(1)}, f32[128,128]{1,0:T(8,128)S(1)}, f32[3,3,128,256]{3,2,1,0:T(8,128)S(1)}) custom-call(f32[256,128]{1,0:T(8,128)} %bitcast.23, f32[256,128]{1,0:T(8,128)} %bitcast.26, f32[2,256,128]{2,1,0:T(8,128)} %filter_ref.1, f32[3,3,256,256]{3,2,1,0:T(8,128)} %taps_ref.7), custom_call_target="tpu_custom_call" | custom-call | tf_op jit(solution)/shard_map/fetch/pallas_call | solution.py:551
  2.3 0.1 collective-permute-done.other_ref
  2.3 0.4 collective-permute-done.1.other_cot_ref
  2.7 0.0 copy-start.3
  2.7 0.0 copy-start.4
  2.7 3.2 %conv.1 = f32[784,128]{1,0:T(8,128)S(1)} custom-call(f32[256,128]{1,0:T(8,128)S(1)} %get-tuple-element.10.own_ref, f32[256,128]{1,0:T(8,128)S(1)} %collective-permute-done.other_ref, f32[256,128]{1,0:T(8,128)S(1)} %get-tuple-element.11.cot_ref, f32[256,128]{1,0:T(8,128)S(1)} %collective-permute-done.1.other_cot_ref, ...), custom_call_target="tpu_custom_call" | custom-call | tf_op jit(solution)/shard_map/conv/pallas_call | solution.py:560
  6.0 0.0 copy-start
  6.0 16.0 %all_to_all.10 = f32[784,1,128]{2,1,0:T(1,128)S(1)} all-to-all(f32[784,1,128]{2,1,0:T(1,128)S(1)} %bitcast.20), channel_id=1, replica_groups={{21,19,5,3,20,18,4,2,23,17,7,1,22,16,6,0},{29,27,13,11,28,26,12,10,31,2..., dimensions={0} | all-to-all | bytes 802816 | tf_op jit(solution)/shard_map/all_to_all | solution.py:520
  22.0 0.0 copy-done.3
  22.0 0.0 copy-done.4
  22.0 0.0 copy-start.1
  22.0 0.0 copy-start.2
  22.0 1.0 %spectral.1 = f32[912,128]{1,0:T(8,128)S(1)} custom-call(f32[784,128]{1,0:T(8,128)S(1)} %bitcast.21, f32[16,128]{1,0:T(8,128)S(1)} %copy-done.4, f32[256,256]{1,0:T(8,128)S(1)} %copy-done.3), custom_call_target="tpu_custom_call" | custom-call | tf_op jit(solution)/shard_map/spectral/pallas_call | solution.py:573
  22.9 11.9 %all_to_all.11 = f32[912,1,128]{2,1,0:T(1,128)S(1)} all-to-all(f32[912,1,128]{2,1,0:T(1,128)S(1)} %bitcast.19), channel_id=1, replica_groups={{21,19,5,3,20,18,4,2,23,17,7,1,22,16,6,0},{29,27,13,11,28,26,12,10,31,2..., dimensions={0} | all-to-all | bytes 933888 | tf_op jit(solution)/shard_map/all_to_all | solution.py:520
  34.8 0.0 collective-permute-start.2
  34.8 0.0 copy-done
  34.8 0.6 %adjoint.1.total_ref = f32[128,256]{1,0:T(8,128)S(1)} custom-call(f32[912,128]{1,0:T(8,128)S(1)} %bitcast.17, f32[3,3,256,256]{3,2,1,0:T(8,128)S(1)} %copy-done), custom_call_target="tpu_custom_call" | custom-call | tf_op jit(solution)/shard_map/adjoint/pallas_call | solution.py:585
  35.4 1.2 %collective-permute-done.2.other_ref = f32[912,128]{1,0:T(8,128)S(1)} collective-permute-done((f32[912,128]{1,0:T(8,128)S(1)}, f32[912,128]{1,0:T(8,128)S(1)}, u32[]{:S(2)}, u32[]{:S(2)}) %collective-permute-start.2) | collective-permute-done | bytes 466976 | tf_op jit(solution)/shard_map/ppermute | solution.py:583
  36.6 0.0 copy-done.1
  36.6 0.0 copy-done.2
  36.6 1.4 %last.1 = (f32[256,128]{1,0:T(8,128)}, f32[256,128]{1,0:T(8,128)}, f32[2,256,128]{2,1,0:T(8,128)}) custom-call(f32[912,128]{1,0:T(8,128)S(1)} %bitcast.18, f32[912,128]{1,0:T(8,128)S(1)} %collective-permute-done.2.other_ref, f32[256,128]{1,0:T(8,128)S(1)} %bitcast.24, f32[256,128]{1,0:T(8,128)S(1)} %bitcast.27, f32[3,3,256,256]{3,2,1,0:T(8,128)S(1)} %copy-done, ...), custom_call_target="tpu_custom_call" | custom-call | tf_op jit(solution)/shard_map/last/pallas_call | solution.py:594
Async XLA Ops:
  0.6 1.7 %collective-permute-start = (f32[256,128]{1,0:T(8,128)}, f32[256,128]{1,0:T(8,128)S(1)}, u32[]{:S(2)}, u32[]{:S(2)}) collective-permute-start(f32[256,128]{1,0:T(8,128)} %bitcast.22), channel_id=1, source_target_pairs={{0,8},{8,0},{16,24},{24,16},{1,9},{9,1},{17,25},{25,17},{2,10},{10... | collective-permute-start | bytes 393224 | tf_op jit(solution)/shard_map/ppermute | solution.py:549
  1.1 1.6 %collective-permute-start.1 = (f32[256,128]{1,0:T(8,128)}, f32[256,128]{1,0:T(8,128)S(1)}, u32[]{:S(2)}, u32[]{:S(2)}) collective-permute-start(f32[256,128]{1,0:T(8,128)} %bitcast.25), channel_id=1, source_target_pairs={{0,8},{8,0},{16,24},{24,16},{1,9},{9,1},{17,25},{25,17},{2,10},{10... | collective-permute-start | bytes 393224 | tf_op jit(solution)/shard_map/ppermute | solution.py:549
  2.7 19.3 %copy-start.3 = (f32[256,256]{1,0:T(8,128)S(1)}, f32[256,256]{1,0:T(8,128)}, u32[]{:S(2)}) copy-start(f32[256,256]{1,0:T(8,128)} %constant.5.clone.dft_ref) | copy-start | bytes 786436
  2.7 19.3 %copy-start.4 = (f32[16,128]{1,0:T(8,128)S(1)}, f32[16,128]{1,0:T(8,128)}, u32[]{:S(2)}) copy-start(f32[16,128]{1,0:T(8,128)} %constant.4.clone.turn_ref) | copy-start | bytes 24580
  6.0 28.9 %copy-start = (f32[3,3,256,256]{3,2,1,0:T(8,128)S(1)}, f32[3,3,256,256]{3,2,1,0:T(8,128)}, u32[]{:S(2)}) copy-start(f32[3,3,256,256]{3,2,1,0:T(8,128)} %taps_ref.7) | copy-start | bytes 7077892
  22.0 14.7 %copy-start.1 = (f32[256,1,128]{2,1,0:T(1,128)S(1)}, f32[256,1,128]{2,1,0:T(1,128)}, u32[]{:S(2)}) copy-start(f32[256,1,128]{2,1,0:T(1,128)} %param.6) | copy-start | bytes 393220
  22.0 14.7 %copy-start.2 = (f32[256,1,128]{2,1,0:T(1,128)S(1)}, f32[256,1,128]{2,1,0:T(1,128)}, u32[]{:S(2)}) copy-start(f32[256,1,128]{2,1,0:T(1,128)} %param.7) | copy-start | bytes 393220
  34.8 1.8 %collective-permute-start.2 = (f32[912,128]{1,0:T(8,128)S(1)}, f32[912,128]{1,0:T(8,128)S(1)}, u32[]{:S(2)}, u32[]{:S(2)}) collective-permute-start(f32[912,128]{1,0:T(8,128)S(1)} %bitcast.16), channel_id=1, source_target_pairs={{0,8},{8,0},{16,24},{24,16},{1,9},{9,1},{17,25},{25,17},{2,10},{10... | collective-permute-start | bytes 1400840 | tf_op jit(solution)/shard_map/ppermute | solution.py:583

commit v10 on v7

--- a/solution.py
+++ b/solution.py
@@ -369,9 +369,9 @@
         work[span, columns:] = turned[1]
     chunk = lon * height // 4
     pieces = [pl.ds(first, chunk) for first in range(0, lon * height, chunk)]
-    table = high_low(dft_ref[...])
+    table = dft_ref[...]
     spectra = jnp.concatenate(
-        [tall_product(work[piece], *table) for piece in pieces], axis=0
+        [jnp.dot(work[piece], table, precision=three_pass) for piece in pieces], axis=0
     )
     scale = 1.0 / (lon * columns)
     half = 8 * rows
@@ -398,7 +398,7 @@
             ]
         )
     back = jnp.concatenate(
-        [tall_product(work[piece], *table) for piece in pieces], axis=0
+        [jnp.dot(work[piece], table, precision=three_pass) for piece in pieces], axis=0
     )
     turned = []
     for residue in range(lon):

time: 38.3 us -> 38.3 us (level)
  no operation moved by 1% of the time
where the time goes in v10:
time: 38.3 us; the launch traced here: 38 us
  blocking collectives  27.9 us (73%)
  Pallas kernels  7.15 us (19%)
  waiting for transfers between devices  1.72 us (4%)
  between operations  0.68 us (2%)
  starting transfers between devices  0.6 us (2%)
    all_to_all x2, blocking collectives, exchanged(): lax.all_to_all(flat.reshape(rows, 1, columns), ('lat', 'lon'), 0, 0, tile...  27.9 us
    pallas_call x1, Pallas kernels, on_device(): pl.pallas_call(conv_kernel, out_shape=forth, in_specs=[vmem] * 6 + [hbm],...  3.23 us
    pallas_call x1, Pallas kernels, on_device(): pl.pallas_call(last_kernel, out_shape=(flat, flat, jax.ShapeDtypeStruct(s...  1.4 us
    ppermute x1, waiting for transfers between devices, on_device(): other = lax.ppermute(mine, 'lat', swap)  1.25 us
    pallas_call x1, Pallas kernels, on_device(): pl.pallas_call(fetch_kernel, out_shape=(flat, flat, gain_half, half_taps)...  1 us
    pallas_call x1, Pallas kernels, on_device(): pl.pallas_call(spectral_kernel, out_shape=back, in_specs=[vmem] * 3, out_...  0.95 us
  transfers between devices with their start and end apart: 3, of which 3 were waited for; matrix products, arithmetic and copies ran while one was open for 0% of the time, Pallas kernels for 4%

profile of v10, /device:TPU:0, one launch (start us, length us, event | category | flops | bytes accessed | tf_op | source)
XLA Modules:
  0.0 38.0 jit_solution(1351610003444956367)
XLA Ops:
  0.6 0.5 %collective-permute-start = (f32[256,128]{1,0:T(8,128)}, f32[256,128]{1,0:T(8,128)S(1)}, u32[]{:S(2)}, u32[]{:S(2)}) collective-permute-start(f32[256,128]{1,0:T(8,128)} %bitcast.22), channel_id=1, source_target_pairs={{0,8},{8,0},{16,24},{24,16},{1,9},{9,1},{17,25},{25,17},{2,10},{10... | collective-permute-start | bytes 393224 | tf_op jit(solution)/shard_map/ppermute | solution.py:548
  1.1 0.1 collective-permute-start.1
  1.2 1.0 %fetch.1 = (f32[256,128]{1,0:T(8,128)S(1)}, f32[256,128]{1,0:T(8,128)S(1)}, f32[128,128]{1,0:T(8,128)S(1)}, f32[3,3,128,256]{3,2,1,0:T(8,128)S(1)}) custom-call(f32[256,128]{1,0:T(8,128)} %bitcast.23, f32[256,128]{1,0:T(8,128)} %bitcast.26, f32[2,256,128]{2,1,0:T(8,128)} %filter_ref.1, f32[3,3,256,256]{3,2,1,0:T(8,128)} %taps_ref.7), custom_call_target="tpu_custom_call" | custom-call | tf_op jit(solution)/shard_map/fetch/pallas_call | solution.py:550
  2.2 0.1 collective-permute-done.other_ref
  2.3 0.4 collective-permute-done.1.other_cot_ref
  2.7 0.0 copy-start.3
  2.7 0.0 copy-start.4
  2.7 3.2 %conv.1 = f32[784,128]{1,0:T(8,128)S(1)} custom-call(f32[256,128]{1,0:T(8,128)S(1)} %get-tuple-element.10.own_ref, f32[256,128]{1,0:T(8,128)S(1)} %collective-permute-done.other_ref, f32[256,128]{1,0:T(8,128)S(1)} %get-tuple-element.11.cot_ref, f32[256,128]{1,0:T(8,128)S(1)} %collective-permute-done.1.other_cot_ref, ...), custom_call_target="tpu_custom_call" | custom-call | tf_op jit(solution)/shard_map/conv/pallas_call | solution.py:559
  6.0 0.0 copy-start
  6.0 16.0 %all_to_all.10 = f32[784,1,128]{2,1,0:T(1,128)S(1)} all-to-all(f32[784,1,128]{2,1,0:T(1,128)S(1)} %bitcast.20), channel_id=1, replica_groups={{21,19,5,3,20,18,4,2,23,17,7,1,22,16,6,0},{29,27,13,11,28,26,12,10,31,2..., dimensions={0} | all-to-all | bytes 802816 | tf_op jit(solution)/shard_map/all_to_all | solution.py:519
  22.0 0.0 copy-done.3
  22.0 0.0 copy-done.4
  22.0 0.0 copy-start.1
  22.0 0.0 copy-start.2
  22.0 1.0 %spectral.1 = f32[912,128]{1,0:T(8,128)S(1)} custom-call(f32[784,128]{1,0:T(8,128)S(1)} %bitcast.21, f32[16,128]{1,0:T(8,128)S(1)} %copy-done.4, f32[256,256]{1,0:T(8,128)S(1)} %copy-done.3), custom_call_target="tpu_custom_call" | custom-call | tf_op jit(solution)/shard_map/spectral/pallas_call | solution.py:572
  22.9 11.9 %all_to_all.11 = f32[912,1,128]{2,1,0:T(1,128)S(1)} all-to-all(f32[912,1,128]{2,1,0:T(1,128)S(1)} %bitcast.19), channel_id=1, replica_groups={{21,19,5,3,20,18,4,2,23,17,7,1,22,16,6,0},{29,27,13,11,28,26,12,10,31,2..., dimensions={0} | all-to-all | bytes 933888 | tf_op jit(solution)/shard_map/all_to_all | solution.py:519
  34.8 0.0 collective-permute-start.2
  34.8 0.0 copy-done
  34.8 0.6 %adjoint.1.total_ref = f32[128,256]{1,0:T(8,128)S(1)} custom-call(f32[912,128]{1,0:T(8,128)S(1)} %bitcast.17, f32[3,3,256,256]{3,2,1,0:T(8,128)S(1)} %copy-done), custom_call_target="tpu_custom_call" | custom-call | tf_op jit(solution)/shard_map/adjoint/pallas_call | solution.py:584
  35.4 1.3 %collective-permute-done.2.other_ref = f32[912,128]{1,0:T(8,128)S(1)} collective-permute-done((f32[912,128]{1,0:T(8,128)S(1)}, f32[912,128]{1,0:T(8,128)S(1)}, u32[]{:S(2)}, u32[]{:S(2)}) %collective-permute-start.2) | collective-permute-done | bytes 466976 | tf_op jit(solution)/shard_map/ppermute | solution.py:582
  36.6 0.0 copy-done.1
  36.6 0.0 copy-done.2
  36.6 1.4 %last.1 = (f32[256,128]{1,0:T(8,128)}, f32[256,128]{1,0:T(8,128)}, f32[2,256,128]{2,1,0:T(8,128)}) custom-call(f32[912,128]{1,0:T(8,128)S(1)} %bitcast.18, f32[912,128]{1,0:T(8,128)S(1)} %collective-permute-done.2.other_ref, f32[256,128]{1,0:T(8,128)S(1)} %bitcast.24, f32[256,128]{1,0:T(8,128)S(1)} %bitcast.27, f32[3,3,256,256]{3,2,1,0:T(8,128)S(1)} %copy-done, ...), custom_call_target="tpu_custom_call" | custom-call | tf_op jit(solution)/shard_map/last/pallas_call | solution.py:593
Async XLA Ops:
  0.6 1.7 %collective-permute-start = (f32[256,128]{1,0:T(8,128)}, f32[256,128]{1,0:T(8,128)S(1)}, u32[]{:S(2)}, u32[]{:S(2)}) collective-permute-start(f32[256,128]{1,0:T(8,128)} %bitcast.22), channel_id=1, source_target_pairs={{0,8},{8,0},{16,24},{24,16},{1,9},{9,1},{17,25},{25,17},{2,10},{10... | collective-permute-start | bytes 393224 | tf_op jit(solution)/shard_map/ppermute | solution.py:548
  1.1 1.6 %collective-permute-start.1 = (f32[256,128]{1,0:T(8,128)}, f32[256,128]{1,0:T(8,128)S(1)}, u32[]{:S(2)}, u32[]{:S(2)}) collective-permute-start(f32[256,128]{1,0:T(8,128)} %bitcast.25), channel_id=1, source_target_pairs={{0,8},{8,0},{16,24},{24,16},{1,9},{9,1},{17,25},{25,17},{2,10},{10... | collective-permute-start | bytes 393224 | tf_op jit(solution)/shard_map/ppermute | solution.py:548
  2.7 19.3 %copy-start.3 = (f32[256,256]{1,0:T(8,128)S(1)}, f32[256,256]{1,0:T(8,128)}, u32[]{:S(2)}) copy-start(f32[256,256]{1,0:T(8,128)} %constant.5.clone.dft_ref) | copy-start | bytes 786436
  2.7 19.3 %copy-start.4 = (f32[16,128]{1,0:T(8,128)S(1)}, f32[16,128]{1,0:T(8,128)}, u32[]{:S(2)}) copy-start(f32[16,128]{1,0:T(8,128)} %constant.4.clone.turn_ref) | copy-start | bytes 24580
  6.0 28.8 %copy-start = (f32[3,3,256,256]{3,2,1,0:T(8,128)S(1)}, f32[3,3,256,256]{3,2,1,0:T(8,128)}, u32[]{:S(2)}) copy-start(f32[3,3,256,256]{3,2,1,0:T(8,128)} %taps_ref.7) | copy-start | bytes 7077892
  22.0 14.7 %copy-start.1 = (f32[256,1,128]{2,1,0:T(1,128)S(1)}, f32[256,1,128]{2,1,0:T(1,128)}, u32[]{:S(2)}) copy-start(f32[256,1,128]{2,1,0:T(1,128)} %param.6) | copy-start | bytes 393220
  22.0 14.7 %copy-start.2 = (f32[256,1,128]{2,1,0:T(1,128)S(1)}, f32[256,1,128]{2,1,0:T(1,128)}, u32[]{:S(2)}) copy-start(f32[256,1,128]{2,1,0:T(1,128)} %param.7) | copy-start | bytes 393220
  34.8 1.8 %collective-permute-start.2 = (f32[912,128]{1,0:T(8,128)S(1)}, f32[912,128]{1,0:T(8,128)S(1)}, u32[]{:S(2)}, u32[]{:S(2)}) collective-permute-start(f32[912,128]{1,0:T(8,128)S(1)} %bitcast.16), channel_id=1, source_target_pairs={{0,8},{8,0},{16,24},{24,16},{1,9},{9,1},{17,25},{25,17},{2,10},{10... | collective-permute-start | bytes 1400840 | tf_op jit(solution)/shard_map/ppermute | solution.py:582
